TPU v7x, 32 devices: a whole 2x2x4 slice. The times are simulated.
32 devices in a mesh: band: 2 (over x), batch: 16 (over z, y, core).
Axes of the slice: x: 2, y: 2, z: 4, core: 2. Of those that a mesh axis runs over, the one named last changes fastest.
Arguments:
- images: bfloat16 [320, 14, 14, 384], P('batch', 'band'), may hold values from -6 to 6
- cotangent: bfloat16 [320, 14, 14, 384], P('batch', 'band'), may hold values from -6 to 6
- norm1_gain: float32 [384], replicated, may hold values from 0.5 to 1.5
- norm1_shift: float32 [384], replicated, may hold values from -1.5 to 1.5
- qkv_weight: bfloat16 [384, 1152], replicated, may hold values from -0.3125 to 0.3125
- qv_bias: float32 [2, 384], replicated, may hold values from -1.5 to 1.5
- proj_weight: bfloat16 [384, 384], replicated, may hold values from -0.875 to 0.875
- proj_bias: float32 [384], replicated, may hold values from -1.5 to 1.5
- pos_in_weight: float32 [2, 96], replicated, may hold values from -4 to 4
- pos_in_bias: float32 [96], replicated, may hold values from -2.5 to 2.5
- pos_norm1_gain: float32 [96], replicated, may hold values from 0.5 to 1.5
- pos_norm1_shift: float32 [96], replicated, may hold values from -1.5 to 1.5
- pos_weight1: float32 [96, 96], replicated, may hold values from -0.625 to 0.625
- pos_bias1: float32 [96], replicated, may hold values from -1.5 to 1.5
- pos_norm2_gain: float32 [96], replicated, may hold values from 0.5 to 1.5
- pos_norm2_shift: float32 [96], replicated, may hold values from -1.5 to 1.5
- pos_weight2: float32 [96, 96], replicated, may hold values from -0.625 to 0.625
- pos_bias2: float32 [96], replicated, may hold values from -1.5 to 1.5
- pos_norm3_gain: float32 [96], replicated, may hold values from 0.5 to 1.5
- pos_norm3_shift: float32 [96], replicated, may hold values from -1.5 to 1.5
- pos_weight3: float32 [96, 12], replicated, may hold values from -1.25 to 1.25
- norm2_gain: float32 [384], replicated, may hold values from 0.5 to 1.5
- norm2_shift: float32 [384], replicated, may hold values from -1.5 to 1.5
- fc1_weight: bfloat16 [384, 1536], replicated, may hold values from -0.3125 to 0.3125
- fc1_bias: float32 [1536], replicated, may hold values from -1.5 to 1.5
- fc2_weight: bfloat16 [1536, 384], replicated, may hold values from -0.15625 to 0.15625
- fc2_bias: float32 [384], replicated, may hold values from -1.5 to 1.5
Outputs:
- out_images: bfloat16 [320, 14, 14, 384], P('batch', 'band')
- grad_images: float32 [320, 14, 14, 384], P('batch', 'band')
- grad_norm1_gain: float32 [384], replicated
- grad_norm1_shift: float32 [384], replicated
- grad_qkv_weight: float32 [384, 1152], replicated
- grad_qv_bias: float32 [2, 384], replicated
- grad_proj_weight: float32 [384, 384], replicated
- grad_proj_bias: float32 [384], replicated
- grad_pos_in_weight: float32 [2, 96], replicated
- grad_pos_in_bias: float32 [96], replicated
- grad_pos_norm1_gain: float32 [96], replicated
- grad_pos_norm1_shift: float32 [96], replicated
- grad_pos_weight1: float32 [96, 96], replicated
- grad_pos_bias1: float32 [96], replicated
- grad_pos_norm2_gain: float32 [96], replicated
- grad_pos_norm2_shift: float32 [96], replicated
- grad_pos_weight2: float32 [96, 96], replicated
- grad_pos_bias2: float32 [96], replicated
- grad_pos_norm3_gain: float32 [96], replicated
- grad_pos_norm3_shift: float32 [96], replicated
- grad_pos_weight3: float32 [96, 12], replicated
- grad_norm2_gain: float32 [384], replicated
- grad_norm2_shift: float32 [384], replicated
- grad_fc1_weight: float32 [384, 1536], replicated
- grad_fc1_bias: float32 [1536], replicated
- grad_fc2_weight: float32 [1536, 384], replicated
- grad_fc2_bias: float32 [384], replicated
All inputs are finite; a program needn't handle non-finite values.
Results may differ from a plain program's by a relative error of at most 0.018.
Values may be sent and summed in bfloat16 or wider, within the bound.
No kernel may reach another device: no remote copies, remote signals or barrier semaphores. Data moves between devices by JAX's collectives and lax.ppermute only.
A program may use at most 192 MiB of HBM per device.

v0:
```python
from functools import partial

import jax
import jax.numpy as jnp
from jax import lax
from jax.sharding import PartitionSpec as P

HEADS = 12
GROUP = 7
HEAD_DIM = 32


HIGH = lax.Precision.HIGHEST
EPSILON = 1e-05


def from_partner(value, axis, stride):
    mask = 2**stride
    pairs = [(source, source ^ mask) for source in range(lax.axis_size(axis))]
    return lax.ppermute(value, axis, pairs)


def layer_norm(values, norm_gain, norm_shift):
    centred = values - jnp.mean(values, axis=-1, keepdims=True)
    variance = jnp.mean(centred * centred, axis=-1, keepdims=True)
    return centred * lax.rsqrt(variance + EPSILON) * norm_gain + norm_shift


def pair_index():
    cells = jnp.arange(GROUP * GROUP, dtype=jnp.int32)
    cell_rows = cells // GROUP
    cell_cols = cells % GROUP
    return (
        (cell_rows[:, None] - cell_rows[None, :] + GROUP - 1) * (2 * GROUP - 1)
        + cell_cols[:, None]
        - cell_cols[None, :]
        + GROUP
        - 1
    )


def position_table(
    in_weight,
    in_bias,
    gain_one,
    shift_one,
    weight_one,
    bias_one,
    gain_two,
    shift_two,
    weight_two,
    bias_two,
    gain_three,
    shift_three,
    weight_three,
):
    offsets = jnp.arange((2 * GROUP - 1) * (2 * GROUP - 1), dtype=jnp.int32)
    coords = jnp.stack(
        [offsets // (2 * GROUP - 1) - (GROUP - 1), offsets % (2 * GROUP - 1) - (GROUP - 1)], axis=1
    ).astype(jnp.float32)
    hidden = jnp.dot(coords, in_weight, precision=HIGH) + in_bias
    hidden = (
        jnp.dot(
            jax.nn.gelu(layer_norm(hidden, gain_one, shift_one), approximate=False),
            weight_one,
            precision=HIGH,
        )
        + bias_one
    )
    hidden = (
        jnp.dot(
            jax.nn.gelu(layer_norm(hidden, gain_two, shift_two), approximate=False),
            weight_two,
            precision=HIGH,
        )
        + bias_two
    )
    return jnp.dot(
        jax.nn.gelu(layer_norm(hidden, gain_three, shift_three), approximate=False),
        weight_three,
        precision=HIGH,
    )


def round_trip(values):
    return lax.optimization_barrier(values.astype(jnp.bfloat16)).astype(jnp.float32)


def to_groups(kept_rows, received, first_band):
    upper = jnp.concatenate([kept_rows, received], axis=1)
    lower = jnp.concatenate([received, kept_rows], axis=1)
    return jnp.where(first_band, upper, lower)


def from_groups(grouped, first_band):
    keep_count = (GROUP + 1) // 2
    kept_rows = jnp.where(first_band, grouped[:, :keep_count], grouped[:, GROUP - keep_count :])
    sent_rows = jnp.where(first_band, grouped[:, keep_count:], grouped[:, : GROUP - keep_count])
    return (kept_rows, sent_rows)


def alternate(kept_rows, received):
    padded = jnp.pad(received, ((0, 0), (0, 1), (0, 0), (0, 0)))
    joined = jnp.stack((kept_rows, padded), axis=2)
    return joined.reshape(
        kept_rows.shape[0], 2 * kept_rows.shape[1], kept_rows.shape[2], kept_rows.shape[3]
    )[:, :GROUP]


def split_groups(image_rows):
    img_count = image_rows.shape[0]
    model_width = image_rows.shape[3]
    parted = image_rows.reshape(img_count, GROUP, GROUP, 2, model_width).transpose(0, 3, 1, 2, 4)
    return parted.reshape(img_count * 2, GROUP * GROUP, model_width)


def join_groups(group_rows):
    img_count = group_rows.shape[0] // 2
    model_width = group_rows.shape[2]
    parted = group_rows.reshape(img_count, 2, GROUP, GROUP, model_width).transpose(0, 2, 3, 1, 4)
    return parted.reshape(img_count, GROUP, 2 * GROUP, model_width)


def body(
    images,
    cotangent,
    norm1_gain,
    norm1_shift,
    qkv_weight,
    qv_bias,
    proj_weight,
    proj_bias,
    pos_in_weight,
    pos_in_bias,
    pos_norm1_gain,
    pos_norm1_shift,
    pos_weight1,
    pos_bias1,
    pos_norm2_gain,
    pos_norm2_shift,
    pos_weight2,
    pos_bias2,
    pos_norm3_gain,
    pos_norm3_shift,
    pos_weight3,
    norm2_gain,
    norm2_shift,
    fc1_weight,
    fc1_bias,
    fc2_weight,
    fc2_bias,
):
    model_width = images.shape[3]
    scale = HEAD_DIM ** (-0.5)
    first_band = lax.axis_index("band") == 0
    image_full = images.astype(jnp.float32)
    norm_one, norm_one_pull = jax.vjp(layer_norm, image_full, norm1_gain, norm1_shift)
    normed = norm_one.astype(jnp.bfloat16)
    partner_rows = from_partner(normed[:, 1::2], "band", 0)
    group_rows = split_groups(to_groups(normed[:, 0::2], partner_rows, first_band))
    group_count = group_rows.shape[0]
    head_shape = (group_count, GROUP * GROUP, HEADS, HEAD_DIM)
    flat_normed = group_rows.reshape(-1, model_width)
    projected = jnp.dot(flat_normed, qkv_weight, preferred_element_type=jnp.float32)
    queries = (projected[:, :model_width] + qv_bias[0]).astype(jnp.bfloat16).reshape(head_shape)
    key_vectors = (
        projected[:, model_width : 2 * model_width].astype(jnp.bfloat16).reshape(head_shape)
    )
    val_vectors = (
        (projected[:, 2 * model_width :] + qv_bias[1]).astype(jnp.bfloat16).reshape(head_shape)
    )
    table, table_pull = jax.vjp(
        position_table,
        pos_in_weight,
        pos_in_bias,
        pos_norm1_gain,
        pos_norm1_shift,
        pos_weight1,
        pos_bias1,
        pos_norm2_gain,
        pos_norm2_shift,
        pos_weight2,
        pos_bias2,
        pos_norm3_gain,
        pos_norm3_shift,
        pos_weight3,
    )
    selector = (
        pair_index().reshape(-1)[:, None] == jnp.arange(table.shape[0], dtype=jnp.int32)[None, :]
    ).astype(jnp.float32)
    bias_heads = (
        jnp.dot(selector, table, precision=HIGH)
        .reshape(GROUP * GROUP, GROUP * GROUP, HEADS)
        .transpose(2, 0, 1)
    )
    scores = (
        scale
        * jnp.einsum("gihd,gjhd->ghij", queries, key_vectors, preferred_element_type=jnp.float32)
        + bias_heads
    )
    log_total = jax.nn.logsumexp(scores, axis=-1, keepdims=True)
    probs = jnp.exp(scores - log_total).astype(jnp.bfloat16)
    attended = jnp.einsum("ghij,gjhd->gihd", probs, val_vectors, preferred_element_type=jnp.float32)
    attended = attended.reshape(group_count, GROUP * GROUP, model_width).astype(jnp.bfloat16)
    kept_back, sent_back = from_groups(join_groups(attended), first_band)
    returned = from_partner(sent_back, "band", 0)
    att_band = alternate(kept_back, returned)
    flat_att = att_band.reshape(-1, model_width)
    middle = image_full + (
        jnp.dot(flat_att, proj_weight, preferred_element_type=jnp.float32) + proj_bias
    ).reshape(image_full.shape)
    norm_two, norm_two_pull = jax.vjp(layer_norm, middle, norm2_gain, norm2_shift)
    flat_normed2 = norm_two.astype(jnp.bfloat16).reshape(-1, model_width)
    pre_act = jnp.dot(flat_normed2, fc1_weight, preferred_element_type=jnp.float32) + fc1_bias
    activ, gelu_pull = jax.vjp(partial(jax.nn.gelu, approximate=False), pre_act)
    activ_round = activ.astype(jnp.bfloat16)
    output = middle + (
        jnp.dot(activ_round, fc2_weight, preferred_element_type=jnp.float32) + fc2_bias
    ).reshape(middle.shape)
    upstream = cotangent.astype(jnp.float32)
    up_round = cotangent.reshape(-1, model_width)
    grad_fc2 = jnp.einsum("nf,nc->fc", activ_round, up_round, preferred_element_type=jnp.float32)
    grad_fc2_bias = jnp.sum(up_round, axis=0, dtype=jnp.float32)
    grad_act = jnp.dot(up_round, fc2_weight.T, preferred_element_type=jnp.float32)
    (grad_pre,) = gelu_pull(grad_act)
    grad_pre_round = grad_pre.astype(jnp.bfloat16)
    grad_fc1 = jnp.einsum(
        "nc,nf->cf", flat_normed2, grad_pre_round, preferred_element_type=jnp.float32
    )
    grad_fc1_bias = jnp.sum(grad_pre_round, axis=0, dtype=jnp.float32)
    grad_normed2 = round_trip(
        jnp.dot(grad_pre_round, fc1_weight.T, preferred_element_type=jnp.float32)
    )
    grad_mid_norm, grad_n2_gain, grad_n2_shift = norm_two_pull(grad_normed2.reshape(middle.shape))
    grad_middle = upstream + grad_mid_norm
    ffn_set = (grad_n2_gain, grad_n2_shift, grad_fc1, grad_fc1_bias, grad_fc2, grad_fc2_bias)
    grad_branch = grad_middle.astype(jnp.bfloat16).reshape(-1, model_width)
    grad_proj = jnp.einsum("nc,nk->ck", flat_att, grad_branch, preferred_element_type=jnp.float32)
    grad_proj_bias = jnp.sum(grad_branch, axis=0, dtype=jnp.float32)
    grad_att = jnp.dot(grad_branch, proj_weight.T, preferred_element_type=jnp.float32).astype(
        jnp.bfloat16
    )
    grad_att = grad_att.reshape(att_band.shape)
    grad_partner = from_partner(grad_att[:, 1::2], "band", 0)
    grad_att_groups = split_groups(to_groups(grad_att[:, 0::2], grad_partner, first_band)).reshape(
        head_shape
    )
    soft_probs = jnp.exp(scores - log_total)
    grad_probs = jnp.einsum(
        "gihd,gjhd->ghij", grad_att_groups, val_vectors, preferred_element_type=jnp.float32
    )
    grad_vals = jnp.einsum(
        "ghij,gihd->gjhd",
        soft_probs.astype(jnp.bfloat16),
        grad_att_groups,
        preferred_element_type=jnp.float32,
    ).astype(jnp.bfloat16)
    inner_sum = jnp.sum(grad_probs * soft_probs, axis=-1, keepdims=True)
    grad_scores = (soft_probs * (grad_probs - inner_sum)).astype(jnp.bfloat16)
    grad_queries = (
        scale
        * jnp.einsum(
            "ghij,gjhd->gihd", grad_scores, key_vectors, preferred_element_type=jnp.float32
        )
    ).astype(jnp.bfloat16)
    grad_keys = (
        scale
        * jnp.einsum("ghij,gihd->gjhd", grad_scores, queries, preferred_element_type=jnp.float32)
    ).astype(jnp.bfloat16)
    grad_bias_heads = jnp.sum(grad_scores, axis=0, dtype=jnp.float32)
    grad_table = jnp.dot(
        selector.T, grad_bias_heads.transpose(1, 2, 0).reshape(-1, HEADS), precision=HIGH
    )
    pos_grads = table_pull(grad_table)
    grad_qkv = jnp.concatenate(
        [
            grad_queries.reshape(-1, model_width),
            grad_keys.reshape(-1, model_width),
            grad_vals.reshape(-1, model_width),
        ],
        axis=1,
    )
    grad_qkv_w = jnp.einsum("nc,nk->ck", flat_normed, grad_qkv, preferred_element_type=jnp.float32)
    grad_qv = jnp.stack(
        [
            jnp.sum(grad_qkv[:, :model_width], axis=0, dtype=jnp.float32),
            jnp.sum(grad_qkv[:, 2 * model_width :], axis=0, dtype=jnp.float32),
        ]
    )
    grad_normed = jnp.dot(grad_qkv, qkv_weight.T, preferred_element_type=jnp.float32).astype(
        jnp.bfloat16
    )
    kept_grad, sent_grad = from_groups(
        join_groups(grad_normed.reshape(group_count, GROUP * GROUP, model_width)), first_band
    )
    grad_received = from_partner(sent_grad, "band", 0)
    grad_band = alternate(kept_grad, grad_received).astype(jnp.float32)
    grad_img_norm, grad_n1_gain, grad_n1_shift = norm_one_pull(grad_band)
    grad_images = grad_middle + grad_img_norm
    attention_set = (
        grad_n1_gain,
        grad_n1_shift,
        grad_qkv_w,
        grad_qv,
        grad_proj,
        grad_proj_bias,
    ) + tuple(pos_grads)
    summed = lax.psum(tuple(attention_set) + tuple(ffn_set), ("band", "batch"))
    return (
        output.astype(jnp.bfloat16),
        grad_images,
        summed[0],
        summed[1],
        summed[2],
        summed[3],
        summed[4],
        summed[5],
        summed[6],
        summed[7],
        summed[8],
        summed[9],
        summed[10],
        summed[11],
        summed[12],
        summed[13],
        summed[14],
        summed[15],
        summed[16],
        summed[17],
        summed[18],
        summed[19],
        summed[20],
        summed[21],
        summed[22],
        summed[23],
        summed[24],
    )


def solution(mesh):
    in_specs = (
        P("batch", "band", None, None),
        P("batch", "band", None, None),
        P(),
        P(),
        P(),
        P(),
        P(),
        P(),
        P(),
        P(),
        P(),
        P(),
        P(),
        P(),
        P(),
        P(),
        P(),
        P(),
        P(),
        P(),
        P(),
        P(),
        P(),
        P(),
        P(),
        P(),
        P(),
    )
    out_specs = (
        P("batch", "band", None, None),
        P("batch", "band", None, None),
        P(),
        P(),
        P(),
        P(),
        P(),
        P(),
        P(),
        P(),
        P(),
        P(),
        P(),
        P(),
        P(),
        P(),
        P(),
        P(),
        P(),
        P(),
        P(),
        P(),
        P(),
        P(),
        P(),
        P(),
        P(),
    )
    return jax.shard_map(body, mesh=mesh, in_specs=in_specs, out_specs=out_specs, check_vma=False)
```

profile of v0, /device:TPU:0, one launch (start us, length us, event | category | flops | bytes accessed | tf_op | source)
XLA Modules:
  0.0 884.3 jit_solution(9984570034334002987)
XLA Ops:
  15.2 19.9 %slice.59 = bf16[20,3,14,384]{3,1,2,0:T(4,128)(2,1)} slice(bf16[20,7,14,384]{3,1,2,0:T(8,128)(2,1)} %fusion.28), slice={[0:20:1], [1:7:2], [0:14:1], [0:384:1]} | slice | bytes 1290240 | tf_op jit(solution)/shard_map/slice | solution.py:159
  45.5 19.8 %slice.58 = bf16[20,4,14,384]{3,1,2,0:T(4,128)(2,1)} slice(bf16[20,7,14,384]{3,1,2,0:T(8,128)(2,1)} %fusion.28), slice={[0:20:1], [0:7:2], [0:14:1], [0:384:1]} | slice | bytes 1720320 | tf_op jit(solution)/shard_map/slice | solution.py:160
  94.9 6.8 reshape.452
  101.7 6.6 reshape.454
  108.3 6.6 reshape.453
  114.9 12.2 %fusion.6 = (f32[40,12,49]{2,1,0:T(8,128)S(1)}, f32[40,12,49,49]{2,3,1,0:T(8,128)}) fusion(f32[12,49,49]{1,2,0:T(8,128)S(1)} %bitcast.101, bf16[40,49,12,32]{1,0,3,2:T(8,128)(2,1)} %reshape.454, bf16[40,49,12,32]{1,0,3,2:T(8,128)(2,1)} %reshape.453), kind=kOutput, calls=%fused_computation.24 | convolution fusion | flops 77192640 | bytes 7829808 | tf_op jit(solution)/shard_map/gihd,gjhd->ghij/dot_general | solution.py:198
  127.1 9.4 %exponential_reduce_fusion = f32[40,12,49]{2,1,0:T(8,128)S(1)} fusion(f32[40,12,49,49]{2,3,1,0:T(8,128)} %get-tuple-element.206, f32[40,12,49]{2,1,0:T(8,128)S(1)} %is-finite_select_fusion, f32[12,49,49]{1,2,0:T(8,128)S(1)} %bitcast.102), kind=kLoop, calls=%fused_computation.5 | loop fusion | flops 4586400 | bytes 4913328 | tf_op jit(solution)/shard_map/reduce_sum | solution.py:201
  137.3 22.0 %convert_bitcast_fusion.1 = bf16[40,49,12,32]{1,3,2,0:T(8,128)(2,1)} fusion(bf16[40,49,12,32]{1,0,3,2:T(8,128)(2,1)S(1)} %copy-done.5, f32[40,12,49,49]{2,3,1,0:T(8,128)} %get-tuple-element.206, f32[40,12,49]{2,1,0:T(8,128)S(1)} %log_add_fusion, f32[12,49,49]{1,2,0:T(8,128)S(1)} %bitcast.103), kind=kOutput, calls=%fused_computation.48 | convolution fusion | flops 79121280 | bytes 7829808 | tf_op jit(solution)/shard_map/ghij,gjhd->gihd/dot_general | solution.py:203
  159.3 10.4 %copy.232 = bf16[40,49,12,32]{3,2,0,1:T(8,128)(2,1)} copy(bf16[40,49,12,32]{1,3,2,0:T(8,128)(2,1)} %convert_bitcast_fusion.1) | data formatting | bytes 3010560 | tf_op jit(solution)/shard_map/convert_element_type | solution.py:204
  169.8 11.0 %convert_element_type.116 = bf16[20,2,7,7,384]{4,1,0,3,2:T(2,128)(2,1)} reshape(bf16[40,49,12,32]{3,2,0,1:T(8,128)(2,1)} %copy.232) | data formatting | bytes 3010560 | tf_op jit(solution)/shard_map/convert_element_type | solution.py:204
  196.4 13.1 %collective-permute-done.1 = bf16[20,3,14,384]{3,2,1,0:T(8,128)(2,1)} collective-permute-done((bf16[20,3,14,384]{3,2,1,0:T(8,128)(2,1)}, bf16[20,3,14,384]{3,2,1,0:T(8,128)(2,1)}, u32[]{:S(2)}, u32[]{:S(2)}) %collective-permute-start.1) | collective-permute-done | bytes 645152 | tf_op jit(solution)/shard_map/ppermute | solution.py:20
  236.5 31.6 %multiply_convert_fusion.1 = (bf16[1960,1536]{1,0:T(8,128)(2,1)}, f32[1960,1536]{1,0:T(8,128)}, f32[1960,1536]{1,0:T(8,128)}) fusion(f32[1536]{0:T(1024)S(1)} %copy-done.106, bf16[1960,384]{1,0:T(8,128)(2,1)S(1)} %reshape.460, bf16[384,1536]{1,0:T(8,128)(2,1)S(1)} %copy-done), kind=kOutput, calls=%fused_computation.10 | convolution fusion | flops 2510807040 | bytes 32796672 | tf_op jit(solution)/shard_map/dot_general | solution.py:214
  268.1 13.1 %convert_reduce_fusion.1 = (f32[1536]{0:T(1024)}, bf16[1960,1536]{1,0:T(8,128)(2,1)S(1)}) fusion(f32[1960,1536]{1,0:T(8,128)} %get-tuple-element.189, bf16[1960,384]{1,0:T(8,128)(2,1)S(1)} %copy-done.31, bf16[1536,384]{1,0:T(8,128)(2,1)S(1)} %copy-done.105, f32[1960,1536]{1,0:T(8,128)} %get-tuple-element.207, f32[1536]{0:T(1024)S(1)} %copy-done.106), kind=kOutput, calls=%fused_computation.8 | convolution fusion | flops 2363288064 | bytes 32802816 | tf_op jit(solution)/shard_map/dot_general | solution.py:224
  291.8 7.9 convolution_add_fusion.1
  330.1 7.6 fusion.120
  337.7 8.7 collective-permute-done.2
  349.5 7.1 reshape_reshape.10
  356.6 9.8 %copy.245 = bf16[40,49,12,32]{1,3,2,0:T(8,128)(2,1)} copy(bf16[40,49,12,32]{3,2,0,1:T(8,128)(2,1)} %reshape_reshape.10) | data formatting | bytes 3010560 | tf_op jit(solution)/shard_map/reshape;reshape | solution.py:245
  366.5 12.4 %convert_reduce_fusion.2 = (f32[12,32]{1,0:T(8,128)}, bf16[40,49,12,32]{1,3,2,0:T(8,128)(2,1)}) fusion(bf16[40,49,12,32]{1,3,2,0:T(8,128)(2,1)} %copy.245, f32[40,12,49,49]{2,3,1,0:T(8,128)} %get-tuple-element.206, f32[40,12,49]{2,1,0:T(8,128)S(1)} %copy-done.18, f32[12,49,49]{1,2,0:T(8,128)S(1)} %bitcast.105), kind=kOutput, calls=%fused_computation.25 | convolution fusion | flops 80626176 | bytes 7831344 | tf_op jit(solution)/shard_map/ghij,gihd->gjhd/dot_general | solution.py:252
  378.9 18.1 %multiply_reduce_fusion = (f32[40,12,49]{2,1,0:T(8,128)}, f32[40,12,49,49]{2,3,1,0:T(8,128)}) fusion(f32[40,12,49,49]{2,3,1,0:T(8,128)} %get-tuple-element.206, f32[40,12,49]{2,1,0:T(8,128)S(1)} %copy-done.18, f32[12,49,49]{1,2,0:T(8,128)S(1)} %bitcast.106, bf16[40,49,12,32]{1,3,2,0:T(8,128)(2,1)} %copy.245, bf16[40,49,12,32]{1,0,3,2:T(8,128)(2,1)} %reshape.452), kind=kOutput, calls=%fused_computation.3 | convolution fusion | flops 79497600 | bytes 12533808 | tf_op jit(solution)/shard_map/gihd,gjhd->ghij/dot_general | solution.py:249
  397.0 12.1 %convert_reduce_fusion = (f32[12,49,49]{1,2,0:T(8,128)}, bf16[40,12,49,49]{2,3,1,0:T(8,128)(2,1)S(1)}) fusion(f32[40,12,49,49]{2,3,1,0:T(8,128)} %get-tuple-element.209, f32[40,12,49]{2,1,0:T(8,128)} %get-tuple-element.208, f32[40,12,49]{2,1,0:T(8,128)} %copy-done.17, f32[12,49,49]{1,2,0:T(8,128)} %bitcast.104, f32[40,12,49,49]{2,3,1,0:T(8,128)} %get-tuple-element.206), kind=kLoop, calls=%fused_computation.1 | loop fusion | flops 9191028 | bytes 11943456 | tf_op jit(solution)/shard_map/reduce_sum | solution.py:270
  409.1 7.7 fusion.14
  416.8 7.4 convert_reduce_fusion.3
  439.2 6.5 copy.255
  451.2 6.5 copy.252
  457.7 6.1 reshape.467
  464.1 6.5 copy.249
  470.6 6.3 reshape.466
  498.0 12.3 %collective-permute-done.3 = bf16[20,3,14,384]{3,2,1,0:T(8,128)(2,1)S(1)} collective-permute-done((bf16[20,3,14,384]{3,2,1,0:T(8,128)(2,1)S(1)}, bf16[20,3,14,384]{3,2,1,0:T(8,128)(2,1)S(1)}, u32[]{:S(2)}, u32[]{:S(2)}) %collective-permute-start.3) | collective-permute-done | bytes 645152 | tf_op jit(solution)/shard_map/ppermute | solution.py:20
  530.4 6.3 fusion.117
  541.9 141.0 %all-reduce.7.cloned.1.call-done = (f32[384]{0:T(512)}, f32[384]{0:T(512)}, f32[2,384]{1,0:T(2,128)}, f32[384]{0:T(512)}, f32[2,96]{1,0:T(2,128)}, /*index=5*/f3...) async-done(((f32[384]{0:T(512)}, f32[384]{0:T(512)}, ...) | async-done | bytes 101008 | tf_op jit(solution)/shard_map/psum | solution.py:308
  683.1 174.3 %all-reduce.9.cloned.1.call-done = (f32[384,1152]{1,0:T(8,128)}, f32[384,384]{1,0:T(8,128)}, f32[384,1536]{1,0:T(8,128)}, f32[1536,384]{1,0:T(8,128)}) async-done(((f32[384,1152]{1,0:T(8,128)}, f32[384,384]{1,0:T(8,128)}, f32[384,1536]{1,0:T(8,128)}, f32[1536,384]{1,0:T(8,128)}), (f32[384,1152]{1,0:T(8,128)}, f32[384,384]{1,0:T(8,128)}, f32[384,1536]{1,0:T(8,128)}, ...) | async-done | bytes 7077904 | tf_op jit(solution)/shard_map/psum | solution.py:308
  (397 shorter events, 220.9 us)
Async XLA Ops:
  7.2 229.3 %copy-start = (bf16[384,1536]{1,0:T(8,128)(2,1)S(1)}, bf16[384,1536]{1,0:T(8,128)(2,1)}, u32[]{:S(2)}) copy-start(bf16[384,1536]{1,0:T(8,128)(2,1)} %param.50) | copy-start | bytes 3538948
  7.3 675.7 %all-reduce.7.cloned.1.call-start = ((), (), s32[]{:S(2)}) async-start(), calls=%async_computation | async-start | bytes 271360 | tf_op jit(solution)/shard_map/psum | solution.py:308
  13.3 30.1 %copy-start.45 = (f32[96,96]{1,0:T(8,128)S(1)}, f32[96,96]{1,0:T(8,128)}, u32[]{:S(2)}) copy-start(f32[96,96]{1,0:T(8,128)} %param.43) | copy-start | bytes 110596
  13.3 31.1 %copy-start.94 = (f32[96]{0:T(128)S(1)}, f32[96]{0:T(128)}, u32[]{:S(2)}) copy-start(f32[96]{0:T(128)} %param.45) | copy-start | bytes 1156
  13.4 31.1 %copy-start.104 = (f32[96]{0:T(128)S(1)}, f32[96]{0:T(128)}, u32[]{:S(2)}) copy-start(f32[96]{0:T(128)} %param.46) | copy-start | bytes 1156
  15.2 50.4 %copy-start.83 = (f32[96,12]{0,1:T(8,128)S(1)}, f32[96,12]{0,1:T(8,128)}, u32[]{:S(2)}) copy-start(f32[96,12]{0,1:T(8,128)} %param.47) | copy-start | bytes 13828
  35.1 34.1 %copy-start.90 = (f32[2,384]{1,0:T(2,128)S(1)}, f32[2,384]{1,0:T(2,128)}, u32[]{:S(2)}) copy-start(f32[2,384]{1,0:T(2,128)} %param.32) | copy-start | bytes 9220
  37.2 32.0 %collective-permute-start = (bf16[20,3,14,384]{3,2,1,0:T(8,128)(2,1)}, bf16[20,3,14,384]{3,2,1,0:T(8,128)(2,1)}, u32[]{:S(2)}, u32[]{:S(2)}) collective-permute-start(bf16[20,3,14,384]{3,2,1,0:T(8,128)(2,1)} %copy.221), channel_id=1, source_target_pairs={{0,16},{16,0},{1,17},{17,1},{2,18},{18,2},{3,19},{19,3},{4,20},{20... | collective-permute-start | bytes 1935368 | tf_op jit(solution)/shard_map/ppermute | solution.py:20
  69.2 67.5 %copy-start.10 = (f32[49,49,12]{0,1,2:T(8,128)}, f32[49,49,12]{0,1,2:T(8,128)S(1)}, u32[]{:S(2)}) copy-start(f32[49,49,12]{0,1,2:T(8,128)S(1)} %copy.229) | copy-start | bytes 345748
  191.2 18.3 %collective-permute-start.1 = (bf16[20,3,14,384]{3,2,1,0:T(8,128)(2,1)}, bf16[20,3,14,384]{3,2,1,0:T(8,128)(2,1)}, u32[]{:S(2)}, u32[]{:S(2)}) collective-permute-start(bf16[20,3,14,384]{3,2,1,0:T(8,128)(2,1)} %slice_select_fusion.3), channel_id=1, source_target_pairs={{0,16},{16,0},{1,17},{17,1},{2,18},{18,2},{3,19},{19,3},{4,20},{20... | collective-permute-start | bytes 1935368 | tf_op jit(solution)/shard_map/ppermute | solution.py:20
  236.5 31.6 %copy-start.31 = (bf16[1960,384]{1,0:T(8,128)(2,1)S(1)}, bf16[1960,384]{1,0:T(8,128)(2,1)}, u32[]{:S(2)}) copy-start(bf16[1960,384]{1,0:T(8,128)(2,1)} %reshape.462) | copy-start | bytes 4515844
  236.5 31.6 %copy-start.105 = (bf16[1536,384]{1,0:T(8,128)(2,1)S(1)}, bf16[1536,384]{1,0:T(8,128)(2,1)}, u32[]{:S(2)}) copy-start(bf16[1536,384]{1,0:T(8,128)(2,1)} %param.52) | copy-start | bytes 3538948
  329.3 17.1 %collective-permute-start.2 = (bf16[20,3,14,384]{3,2,1,0:T(8,128)(2,1)S(1)}, bf16[20,3,14,384]{3,2,1,0:T(8,128)(2,1)S(1)}, u32[]{:S(2)}, u32[]{:S(2)}) collective-permute-start(bf16[20,3,14,384]{3,2,1,0:T(8,128)(2,1)S(1)} %slice.71), channel_id=1, source_target_pairs={{0,16},{16,0},{1,17},{17,1},{2,18},{18,2},{3,19},{19,3},{4,20},{20... | collective-permute-start | bytes 1935368 | tf_op jit(solution)/shard_map/ppermute | solution.py:20
  494.0 16.2 %collective-permute-start.3 = (bf16[20,3,14,384]{3,2,1,0:T(8,128)(2,1)S(1)}, bf16[20,3,14,384]{3,2,1,0:T(8,128)(2,1)S(1)}, u32[]{:S(2)}, u32[]{:S(2)}) collective-permute-start(bf16[20,3,14,384]{3,2,1,0:T(8,128)(2,1)S(1)} %slice_select_fusion.2), channel_id=1, source_target_pairs={{0,16},{16,0},{1,17},{17,1},{2,18},{18,2},{3,19},{19,3},{4,20},{20... | collective-permute-start | bytes 1935368 | tf_op jit(solution)/shard_map/ppermute | solution.py:20
  530.3 327.1 %all-reduce.9.cloned.1.call-start = ((), (), s32[]{:S(2)}) async-start(), calls=%async_computation.1 | async-start | bytes 14155776 | tf_op jit(solution)/shard_map/psum | solution.py:308
  683.0 179.9 %copy-start.91 = (f32[2,384]{1,0:T(2,128)S(1)}, f32[2,384]{1,0:T(2,128)}, u32[]{:S(2)}) copy-start(f32[2,384]{1,0:T(2,128)} %get-tuple-element.228) | copy-start | bytes 9220
  683.0 181.3 %copy-start.98 = (f32[384]{0:T(512)S(1)}, f32[384]{0:T(512)}, u32[]{:S(2)}) copy-start(f32[384]{0:T(512)} %get-tuple-element.230) | copy-start | bytes 4612
  683.0 181.9 %copy-start.100 = (f32[2,96]{1,0:T(2,128)S(1)}, f32[2,96]{1,0:T(2,128)}, u32[]{:S(2)}) copy-start(f32[2,96]{1,0:T(2,128)} %get-tuple-element.231) | copy-start | bytes 2308
  683.0 182.4 %copy-start.116 = (f32[96]{0:T(128)S(1)}, f32[96]{0:T(128)}, u32[]{:S(2)}) copy-start(f32[96]{0:T(128)} %get-tuple-element.232) | copy-start | bytes 1156
  683.0 182.9 %copy-start.115 = (f32[96]{0:T(128)S(1)}, f32[96]{0:T(128)}, u32[]{:S(2)}) copy-start(f32[96]{0:T(128)} %get-tuple-element.233) | copy-start | bytes 1156
  683.0 183.4 %copy-start.114 = (f32[96]{0:T(128)S(1)}, f32[96]{0:T(128)}, u32[]{:S(2)}) copy-start(f32[96]{0:T(128)} %get-tuple-element.234) | copy-start | bytes 1156
  683.0 183.9 %copy-start.49 = (f32[96,96]{1,0:T(8,128)S(1)}, f32[96,96]{1,0:T(8,128)}, u32[]{:S(2)}) copy-start(f32[96,96]{1,0:T(8,128)} %get-tuple-element.235) | copy-start | bytes 110596
  683.0 184.6 %copy-start.113 = (f32[96]{0:T(128)S(1)}, f32[96]{0:T(128)}, u32[]{:S(2)}) copy-start(f32[96]{0:T(128)} %get-tuple-element.236) | copy-start | bytes 1156
  683.0 185.1 %copy-start.112 = (f32[96]{0:T(128)S(1)}, f32[96]{0:T(128)}, u32[]{:S(2)}) copy-start(f32[96]{0:T(128)} %get-tuple-element.237) | copy-start | bytes 1156
  683.0 185.6 %copy-start.111 = (f32[96]{0:T(128)S(1)}, f32[96]{0:T(128)}, u32[]{:S(2)}) copy-start(f32[96]{0:T(128)} %get-tuple-element.238) | copy-start | bytes 1156
  683.0 186.1 %copy-start.48 = (f32[96,96]{1,0:T(8,128)S(1)}, f32[96,96]{1,0:T(8,128)}, u32[]{:S(2)}) copy-start(f32[96,96]{1,0:T(8,128)} %get-tuple-element.239) | copy-start | bytes 110596
  683.0 186.7 %copy-start.110 = (f32[96]{0:T(128)S(1)}, f32[96]{0:T(128)}, u32[]{:S(2)}) copy-start(f32[96]{0:T(128)} %get-tuple-element.240) | copy-start | bytes 1156
  683.1 187.2 %copy-start.109 = (f32[96]{0:T(128)S(1)}, f32[96]{0:T(128)}, u32[]{:S(2)}) copy-start(f32[96]{0:T(128)} %get-tuple-element.241) | copy-start | bytes 1156
  683.1 187.7 %copy-start.108 = (f32[96]{0:T(128)S(1)}, f32[96]{0:T(128)}, u32[]{:S(2)}) copy-start(f32[96]{0:T(128)} %get-tuple-element.242) | copy-start | bytes 1156
  683.1 188.2 %copy-start.85 = (f32[96,12]{0,1:T(8,128)S(1)}, f32[96,12]{0,1:T(8,128)}, u32[]{:S(2)}) copy-start(f32[96,12]{0,1:T(8,128)} %get-tuple-element.243) | copy-start | bytes 13828
  683.1 188.8 %copy-start.97 = (f32[384]{0:T(512)S(1)}, f32[384]{0:T(512)}, u32[]{:S(2)}) copy-start(f32[384]{0:T(512)} %get-tuple-element.244) | copy-start | bytes 4612
  683.1 189.4 %copy-start.96 = (f32[384]{0:T(512)S(1)}, f32[384]{0:T(512)}, u32[]{:S(2)}) copy-start(f32[384]{0:T(512)} %get-tuple-element.245) | copy-start | bytes 4612
  (91 other events, 752.2 us)
Sparse Core Ops, SparseCore 0:
  530.4 152.5 all-reduce.6
  690.9 166.4 all-reduce.8
where the time goes:
time: 900 us; the launch traced here: 884 us
  waiting for transfers between devices  349 us (39%)
  local copies, waits for them, and re-layouts  250 us (28%)
  matrix products  187 us (21%)
  other arithmetic  77.6 us (9%)
  between operations  16 us (2%)
    psum x2, waiting for transfers between devices, body(): summed = lax.psum(tuple(attention_set) + tuple(ffn_set), ('band', 'batch'))  315 us
    unnamed x264, local copies, waits for them, and re-layouts  36.3 us
    ppermute x4, waiting for transfers between devices, from_partner(): return lax.ppermute(value, axis, pairs)  34.1 us
    dot_general x1, matrix products, body(): jnp.dot(flat_normed2, fc1_weight, preferred_element_type=jnp.float32)  31.6 us
    slice x2, local copies, waits for them, and re-layouts, body(): partner_rows = from_partner(normed[:, 1::2], 'band', 0)  22.1 us
    dot_general x1, matrix products, body(): jnp.einsum('ghij,gjhd->gihd', probs, val_vectors, preferred_element_type=...  22 us
    convert_element_type x2, local copies, waits for them, and re-layouts, body(): attended.reshape(group_count, GROUP * GROUP, model_width)  21.5 us
    slice x1, local copies, waits for them, and re-layouts, body(): normed[:, 0::2]  19.8 us
  transfers between devices with their start and end apart: 6, of which 5 were waited for; matrix products, arithmetic and copies ran while one was open for 6% of the time, Pallas kernels for 0%

commit v1 on v0

v1 whole, which is shorter than its diff:
```python
import math
from functools import partial

import jax
import jax.numpy as jnp
import numpy as np
from jax import lax
from jax.experimental import pallas as pl
from jax.experimental.pallas import tpu as pltpu
from jax.sharding import PartitionSpec as P

HEADS = 12
GROUP = 7
HEAD_DIM = 32
SPAN = 2 * GROUP - 1
HIGH = lax.Precision.HIGHEST
EPSILON = 1e-05
SCALE = HEAD_DIM**-0.5
MASKED = -1e30
PAD_COLS = 16
TOKENS = GROUP * PAD_COLS
LANES = 128
PER_BLOCK = LANES // HEAD_DIM
STACK = PER_BLOCK * TOKENS
KEPT = (GROUP + 1) // 2
SENT = GROUP - KEPT
OFFSETS = 176
WIDE = SPAN * PAD_COLS
F32 = jnp.float32
BF16 = jnp.bfloat16


def dot(a, b, precision=None):
    return lax.dot_general(a, b, (((1,), (0,)), ((), ())), precision=precision, preferred_element_type=F32)


def dot_nt(a, b, precision=None):
    return lax.dot_general(a, b, (((1,), (1,)), ((), ())), precision=precision, preferred_element_type=F32)


def dot_tn(a, b, precision=None):
    return lax.dot_general(a, b, (((0,), (0,)), ((), ())), precision=precision, preferred_element_type=F32)


def whole(shape):
    zeros = (0,) * len(shape)
    return pl.BlockSpec(shape, lambda *_: zeros, pipeline_mode=pl.Buffered(1))


def normalise(values):
    mean = jnp.mean(values, axis=-1, keepdims=True)
    centred = values - mean
    inverse = lax.rsqrt(jnp.mean(centred * centred, axis=-1, keepdims=True) + EPSILON)
    return centred * inverse, inverse


def normalise_back(grad_hat, hat, inverse):
    first = jnp.mean(grad_hat, axis=-1, keepdims=True)
    second = jnp.mean(grad_hat * hat, axis=-1, keepdims=True)
    return inverse * (grad_hat - first - hat * second)


def gelu_both(v):
    cdf = 0.5 + 0.5 * lax.erf(v * (0.5**0.5))
    density = jnp.exp(-0.5 * v * v) * ((2.0 * np.pi) ** -0.5)
    return v * cdf, cdf + v * density


def column_sum(values):
    return jnp.sum(values, axis=0, keepdims=True)


SMALL = 24


def launch(kernel, name, grid, inputs, in_specs, out_shape, out_specs, so_far=(), scratch=(), flops=0,
           after=(), vmem=16, through=()):
    count, held = len(inputs), len(so_far) + len(after) + len(through)
    own = len(out_shape)
    hand = {count + len(so_far) + len(after) + i: own + i for i in range(len(through))}
    inner = kernel
    if held:
        kernel = lambda *refs: inner(
            *refs[:count], *refs[count + held : count + held + own], *refs[count + held + own + len(through) :]
        )
    moved = sum(a.size * a.dtype.itemsize for a in (*inputs, *out_shape))
    return pl.pallas_call(
        kernel,
        grid=grid,
        in_specs=list(in_specs) + [pl.BlockSpec(memory_space=pl.ANY)] * held,
        out_specs=list(out_specs) + [pl.BlockSpec(memory_space=pl.ANY)] * len(through),
        out_shape=list(out_shape) + [shaped(a.shape, a.dtype) for a in through],
        input_output_aliases={count + i: i for i in range(len(so_far))} | hand,
        scratch_shapes=list(scratch),
        compiler_params=pltpu.CompilerParams(vmem_limit_bytes=vmem * 2**20),
        cost_estimate=pl.CostEstimate(flops=int(flops), bytes_accessed=int(moved), transcendentals=0),
        name=name,
    )(*inputs, *so_far, *after, *through)


def small_launch(kernel, name, inputs, out_shape, scratch=(), flops=0, after=(), vmem=16, through=()):
    specs = [pl.BlockSpec(memory_space=pltpu.SMEM if a.dtype == jnp.int32 else pltpu.VMEM) for a in inputs]
    outs = [pl.BlockSpec(memory_space=pltpu.VMEM)] * len(out_shape)
    return launch(kernel, name, (), inputs, specs, out_shape, outs, scratch=scratch, flops=flops, after=after, vmem=vmem,
                  through=through)


def shaped(shape, dtype):
    return jax.ShapeDtypeStruct(shape, dtype)


FEED_PART = 512
TOKEN = shaped((8, LANES), F32)


def token_kernel(token):
    token[...] = jnp.zeros_like(token)


def merge_kernel(source, target, token):
    target[...] = source[...].astype(target.dtype)
    token[...] = jnp.zeros_like(token)


def pack_kernel(pieces, *refs):
    count = 1 + max(piece[0] for piece in pieces)
    sources, outs, (token, sems) = refs[:count], refs[count:-2], refs[-2:]
    token[...] = jnp.zeros_like(token)
    copies = []
    for (source, first, images), out in zip(pieces, outs):
        for row in range(SENT):
            copies.append(
                pltpu.make_async_copy(
                    sources[source].at[first : first + images, 2 * row + 1], out.at[:, row], sems.at[len(copies)]
                )
            )
    for copy in copies:
        copy.start()
    for copy in copies:
        copy.wait()


def pack_rows(sources, pieces, after=()):
    _, _, cols, width = sources[0].shape
    vector = pl.BlockSpec(memory_space=pltpu.VMEM)
    return launch(
        partial(pack_kernel, pieces),
        "pack_rows",
        (),
        sources,
        [pl.BlockSpec(memory_space=pl.ANY)] * len(sources),
        [shaped((count, SENT, cols, width), BF16) for _, _, count in pieces] + [TOKEN],
        [vector] * (len(pieces) + 1),
        scratch=[pltpu.SemaphoreType.DMA((SENT * len(pieces),))],
        after=after,
        vmem=60,
    )


def merge_rows(received, target, first):
    count, _, cols, width = received.shape
    unit = math.gcd(first, count)
    begin = first // unit
    return launch(
        merge_kernel,
        "merge_rows",
        (count // unit, SENT),
        (received,),
        [pl.BlockSpec((unit, 1, cols, width), lambda i, r: (i, r, 0, 0))],
        [shaped(target.shape, target.dtype), TOKEN],
        [pl.BlockSpec((unit, 1, cols, width), lambda i, r: (i + begin, 2 * r + 1, 0, 0)), whole(TOKEN.shape)],
        so_far=(target,),
    )


def position_layers(refs):
    (in_w, in_b, g1, s1, w1, b1, g2, s2, w2, b2, g3, s3, _) = refs
    width = in_w.shape[1]
    offset = lax.broadcasted_iota(jnp.int32, (OFFSETS, width), 0)
    rows = (offset // SPAN - (GROUP - 1)).astype(F32)
    cols = (offset % SPAN - (GROUP - 1)).astype(F32)
    hidden = rows * in_w[0:1, :] + cols * in_w[1:2, :] + in_b[...][None, :]
    kept = []
    for gain, shift, weight, bias in ((g1, s1, w1, b1), (g2, s2, w2, b2), (g3, s3, None, None)):
        hat, inverse = normalise(hidden)
        active, slope = gelu_both(hat * gain[...][None, :] + shift[...][None, :])
        kept.append((hat, inverse, active, slope))
        if weight is not None:
            hidden = dot(active, weight[...], HIGH) + bias[...][None, :]
    return rows, cols, kept


def pick_offsets(place):
    offset = lax.broadcasted_iota(jnp.int32, (OFFSETS, WIDE), 0)
    lane = lax.broadcasted_iota(jnp.int32, (OFFSETS, WIDE), 1)
    wanted = lane // PAD_COLS * SPAN + lane % PAD_COLS // 2 - place + GROUP - 1
    return jnp.where(offset == wanted, 1.0, 0.0).astype(F32)


def bias_kernel(*refs):
    ins, (out, strip) = refs[:13], refs[13:]
    _, _, kept = position_layers(ins)
    table = dot_nt(ins[12][...], kept[2][2], HIGH)
    lane = lax.broadcasted_iota(jnp.int32, (HEADS, WIDE), 1)
    even = lane % 2 == 0
    strip[...] = jnp.full(strip.shape, MASKED, F32)
    for place in range(GROUP):
        spread = dot(table, pick_offsets(place), HIGH)
        strip[:, 2 * place, 0:WIDE] = jnp.where(even, spread, MASKED)
        strip[:, 2 * place + 1, 0:WIDE] = jnp.where(even, MASKED, spread)
    for row in range(GROUP):
        start = (GROUP - 1 - row) * PAD_COLS
        out[:, row * PAD_COLS : (row + 1) * PAD_COLS, :] = strip[:, :, start : start + TOKENS]


def pair_bias(pos, through):
    return small_launch(
        bias_kernel,
        "pair_bias",
        pos,
        [shaped((HEADS, TOKENS, TOKENS), F32)],
        [pltpu.VMEM((HEADS, PAD_COLS, 2 * LANES), F32)],
        through=through,
        vmem=60,
    )


def put_pair(ref, start, values):
    high = values.astype(BF16)
    ref[start : start + SMALL, :] = high
    ref[start + SMALL : start + 2 * SMALL, :] = (values - high.astype(F32)).astype(BF16)


def get_pair(ref, start):
    return ref[start : start + SMALL, :].astype(F32) + ref[start + SMALL : start + 2 * SMALL, :].astype(F32)


def gather_small_kernel(feed_small, feed_b1, att_small, norm_small, grad_pair, out, small):
    width = feed_small.shape[1]
    strip = jnp.zeros((HEADS, PAD_COLS, WIDE), F32)
    for row in range(GROUP):
        start = (GROUP - 1 - row) * PAD_COLS
        piece = grad_pair[:, row * PAD_COLS : (row + 1) * PAD_COLS, :]
        strip = strip + jnp.pad(piece, ((0, 0), (0, 0), (start, WIDE - start - TOKENS)))
    table = jnp.zeros((HEADS, OFFSETS), F32)
    for place in range(GROUP):
        folded = strip[:, 2 * place, :] + strip[:, 2 * place + 1, :]
        table = table + dot_nt(folded, pick_offsets(place), HIGH)
    small[...] = jnp.zeros_like(small)
    small[0:4, :] = feed_small[0:4, :]
    small[4:6, :] = norm_small[0:2, :]
    small[6:8, :] = att_small[0:2, :]
    for part in range(feed_b1.shape[1] // width):
        small[8 + part : 9 + part, :] = feed_b1[:, part * width : (part + 1) * width]
    small[12 : 12 + HEADS, 0:OFFSETS] = table
    put_pair(out, 0, small[...])


def gather_small(feed_small, feed_b1, att_small, norm_small, grad_pair):
    width = feed_small.shape[1]
    return small_launch(
        gather_small_kernel,
        "gather_small",
        (feed_small, feed_b1, att_small, norm_small, grad_pair.reshape(HEADS, TOKENS, TOKENS)),
        [shaped((2 * SMALL, width), BF16)],
        [pltpu.VMEM((SMALL, width), F32)],
    )[0]


def finish_small_kernel(*refs):
    ins, small, outs = refs[:13], refs[13], refs[14:]
    (in_w, in_b, g1, s1, w1, b1, g2, s2, w2, b2, g3, s3, w3) = ins
    (o_n1_gain, o_n1_shift, o_qv, o_proj_b, o_n2_gain, o_n2_shift, o_fc1_b, o_fc2_b) = outs[:8]
    (o_in_w, o_in_b, o_g1, o_s1, o_w1, o_b1, o_g2, o_s2, o_w2, o_b2, o_g3, o_s3, o_w3) = outs[8:]
    o_n2_gain[...] = small[0, :]
    o_n2_shift[...] = small[1, :]
    o_fc2_b[...] = small[2, :]
    o_proj_b[...] = small[3, :]
    o_n1_gain[...] = small[4, :]
    o_n1_shift[...] = small[5, :]
    o_qv[...] = small[6:8, :]
    width = small.shape[1]
    for part in range(o_fc1_b.shape[0] // width):
        o_fc1_b[part * width : (part + 1) * width] = small[8 + part, :]
    rows, cols, kept = position_layers(ins)
    table = small[12 : 12 + HEADS, 0:OFFSETS]
    o_w3[...] = dot(table, kept[2][2], HIGH)
    grad_active = dot(table.T, w3[...], HIGH)
    stages = (
        (g3, o_g3, o_s3, o_b2, o_w2, w2),
        (g2, o_g2, o_s2, o_b1, o_w1, w1),
        (g1, o_g1, o_s1, o_in_b, None, None),
    )
    for level, (gain, o_gain, o_shift, o_bias, o_weight, weight) in zip((2, 1, 0), stages):
        hat, inverse, _, slope = kept[level]
        grad_norm = grad_active * slope
        o_gain[...] = jnp.sum(grad_norm * hat, axis=0)
        o_shift[...] = jnp.sum(grad_norm, axis=0)
        grad_hidden = normalise_back(grad_norm * gain[...][None, :], hat, inverse)
        o_bias[...] = jnp.sum(grad_hidden, axis=0)
        if weight is not None:
            o_weight[...] = dot(kept[level - 1][2].T, grad_hidden, HIGH)
            grad_active = dot_nt(grad_hidden, weight[...], HIGH)
        else:
            o_in_w[0:1, :] = column_sum(grad_hidden * rows)
            o_in_w[1:2, :] = column_sum(grad_hidden * cols)


def finish_small(pos, small, hidden):
    width = small.shape[1]
    shapes = [(width,), (width,), (2, width), (width,), (width,), (width,), (hidden,), (width,)]
    return small_launch(
        finish_small_kernel,
        "finish_small",
        (*pos, small),
        [shaped(s, F32) for s in shapes] + [shaped(p.shape, F32) for p in pos],
    )


def stack_heads(block, mask):
    return jnp.concatenate([block] * PER_BLOCK, axis=0) * mask


def place_rows(band, kept_ref, received_ref, padded):
    upper = band * SENT
    lower = (1 - band) * KEPT
    for row in range(KEPT):
        padded[:, row + upper, 0 : 2 * GROUP, :] = kept_ref[:, 2 * row]
    for row in range(SENT):
        padded[:, row + lower, 0 : 2 * GROUP, :] = received_ref[:, row]


def return_rows(band, placed, kept_ref, sent_ref):
    upper = band * SENT
    lower = (1 - band) * KEPT
    for row in range(KEPT):
        kept_ref[:, 2 * row] = placed[:, row + upper, 0 : 2 * GROUP, :]
    for row in range(SENT):
        sent_ref[:, row] = placed[:, row + lower, 0 : 2 * GROUP, :].astype(sent_ref.dtype)


def attend_kernel(count, where, images, received, gain, shift, weight, bias, pair, mask,
                  x_out, normed_out, qkv_out, probs_out, att_out, padded):
    width = images.shape[3]

    @pl.when(pl.program_id(0) == 0)
    def _():
        padded[...] = jnp.zeros_like(padded)

    place_rows(where[0], images, received, padded)
    x = padded[...].reshape(count * TOKENS, width)
    x_out[...] = x
    hat, _ = normalise(x.astype(F32))
    normed = (hat * gain[...][None, :] + shift[...][None, :]).astype(BF16)
    normed_out[...] = normed
    piece = dot(normed, weight[...])
    qkv_out[:, 0:width] = (piece[:, 0:width] + bias[0:1, :]).astype(BF16)
    qkv_out[:, width : 2 * width] = piece[:, width : 2 * width].astype(BF16)
    qkv_out[:, 2 * width :] = (piece[:, 2 * width :] + bias[1:2, :]).astype(BF16)
    masks = mask[...]
    for image in range(count):
        rows = slice(image * TOKENS, (image + 1) * TOKENS)
        for block in range(HEADS // PER_BLOCK):
            at = block * LANES
            query = qkv_out[rows, at : at + LANES]
            keys = stack_heads(qkv_out[rows, width + at : width + at + LANES], masks)
            vals = stack_heads(qkv_out[rows, 2 * width + at : 2 * width + at + LANES], masks)
            here = slice(block * STACK, (block + 1) * STACK)
            scores = dot_nt(keys, query) * SCALE + pair[here, :]
            scores = scores.reshape(PER_BLOCK, TOKENS, TOKENS)
            probs = jnp.exp(scores - jnp.max(scores, axis=1, keepdims=True))
            probs = probs * (1.0 / jnp.sum(probs, axis=1, keepdims=True))
            probs = probs.astype(BF16).reshape(STACK, TOKENS)
            probs_out[image, here, :] = probs
            att_out[rows, at : at + LANES] = dot_tn(probs, vals).astype(BF16)


def attend(where, images, received, first, per_step, gain, shift, weight, bias, pair, mask, so_far, through):
    total, _, cols, width = images.shape
    count = received.shape[0]
    begin = first // per_step
    rows = per_step * TOKENS
    row_spec = lambda w: pl.BlockSpec((rows, w), lambda i: (i + begin, 0))
    fixed = (gain, shift, weight, bias, pair.reshape(HEADS * TOKENS, TOKENS), mask)
    return launch(
        partial(attend_kernel, per_step),
        "attend",
        (count // per_step,),
        (where, images, received, *fixed),
        [
            pl.BlockSpec(memory_space=pltpu.SMEM),
            pl.BlockSpec((per_step, GROUP, cols, width), lambda i: (i + begin, 0, 0, 0)),
            pl.BlockSpec((per_step, SENT, cols, width), lambda i: (i, 0, 0, 0)),
        ]
        + [whole(a.shape) for a in fixed],
        [
            shaped((total * TOKENS, width), BF16),
            shaped((total * TOKENS, width), BF16),
            shaped((total * TOKENS, 3 * width), BF16),
            shaped((total, HEADS * TOKENS, TOKENS), BF16),
            shaped((total * TOKENS, width), BF16),
        ],
        [
            row_spec(width),
            row_spec(width),
            row_spec(3 * width),
            pl.BlockSpec((per_step, HEADS * TOKENS, TOKENS), lambda i: (i + begin, 0, 0)),
            row_spec(width),
        ],
        so_far=so_far,
        scratch=[pltpu.VMEM((per_step, GROUP, PAD_COLS, width), BF16)],
        flops=count * TOKENS * width * width * 12,
        through=through,
        vmem=60,
    )


def feed_kernel(count, where, cot, received, x_ref, att_ref, proj_w, proj_b, gain, shift, w1, b1, w2, b2,
                out_kept, grad_mid, grad_att, out_send, o_small, o_b1, o_first, o_second, a_proj,
                padded, placed, pair):
    width = x_ref.shape[1]
    hidden = w1.shape[1]
    step = pl.program_id(0)

    @pl.when(step == 0)
    def _():
        for ref in (padded, o_small, o_b1, pair, a_proj):
            ref[...] = jnp.zeros_like(ref)

    place_rows(where[0], cot, received, padded)
    up = padded[...].reshape(count * TOKENS, width)
    up_f = up.astype(F32)
    up_turned = up.T
    att = att_ref[...]
    middle = x_ref[...].astype(F32) + (dot(att, proj_w[...]) + proj_b[...][None, :])
    hat, inverse = normalise(middle)
    normed = (hat * gain[...][None, :] + shift[...][None, :]).astype(BF16)
    normed_turned = normed.T
    result = middle + b2[...][None, :]
    grad_normed = jnp.zeros((count * TOKENS, width), F32)
    for start in range(0, hidden, FEED_PART):
        cols = slice(start, start + FEED_PART)
        active, slope = gelu_both(dot(normed, w1[:, cols]) + b1[cols][None, :])
        active = active.astype(BF16)
        result = result + dot(active, w2[cols, :])
        grad_pre = (dot_nt(up, w2[cols, :]) * slope).astype(BF16)
        grad_normed = grad_normed + dot_nt(grad_pre, w1[:, cols])
        pair[0, :, cols] += dot(normed_turned, grad_pre)
        pair[1, :, cols] += dot(up_turned, active)
        o_b1[:, cols] += column_sum(grad_pre.astype(F32))
    placed[...] = result.astype(BF16).reshape(placed.shape)
    return_rows(where[0], placed, out_kept, out_send)
    grad_normed = grad_normed.astype(BF16).astype(F32)
    grad_middle = up_f + normalise_back(grad_normed * gain[...][None, :], hat, inverse)
    grad_mid[...] = grad_middle
    branch = grad_middle.astype(BF16)
    a_proj[...] += dot(att.T, branch)
    grad_att[...] = dot_nt(branch, proj_w[...]).astype(BF16)
    o_small[0:1, :] += column_sum(grad_normed * hat)
    o_small[1:2, :] += column_sum(grad_normed)
    o_small[2:3, :] += column_sum(up_f)
    o_small[3:4, :] += column_sum(branch.astype(F32))

    @pl.when(step == pl.num_programs(0) - 1)
    def _():
        core = where[1]
        for part in range(hidden // width):
            cols = slice(part * width, (part + 1) * width)
            o_first[part] = pair[core, :, cols].astype(BF16)
            o_second[part] = pair[1 - core, :, cols].astype(BF16)


def feed(where, cotangent, received, per_step, x, att, weights):
    total, _, cols, width = cotangent.shape
    hidden = weights[4].shape[1]
    rows = per_step * TOKENS
    row_spec = lambda w: pl.BlockSpec((rows, w), lambda i: (i, 0))
    image_spec = lambda n: pl.BlockSpec((per_step, n, cols, width), lambda i: (i, 0, 0, 0))
    accumulated = [
        shaped((8, width), F32),
        shaped((1, hidden), F32),
        shaped((hidden // width, width, width), BF16),
        shaped((hidden // width, width, width), BF16),
        shaped((width, width), F32),
    ]
    return launch(
        partial(feed_kernel, per_step),
        "feed",
        (total // per_step,),
        (where, cotangent, received, x, att, *weights),
        [pl.BlockSpec(memory_space=pltpu.SMEM), image_spec(GROUP), image_spec(SENT), row_spec(width), row_spec(width)]
        + [whole(a.shape) for a in weights],
        [
            shaped((total, GROUP, cols, width), BF16),
            shaped((total * TOKENS, width), F32),
            shaped((total * TOKENS, width), BF16),
            shaped((total, SENT, cols, width), BF16),
        ]
        + accumulated,
        [image_spec(GROUP), row_spec(width), row_spec(width), image_spec(SENT)]
        + [whole(a.shape) for a in accumulated],
        scratch=[
            pltpu.VMEM((per_step, GROUP, PAD_COLS, width), BF16),
            pltpu.VMEM((per_step, GROUP, PAD_COLS, width), BF16),
            pltpu.VMEM((2, width, hidden), F32),
        ],
        flops=total * TOKENS * width * width * 54,
        vmem=60,
    )


def pick_heads(stacked):
    parts = stacked.reshape(PER_BLOCK, TOKENS, LANES)
    lane = lax.broadcasted_iota(jnp.int32, (TOKENS, LANES), 1)
    picked = parts[PER_BLOCK - 1]
    for head in range(PER_BLOCK - 2, -1, -1):
        picked = jnp.where(lane < (head + 1) * HEAD_DIM, parts[head], picked)
    return picked


def back_kernel(count, first_call, last_call, where, normed, qkv, probs_ref, grad_att, mask, a_proj, *refs):
    carried = () if first_call else refs[:3]
    (grads, o_small, o_pair, o_first, o_second, a_w, packed) = refs[len(carried) :]
    width = normed.shape[1]
    step = pl.program_id(0)

    @pl.when(step == 0)
    def _():
        for index, ref in enumerate((o_small, o_pair, a_w)):
            ref[...] = jnp.zeros_like(ref) if first_call else carried[index][...]

    masks = mask[...]
    for image in range(count):
        rows = slice(image * TOKENS, (image + 1) * TOKENS)
        for block in range(HEADS // PER_BLOCK):
            at = block * LANES
            here = slice(block * STACK, (block + 1) * STACK)
            query = qkv[rows, at : at + LANES]
            keys = stack_heads(qkv[rows, width + at : width + at + LANES], masks)
            vals = stack_heads(qkv[rows, 2 * width + at : 2 * width + at + LANES], masks)
            grad = grad_att[rows, at : at + LANES]
            probs = probs_ref[image, here, :]
            exact = probs.astype(F32).reshape(PER_BLOCK, TOKENS, TOKENS)
            grad_probs = dot_nt(vals, grad).reshape(PER_BLOCK, TOKENS, TOKENS)
            inner = jnp.sum(grad_probs * exact, axis=1, keepdims=True)
            grad_scores = (exact * (grad_probs - inner)).reshape(STACK, TOKENS).astype(BF16)
            o_pair[here, :] += grad_scores.astype(F32)
            grads[rows, at : at + LANES] = (dot_tn(grad_scores, keys) * SCALE).astype(BF16)
            grads[rows, width + at : width + at + LANES] = (
                pick_heads(dot(grad_scores, query)) * SCALE
            ).astype(BF16)
            grads[rows, 2 * width + at : 2 * width + at + LANES] = pick_heads(
                dot(probs, grad)
            ).astype(BF16)
    all_grads = grads[...]
    a_w[...] += dot(normed[...].T, all_grads)
    o_small[0:1, :] += column_sum(all_grads[:, :width].astype(F32))
    o_small[1:2, :] += column_sum(all_grads[:, 2 * width :].astype(F32))

    @pl.when(step == pl.num_programs(0) - 1)
    def _():
        if last_call:
            core = where[1]
            for part in range(3):
                packed[part] = a_w[:, part * width : (part + 1) * width].astype(BF16)
            packed[3] = a_proj[...].astype(BF16)
            for part in range(2):
                o_first[part] = packed[2 * core + part]
                o_second[part] = packed[2 - 2 * core + part]
        else:
            o_first[...] = a_w[...]
            o_second[...] = jnp.zeros_like(o_second)


def attend_back(where, first, count, per_step, saved, mask, grad_proj, carried, so_far, last_call, after):
    normed, qkv, probs, grad_att = saved
    width = normed.shape[1]
    begin = first // per_step
    rows = per_step * TOKENS
    extra = () if carried is None else tuple(carried)
    row_spec = lambda w: pl.BlockSpec((rows, w), lambda i: (i + begin, 0))
    fixed = (mask, grad_proj)
    if last_call:
        first_shape = second_shape = shaped((2, width, width), BF16)
    else:
        first_shape = shaped((width, 3 * width), F32)
        second_shape = shaped((8, LANES), F32)
    accumulated = [
        shaped((8, width), F32),
        shaped((HEADS * TOKENS, TOKENS), F32),
        first_shape,
        second_shape,
    ]
    return launch(
        partial(back_kernel, per_step, carried is None, last_call),
        "attend_back",
        (count // per_step,),
        (where, normed, qkv, probs, grad_att, *fixed, *extra),
        [
            pl.BlockSpec(memory_space=pltpu.SMEM),
            row_spec(width),
            row_spec(3 * width),
            pl.BlockSpec((per_step, HEADS * TOKENS, TOKENS), lambda i: (i + begin, 0, 0)),
            row_spec(width),
        ]
        + [whole(a.shape) for a in (*fixed, *extra)],
        [shaped(qkv.shape, BF16)] + accumulated,
        [row_spec(3 * width)] + [whole(a.shape) for a in accumulated],
        so_far=so_far,
        scratch=[
            pltpu.VMEM((width, 3 * width), F32),
            pltpu.VMEM((4, width, width), BF16),
        ],
        flops=count * TOKENS * width * width * 18,
        after=after,
        vmem=60,
    )


def images_kernel(first_call, where, grads, x_ref, grad_mid, gain, weight, *refs):
    carried = () if first_call else refs[:1]
    (gi_kept, gi_send, o_small, placed) = refs[len(carried) :]

    @pl.when(pl.program_id(0) == 0)
    def _():
        o_small[...] = jnp.zeros_like(o_small) if first_call else carried[0][...]

    grad_normed = dot_nt(grads[...], weight[...]).astype(BF16).astype(F32)
    hat, inverse = normalise(x_ref[...].astype(F32))
    o_small[0:1, :] += column_sum(grad_normed * hat)
    o_small[1:2, :] += column_sum(grad_normed)
    grad_image = grad_mid[...] + normalise_back(grad_normed * gain[...][None, :], hat, inverse)
    placed[...] = grad_image.reshape(placed.shape)
    return_rows(where[0], placed, gi_kept, gi_send)


def image_grads(where, first, count, per_step, grads, x, grad_mid, gain, weight, shape, carried, so_far, after):
    total, _, cols, width = shape
    begin = first // per_step
    rows = per_step * TOKENS
    row_spec = lambda w: pl.BlockSpec((rows, w), lambda i: (i + begin, 0))
    fixed = (gain, weight, *carried)
    return launch(
        partial(images_kernel, not carried),
        "image_grads",
        (count // per_step,),
        (where, grads, x, grad_mid, *fixed),
        [pl.BlockSpec(memory_space=pltpu.SMEM), row_spec(3 * width), row_spec(width), row_spec(width)]
        + [whole(a.shape) for a in fixed],
        [
            shaped((total, GROUP, cols, width), F32),
            shaped((count, SENT, cols, width), BF16),
            shaped((8, width), F32),
        ],
        [
            pl.BlockSpec((per_step, GROUP, cols, width), lambda i: (i + begin, 0, 0, 0)),
            pl.BlockSpec((per_step, SENT, cols, width), lambda i: (i, 0, 0, 0)),
            whole((8, width)),
        ],
        so_far=so_far,
        scratch=[pltpu.VMEM((per_step, GROUP, PAD_COLS, width), F32)],
        flops=count * TOKENS * width * width * 6,
        after=after,
        vmem=32,
    )


def swap(value, flip):
    bands, batches = lax.axis_size("band"), lax.axis_size("batch")
    pairs = []
    for band in range(bands):
        for batch in range(batches):
            other = (band ^ flip[0]) * batches + (batch ^ flip[1])
            pairs.append((band * batches + batch, other))
    return lax.ppermute(value, ("band", "batch"), pairs)


def in_plane(value, d):
    return swap(value, (d >> 1, (d & 1) << 1))


PLANE = 4
ALONG = 4


def tree_sum(values):
    while len(values) > 1:
        values = [values[i] + values[i + 1] for i in range(0, len(values), 2)]
    return values[0]


def split_kernel(slot, count, small_rows, where, *refs):
    *refs, token = refs
    token[...] = jnp.zeros_like(token)
    outs = refs[-count - (1 if small_rows else 0) :]
    ins = refs[: len(refs) - len(outs)]
    me = where[slot]
    rows = outs[0].shape[0]
    if small_rows:
        ins, small_ins = ins[:small_rows], ins[small_rows:]
        small = tree_sum([r[...] if r.dtype == F32 else get_pair(r, r.shape[0] - 2 * SMALL) for r in small_ins])

    def total(index):
        start = pl.multiple_of(index * rows, rows)
        return tree_sum([ref[pl.ds(start, rows), :].astype(F32) for ref in ins])

    for d in range(count):
        outs[d][0:rows, :] = total(me ^ d).astype(outs[d].dtype)
        if small_rows and d > 0:
            put_pair(outs[d], rows, small)
    if small_rows:
        high = small.astype(BF16).astype(F32)
        outs[count][...] = high + (small - high).astype(BF16).astype(F32)


def split_share(where, slot, count, values, after, flops=0):
    rows, width = values[0].shape
    size = rows // count
    outs = [shaped((size, width), F32 if d == 0 else BF16) for d in range(count)] + [TOKEN]
    return small_launch(
        partial(split_kernel, slot, count, 0), "split_share", (where, *values), outs, after=after,
        flops=flops,
    )


def split_with_small(where, slot, count, values, smalls, after):
    rows, width = values[0].shape
    size = rows // count
    outs = [shaped((size, width), F32)] + [shaped((size + 2 * SMALL, width), BF16)] * (count - 1)
    outs += [shaped((SMALL, width), F32), TOKEN]
    return small_launch(
        partial(split_kernel, slot, count, len(values)), "split_with_small", (where, *values, *smalls), outs, after=after,
    )


def join_kernel(count, *refs):
    early, late = refs[:count], refs[count : 2 * count]
    small, share, small_out = refs[2 * count :]
    rows, more = early[0].shape[0], late[0].shape[0]
    share[0:rows, :] = tree_sum([r[...].astype(F32) for r in early]).astype(BF16)
    share[rows : rows + more, :] = tree_sum([r[0:more, :].astype(F32) for r in late]).astype(BF16)
    small_out[...] = tree_sum([small[...]] + [get_pair(r, more) for r in late[1:]])


def join_shares(early, late, small, after):
    rows, width = early[0].shape
    return small_launch(
        partial(join_kernel, len(early)),
        "join_shares",
        (*early, *late, small),
        [shaped((rows + late[0].shape[0], width), BF16), shaped((SMALL, width), F32)],
        after=after,
    )


def lay_kernel(slot, where, *refs):
    parts, (small, other, out) = refs[:-3], refs[-3:]
    rows = parts[0].shape[0]
    for d, ref in enumerate(parts):
        out[pl.ds(pl.multiple_of((where[slot] ^ d) * rows, rows), rows), :] = ref[...]
    put_pair(out, len(parts) * rows, small[...] + other[...])


def along(value, d):
    return swap(value, (0, 4 * d))


def spread(pieces, send):
    return [pieces[0]] + [send(piece, d) for d, piece in enumerate(pieces) if d > 0]


def gather_along(where, share, small, after):
    rows, width = share.shape
    parts = spread([share] * ALONG, along)
    return small_launch(
        partial(lay_kernel, 3),
        "lay",
        (where, *parts, small, swap(small, (0, 1))),
        [shaped((ALONG * rows + 2 * SMALL, width), BF16)],
        after=after,
    )[0]


def halve_kernel(across, along_row, low, high):
    low[...] = across[0 : low.shape[0], :]
    high[...] = along_row[low.shape[0] :, :]


def collect_kernel(own, across, along_row, low, high, out, small):
    rows, cut = out.shape[1], low.shape[0]
    out[0] = along_row[0:rows, :]
    out[1] = across[0:rows, :]
    out[2, 0:cut, :] = low[...]
    out[2, cut:rows, :] = high[0 : rows - cut, :]
    far = get_pair(high, rows - cut)
    small[...] = (get_pair(own, rows) + get_pair(along_row, rows)) + (get_pair(across, rows) + far)


def gather_plane(quarter, after):
    theirs = swap(quarter, (0, 1))
    rows, width = quarter.shape
    across, along_row = in_plane(quarter, 2), in_plane(quarter, 1)
    cut = rows // 32 * 16
    low, high = small_launch(
        halve_kernel, "halve", (across, along_row), [shaped((cut, width), BF16), shaped((rows - cut, width), BF16)],
        after=after,
    )
    mine, small = small_launch(
        collect_kernel,
        "collect",
        (quarter, across, along_row, in_plane(low, 1), in_plane(high, 2)),
        [shaped((PLANE - 1, rows - 2 * SMALL, width), BF16), shaped((SMALL, width), F32)],
    )
    return small, (quarter, mine), (theirs, swap(mine, (0, 1)))


def unpack_kernel(flip, early, where, first, rest, o_w1, o_w2, o_qkv, o_proj, feed_buf, att_buf, sems):
    me, side = where[2], where[1] ^ flip
    width = o_proj.shape[0]
    late = width // 2 // ALONG
    low, high = slice(0, width // 2), slice(width // 2, width)
    for d in range(PLANE):
        quarter = first if d == 0 else rest.at[d - 1]
        for share in range(ALONG):
            start = share * (early + late)
            feed_buf[d, share * early : (share + 1) * early, :] = quarter[start : start + early, :].astype(F32)
            att_buf[me ^ d, share * late : (share + 1) * late, :] = quarter[
                start + early : start + early + late, :
            ].astype(F32)

    def send(copies):
        for index, (source, target) in enumerate(copies):
            pltpu.make_async_copy(source, target, sems.at[index]).start()
        for index, (source, target) in enumerate(copies):
            pltpu.make_async_copy(source, target, sems.at[index]).wait()

    def place(d):
        return pl.ds(pl.multiple_of((me ^ d) * width, width), width)

    def halves(target, cols, at):
        return [(att_buf.at[at], target.at[low, cols]), (att_buf.at[at + 1], target.at[high, cols])]

    @pl.when(side == 0)
    def _():
        copies = [(feed_buf.at[d], o_w1.at[:, place(d)]) for d in range(PLANE)]
        copies += halves(o_qkv, slice(0, width), 0) + halves(o_qkv, slice(width, 2 * width), 2)
        send(copies)

    @pl.when(side == 1)
    def _():
        for d in range(PLANE):
            feed_buf[d] = feed_buf[d].T
        copies = [(feed_buf.at[d], o_w2.at[place(d), :]) for d in range(PLANE)]
        copies += halves(o_qkv, slice(2 * width, 3 * width), 0) + halves(o_proj, slice(0, width), 2)
        send(copies)


def unpack(flip, early, where, half, shapes, so_far):
    width = half[0].shape[1]
    vector = pl.BlockSpec(memory_space=pltpu.VMEM)
    return launch(
        partial(unpack_kernel, flip, early),
        "unpack",
        (),
        (where, *half),
        [pl.BlockSpec(memory_space=pltpu.SMEM), vector, vector],
        [shaped(shape, F32) for shape in shapes],
        [pl.BlockSpec(memory_space=pl.ANY)] * len(shapes),
        so_far=so_far,
        scratch=[
            pltpu.VMEM((PLANE, width, width), F32),
            pltpu.VMEM((PLANE, width // 2, width), F32),
            pltpu.SemaphoreType.DMA((2 * PLANE,)),
        ],
        vmem=24,
    )


def body(images, cotangent, norm1_gain, norm1_shift, qkv_weight, qv_bias, proj_weight, proj_bias, *rest):
    pos = rest[:13]
    norm2_gain, norm2_shift, fc1_weight, fc1_bias, fc2_weight, fc2_bias = rest[13:]
    total, _, cols, width = images.shape
    hidden = fc1_weight.shape[1]
    per_step = 4
    band, batch = lax.axis_index("band"), lax.axis_index("batch")
    where = jnp.stack([band, batch % 2, band * 2 + batch // 2 % 2, batch // 4 % ALONG]).astype(jnp.int32)
    head_of_row = np.arange(STACK)[:, None] // TOKENS
    mask = jnp.asarray(head_of_row == np.arange(LANES)[None, :] // HEAD_DIM, BF16)
    to_partner = lambda value: swap(value, (1, 0))
    pos = (*pos[:12], pos[12].T)

    later = (total // per_step * 2 // 5) * per_step
    image_chunks = [(0, later), (later, total - later)]
    packed, token = pack_rows((images,), [(0, *image_chunks[0])])
    received = to_partner(packed)
    later_packed, cot_packed, _ = pack_rows(
        (images, cotangent), [(0, *image_chunks[1]), (1, 0, total)], (token,)
    )
    pair, later_packed, cot_packed = pair_bias(pos, (later_packed, cot_packed))
    later_received = to_partner(later_packed)
    norm_one = (norm1_gain, norm1_shift, qkv_weight, qv_bias, pair, mask)
    so_far = attend(where, images, received, 0, per_step, *norm_one, (), ())
    _, cot_packed = small_launch(
        token_kernel, "order", (), [TOKEN], after=(*so_far[:1], later_received), vmem=60, through=(cot_packed,)
    )
    cot_rows = to_partner(cot_packed)
    so_far = attend(where, images, later_received, later, per_step, *norm_one, so_far, ())
    x, normed, qkv, probs, att = so_far
    weights = (proj_weight, proj_bias, norm2_gain, norm2_shift, fc1_weight, fc1_bias, fc2_weight, fc2_bias)
    result = feed(where, cotangent, cot_rows, per_step, x, att, weights)
    out_images, grad_mid, grad_att, out_sent, feed_small, feed_b1, mine, theirs, grad_proj = result
    out_rows = to_partner(out_sent)
    flat = lambda value: value.reshape(-1, width)
    early = [flat(mine), swap(flat(theirs), (0, 1))]

    saved = (normed, qkv, probs, grad_att)
    chunks = [(0, total - later), (total - later, later)]
    result = attend_back(where, *chunks[0], per_step, saved, mask, grad_proj, None, (), False, ())
    *pieces, token = split_share(where, 2, PLANE, early, (result[1],))
    early = spread(pieces, in_plane)
    result = attend_back(where, *chunks[1], per_step, saved, mask, grad_proj, result[1:4], result[:1], True,
                         (token, out_rows))
    grads, att_small, grad_pair = result[:3]
    mine, theirs = flat(result[3]), flat(result[4])
    *pieces, token = split_share(where, 3, ALONG, early, (att_small,), 5e9)
    early = spread(pieces, along)
    *pieces, token = split_share(where, 2, PLANE, [mine, swap(theirs, (0, 1))], (token,))
    late = spread(pieces, in_plane)
    grad_images, sent, norm_small = image_grads(where, 0, total, per_step, grads, x, grad_mid, norm1_gain,
                                                qkv_weight, images.shape, (), (), (token,))
    grad_rows = to_partner(sent)
    small = gather_small(feed_small, feed_b1, att_small, norm_small, grad_pair)
    *pieces, small, _ = split_with_small(where, 3, ALONG, late, [small], early[1:])
    late = spread(pieces, along)
    share, small = join_shares(early, late, small, ())
    stride = PLANE * ALONG
    while stride < lax.axis_size("batch"):
        share = (share.astype(F32) + swap(share, (0, stride)).astype(F32)).astype(BF16)
        small = small + swap(small, (0, stride))
        stride *= 2
    out_images, token = merge_rows(out_rows, out_images, 0)
    quarter = gather_along(where, share, small, (token,))
    grad_images, token = merge_rows(grad_rows, grad_images, 0)
    small, half, other_half = gather_plane(quarter, (token,))
    smalls = finish_small(pos, small, hidden)
    shapes = [w.shape for w in (fc1_weight, fc2_weight, qkv_weight, proj_weight)]
    large = unpack(0, early[0].shape[0], where, half, shapes, ())
    grad_fc1, grad_fc2, grad_qkv, grad_proj = unpack(1, early[0].shape[0], where, other_half, shapes, large)
    n1_gain, n1_shift, qv, proj_b, n2_gain, n2_shift, fc1_b, fc2_b = smalls[:8]
    return (out_images, grad_images, n1_gain, n1_shift, grad_qkv, qv, grad_proj, proj_b, *smalls[8:20], smalls[20].T,
            n2_gain, n2_shift, grad_fc1, fc1_b, grad_fc2, fc2_b)


def solution(mesh):
    tokens = P("batch", "band", None, None)
    return jax.shard_map(
        body,
        mesh=mesh,
        in_specs=(tokens, tokens) + (P(),) * 25,
        out_specs=(tokens, tokens) + (P(),) * 25,
        check_vma=False,
    )
```

time: 900 us -> 182 us (0.20); the launches traced: 884 us -> 182 us
  waiting for transfers between devices: 349 us -> 26.4 us
  local copies, waits for them, and re-layouts: 250 us -> 4.9 us
  matrix products: 187 us -> 0 us
  Pallas kernels: 0 us -> 117 us
  other arithmetic: 77.6 us -> 0.59 us
  starting transfers between devices: 4.08 us -> 31.9 us
  between operations: 16 us -> 1.41 us
    psum x2 -> x0, waiting for transfers between devices: 315 us -> none  [body(): summed = lax.psum(tuple(attention_set) + tuple(ffn_set), ('band', 'batch'))]
    dot_general x31 -> x0, matrix products: 187 us -> none  [the longest x1 31.6 us: body(): jnp.dot(flat_normed2, fc1_weight, preferred_element_type=jnp.float32)]
    pallas_call x0 -> x24, Pallas kernels: none -> 117 us  [launch(): pl.pallas_call(kernel, grid=grid, in_specs=list(in_specs) + [pl.BlockSpec...]
    reshape x20 -> x0, local copies, waits for them, and re-layouts: 77.6 us -> none  [the longest x2 8.27 us: join_groups(): return parted.reshape(img_count, GROUP, 2 * GROUP, model_width)]
    reduce_sum x22 -> x0, other arithmetic: 59.9 us -> none  [the longest x4 13.6 us: layer_norm(): return centred * lax.rsqrt(variance + EPSILON) * norm_gain + norm_shift]
    convert_element_type x9 -> x0, local copies, waits for them, and re-layouts: 47.9 us -> none  [the longest x2 21.5 us: body(): attended.reshape(group_count, GROUP * GROUP, model_width)]
    slice x10 -> x0, local copies, waits for them, and re-layouts: 47.6 us -> none  [the longest x2 22.1 us: body(): partner_rows = from_partner(normed[:, 1::2], 'band', 0)]
    unnamed x264 -> x70, local copies, waits for them, and re-layouts: 36.3 us -> 4.9 us
  transfers between devices with their start and end apart: 6 -> 29, of which waited for: 5 -> 8; matrix products, arithmetic and copies ran while one was open for 6% -> 0% of each run, Pallas kernels for 0% -> 41%
where the time goes in v1:
time: 182 us
  Pallas kernels  117 us (64%)
  starting transfers between devices  31.9 us (18%)
  waiting for transfers between devices  26.4 us (15%)
  local copies, waits for them, and re-layouts  4.9 us (3%)
    pallas_call x24, Pallas kernels, launch(): pl.pallas_call(kernel, grid=grid, in_specs=list(in_specs) + [pl.BlockSpec...  117 us
    ppermute x29, starting transfers between devices, swap(): return lax.ppermute(value, ('band', 'batch'), pairs)  31.9 us
    ppermute x29, waiting for transfers between devices, swap(): return lax.ppermute(value, ('band', 'batch'), pairs)  26.4 us
    unnamed x70, local copies, waits for them, and re-layouts  4.9 us
  transfers between devices with their start and end apart: 29, of which 8 were waited for; matrix products, arithmetic and copies ran while one was open for 0% of the time, Pallas kernels for 41%

profile of v1, /device:TPU:0, one launch (start us, length us, event | category | flops | bytes accessed | tf_op | source)
XLA Modules:
  0.0 181.9 jit_solution(1907896414871888349)
XLA Ops:
  0.7 1.7 pack_rows.2
  2.4 3.0 %collective-permute-start = (bf16[8,3,14,384]{3,2,1,0:T(8,128)(2,1)}, bf16[8,3,14,384]{3,2,1,0:T(8,128)(2,1)S(1)}, u32[]{:S(2)}, u32[]{:S(2)}) collective-permute-start(bf16[8,3,14,384]{3,2,1,0:T(8,128)(2,1)} %get-tuple-element.125), channel_id=1, source_target_pairs={{0,16},{1,17},{2,18},{3,19},{4,20},{5,21},{6,22},{7,23},{8,24},{9,... | collective-permute-start | bytes 774152 | tf_op jit(solution)/shard_map/ppermute | solution.py:675
  5.4 2.4 %pack_rows.3 = (bf16[12,3,14,384]{3,2,1,0:T(8,128)(2,1)}, bf16[20,3,14,384]{3,2,1,0:T(8,128)(2,1)}, f32[8,128]{1,0:T(8,128)}) custom-call(bf16[20,7,14,384]{3,2,1,0:T(8,128)(2,1)} %refs_1_.6, bf16[20,7,14,384]{3,2,1,0:T(8,128)(2,1)} %cot.1, f32[8,128]{1,0:T(8,128)} %get-tuple-element.126.refs_2_), custom_call_target="tpu_custom_call" | custom-call | bytes 4046848 | tf_op jit(solution)/shard_map/pack_rows/pallas_call | solution.py:87
  7.8 4.3 %pair_bias.1 = (f32[12,112,112]{2,1,0:T(8,128)}, bf16[12,3,14,384]{3,2,1,0:T(8,128)(2,1)}, bf16[20,3,14,384]{3,2,1,0:T(8,128)(2,1)}) custom-call(f32[2,96]{1,0:T(2,128)} %refs_0_.7, f32[96]{0:T(128)} %refs_1_.7, f32[96]{0:T(128)} %refs_2_.3, f32[96]{0:T(128)} %refs_3_.5, f32[96,96]{1,0:T(8,128)} %refs_4_.7, ...), custom_call_target="tpu_custom_call", output_to_operand_aliasing={{1}: (13, {}), {2}: (14, {})} | custom-call | bytes 684672 | tf_op jit(solution)/shard_map/pair_bias/pallas_call | solution.py:87
  13.5 8.7 %attend.2 = (bf16[2240,384]{1,0:T(8,128)(2,1)}, bf16[2240,384]{1,0:T(8,128)(2,1)}, bf16[2240,1152]{1,0:T(8,128)(2,1)}, bf16[20,1344,112]{2,1,0:T(8,128)(2,1)}, bf16[2240,384]{1,0:T(8,128)(2,1)}) custom-call(s32[4]{0:T(128)} %pad_add_fusion.where.refs_0_, bf16[20,7,14,384]{3,2,1,0:T(8,128)(2,1)} %refs_1_.6, bf16[8,3,14,384]{3,2,1,0:T(8,128)(2,1)} %copy-done.32, ...), custom_call_target="tpu_custom_call" | custom-call | flops 1585446912 | bytes 19714064 | tf_op jit(solution)/shard_map/attend/pallas_call | solution.py:87
  22.2 1.8 collective-permute-done.1.refs_1_.refs_2_
  25.6 11.7 %attend.3 = (bf16[2240,384]{1,0:T(8,128)(2,1)}, bf16[2240,384]{1,0:T(8,128)(2,1)}, bf16[2240,1152]{1,0:T(8,128)(2,1)}, bf16[20,1344,112]{2,1,0:T(8,128)(2,1)}, bf16[2240,384]{1,0:T(8,128)(2,1)}) custom-call(s32[4]{0:T(128)} %pad_add_fusion.where.refs_0_, ...), custom_call_target="tpu_custom_call", output_to_operand_aliasing={{0}: (9, {}), {1}: (10, {}), {2}: (11, {}), {3}: (12, {}), ... | custom-call | flops 2378170368 | bytes 19843088 | tf_op jit(solution)/shard_map/attend/pallas_call | solution.py:87
  37.3 5.2 %collective-permute-done.2.received = bf16[20,3,14,384]{3,2,1,0:T(8,128)(2,1)S(1)} collective-permute-done((bf16[20,3,14,384]{3,2,1,0:T(8,128)(2,1)}, bf16[20,3,14,384]{3,2,1,0:T(8,128)(2,1)S(1)}, u32[]{:S(2)}, u32[]{:S(2)}) %collective-permute-start.2) | collective-permute-done | bytes 645152 | tf_op jit(solution)/shard_map/ppermute | solution.py:675
  43.4 34.4 %feed.1 = (bf16[20,7,14,384]{3,2,1,0:T(8,128)(2,1)}, f32[2240,384]{1,0:T(8,128)}, bf16[2240,384]{1,0:T(8,128)(2,1)}, bf16[20,3,14,384]{3,2,1,0:T(8,128)(2,1)}, f...) custom-call(s32[4]{0:T(128)} %pad_add_fusion.where.refs_0_, ...), custom_call_target="tpu_custom_call" | custom-call | flops 17836277760 | bytes 18536464 | tf_op jit(solution)/shard_map/feed/pallas_call | solution.py:87
  78.8 15.6 %attend_back.2 = (bf16[2240,1152]{1,0:T(8,128)(2,1)}, f32[8,384]{1,0:T(8,128)}, f32[1344,112]{1,0:T(8,128)}, f32[384,1152]{1,0:T(8,128)}, f32[8,128]{1,0:T(8,128)}) custom-call(s32[4]{0:T(128)} %pad_add_fusion.where.refs_0_, bf16[2240,384]{1,0:T(8,128)(2,1)} %get-tuple-element.143.normed.refs_1_, bf16[2240,1152]{1,0:T(8,128)(2,1)} %get-tuple-element.144.qkv.refs_2_, ...), custom_call_target="tpu_custom_call" | custom-call | flops 3567255552 | bytes 22876176 | tf_op jit(solution)/shard_map/attend_back/pallas_call | solution.py:87
  95.2 1.5 split_share.3
  96.7 1.5 collective-permute-start.6
  101.0 12.5 %attend_back.3 = (bf16[2240,1152]{1,0:T(8,128)(2,1)}, f32[8,384]{1,0:T(8,128)}, f32[1344,112]{1,0:T(8,128)}, bf16[2,384,384]{2,1,0:T(8,128)(2,1)}, bf16[2,384,384]{2,1,0:T(8,128)(2,1)}) custom-call(s32[4]{0:T(128)} %pad_add_fusion.where.refs_0_, bf16[2240,384]{1,0:T(8,128)(2,1)} %get-tuple-element.143.normed.refs_1_, ...), custom_call_target="tpu_custom_call", output_to_operand_aliasing={{0}: (10, {})} | custom-call | flops 2378170368 | bytes 24666128 | tf_op jit(solution)/shard_map/attend_back/pallas_call | solution.py:87
  115.2 1.6 collective-permute-start.10
  116.8 2.6 %collective-permute-start.11 = (bf16[96,384]{1,0:T(8,128)(2,1)S(1)}, bf16[96,384]{1,0:T(8,128)(2,1)S(1)}, u32[]{:S(2)}, u32[]{:S(2)}) collective-permute-start(bf16[96,384]{1,0:T(8,128)(2,1)S(1)} %get-tuple-element.171), channel_id=1, source_target_pairs={{0,8},{1,9},{2,10},{3,11},{4,12},{5,13},{6,14},{7,15},{8,0},{9,1},... | collective-permute-start | bytes 221192 | tf_op jit(solution)/shard_map/ppermute | solution.py:675
  120.4 1.6 collective-permute-start.13
  124.0 7.0 %image_grads.1 = (f32[20,7,14,384]{3,2,1,0:T(8,128)}, bf16[20,3,14,384]{3,2,1,0:T(8,128)(2,1)S(1)}, f32[8,384]{1,0:T(8,128)S(1)}) custom-call(s32[4]{0:T(128)S(1)} %copy-done.11, bf16[2240,1152]{1,0:T(8,128)(2,1)S(1)} %bitcast.13, bf16[2240,384]{1,0:T(8,128)(2,1)S(1)} %copy-done, f32[2240,384]{1,0:T(8,128)S(1)} %copy-done.2, f32[384]{0:T(512)S(1)} %copy-done.17, ...), custom_call_target="tpu_custom_call" | custom-call | flops 1981808640 | bytes 14876176 | tf_op jit(solution)/shard_map/image_grads/pallas_call | solution.py:87
  134.2 3.5 %collective-permute-start.17 = (bf16[96,384]{1,0:T(8,128)(2,1)S(1)}, bf16[96,384]{1,0:T(8,128)(2,1)S(1)}, u32[]{:S(2)}, u32[]{:S(2)}) collective-permute-start(bf16[96,384]{1,0:T(8,128)(2,1)S(1)} %get-tuple-element.183), channel_id=1, source_target_pairs={{0,8},{1,9},{2,10},{3,11},{4,12},{5,13},{6,14},{7,15},{8,0},{9,1},... | collective-permute-start | bytes 221192 | tf_op jit(solution)/shard_map/ppermute | solution.py:675
  139.1 2.8 %collective-permute-done.17.refs_6_ = bf16[96,384]{1,0:T(8,128)(2,1)S(1)} collective-permute-done((bf16[96,384]{1,0:T(8,128)(2,1)S(1)}, bf16[96,384]{1,0:T(8,128)(2,1)S(1)}, u32[]{:S(2)}, u32[]{:S(2)}) %collective-permute-start.17) | collective-permute-done | bytes 73760 | tf_op jit(solution)/shard_map/ppermute | solution.py:675
  141.8 2.1 %collective-permute-done.18.refs_7_ = bf16[96,384]{1,0:T(8,128)(2,1)S(1)} collective-permute-done((bf16[96,384]{1,0:T(8,128)(2,1)S(1)}, bf16[96,384]{1,0:T(8,128)(2,1)S(1)}, u32[]{:S(2)}, u32[]{:S(2)}) %collective-permute-start.18) | collective-permute-done | bytes 73760 | tf_op jit(solution)/shard_map/ppermute | solution.py:675
  144.0 1.7 collective-permute-start.20
  145.7 2.7 %collective-permute-start.21 = (bf16[144,384]{1,0:T(8,128)(2,1)S(1)}, bf16[144,384]{1,0:T(8,128)(2,1)S(1)}, u32[]{:S(2)}, u32[]{:S(2)}) collective-permute-start(bf16[144,384]{1,0:T(8,128)(2,1)S(1)} %get-tuple-element.186.refs_1_), channel_id=1, source_target_pairs={{0,12},{1,13},{2,14},{3,15},{4,8},{5,9},{6,10},{7,11},{8,4},{9,5},... | collective-permute-start | bytes 331784 | tf_op jit(solution)/shard_map/ppermute | solution.py:675
  148.4 1.5 merge_rows.2
  150.4 2.8 %collective-permute-done.20.refs_3_ = bf16[144,384]{1,0:T(8,128)(2,1)S(1)} collective-permute-done((bf16[144,384]{1,0:T(8,128)(2,1)S(1)}, bf16[144,384]{1,0:T(8,128)(2,1)S(1)}, u32[]{:S(2)}, u32[]{:S(2)}) %collective-permute-start.20) | collective-permute-done | bytes 110624 | tf_op jit(solution)/shard_map/ppermute | solution.py:675
  155.0 1.5 collective-permute-start.24
  156.5 1.7 merge_rows.3
  158.2 6.7 %collective-permute-done.23.refs_0_.across = bf16[624,384]{1,0:T(8,128)(2,1)S(1)} collective-permute-done((bf16[624,384]{1,0:T(8,128)(2,1)S(1)}, bf16[624,384]{1,0:T(8,128)(2,1)S(1)}, u32[]{:S(2)}, u32[]{:S(2)}) %collective-permute-start.23) | collective-permute-done | bytes 479264 | tf_op jit(solution)/shard_map/ppermute | solution.py:675
  166.2 1.6 collective-permute-start.25
  167.8 4.5 %collective-permute-done.25.low = bf16[304,384]{1,0:T(8,128)(2,1)S(1)} collective-permute-done((bf16[304,384]{1,0:T(8,128)(2,1)S(1)}, bf16[304,384]{1,0:T(8,128)(2,1)S(1)}, u32[]{:S(2)}, u32[]{:S(2)}) %collective-permute-start.25) | collective-permute-done | bytes 233504 | tf_op jit(solution)/shard_map/ppermute | solution.py:675
  173.1 2.5 %unpack.2 = (f32[384,1536]{1,0:T(8,128)}, f32[1536,384]{1,0:T(8,128)}, f32[384,1152]{1,0:T(8,128)}, f32[384,384]{1,0:T(8,128)}) custom-call(s32[4]{0:T(128)S(1)} %copy-done.11, bf16[624,384]{1,0:T(8,128)(2,1)S(1)} %lay.1.own.first, bf16[3,576,384]{2,1,0:T(8,128)(2,1)S(1)} %get-tuple-element.195.rest), custom_call_target="tpu_custom_call" | custom-call | bytes 8884240 | tf_op jit(solution)/shard_map/unpack/pallas_call | solution.py:87
  175.8 2.6 %finish_small.1 = (f32[384]{0:T(512)}, f32[384]{0:T(512)}, f32[2,384]{1,0:T(2,128)}, f32[384]{0:T(512)}, f32[384]{0:T(512)}, /*index=5*/f32[384]{0:T(512)}, f32[...) custom-call(f32[2,96]{1,0:T(2,128)S(1)} %copy-done.20, ...), custom_call_target="tpu_custom_call" | custom-call | bytes 220416 | tf_op jit(solution)/shard_map/finish_small/pallas_call | solution.py:87
  178.4 3.3 %unpack.3 = (f32[384,1536]{1,0:T(8,128)}, f32[1536,384]{1,0:T(8,128)}, f32[384,1152]{1,0:T(8,128)}, f32[384,384]{1,0:T(8,128)}) custom-call(s32[4]{0:T(128)S(1)} %copy-done.11, bf16[624,384]{1,0:T(8,128)(2,1)S(1)} %collective-permute-done.27.refs_1_, ...), custom_call_target="tpu_custom_call", output_to_operand_aliasing={{0}: (3, {}), {1}: (4, {}), {2}: (5, {}), {3}: (6, {})} | custom-call | bytes 8884240 | tf_op jit(solution)/shard_map/unpack/pallas_call | solution.py:87
  (122 shorter events, 21.7 us)
Async XLA Ops:
  2.4 10.3 %collective-permute-start = (bf16[8,3,14,384]{3,2,1,0:T(8,128)(2,1)}, bf16[8,3,14,384]{3,2,1,0:T(8,128)(2,1)S(1)}, u32[]{:S(2)}, u32[]{:S(2)}) collective-permute-start(bf16[8,3,14,384]{3,2,1,0:T(8,128)(2,1)} %get-tuple-element.125), channel_id=1, source_target_pairs={{0,16},{1,17},{2,18},{3,19},{4,20},{5,21},{6,22},{7,23},{8,24},{9,... | collective-permute-start | bytes 774152 | tf_op jit(solution)/shard_map/ppermute | solution.py:675
  12.1 11.8 %collective-permute-start.1 = (bf16[12,3,14,384]{3,2,1,0:T(8,128)(2,1)}, bf16[12,3,14,384]{3,2,1,0:T(8,128)(2,1)S(1)}, u32[]{:S(2)}, u32[]{:S(2)}) collective-permute-start(bf16[12,3,14,384]{3,2,1,0:T(8,128)(2,1)} %get-tuple-element.131), channel_id=1, source_target_pairs={{0,16},{1,17},{2,18},{3,19},{4,20},{5,21},{6,22},{7,23},{8,24},{9,... | collective-permute-start | bytes 1161224 | tf_op jit(solution)/shard_map/ppermute | solution.py:675
  25.3 17.2 %collective-permute-start.2 = (bf16[20,3,14,384]{3,2,1,0:T(8,128)(2,1)}, bf16[20,3,14,384]{3,2,1,0:T(8,128)(2,1)S(1)}, u32[]{:S(2)}, u32[]{:S(2)}) collective-permute-start(bf16[20,3,14,384]{3,2,1,0:T(8,128)(2,1)} %get-tuple-element.133), channel_id=1, source_target_pairs={{0,16},{1,17},{2,18},{3,19},{4,20},{5,21},{6,22},{7,23},{8,24},{9,... | collective-permute-start | bytes 1935368 | tf_op jit(solution)/shard_map/ppermute | solution.py:675
  77.8 16.7 %collective-permute-start.4 = (bf16[1536,384]{1,0:T(8,128)(2,1)}, bf16[1536,384]{1,0:T(8,128)(2,1)S(1)}, u32[]{:S(2)}, u32[]{:S(2)}) collective-permute-start(bf16[1536,384]{1,0:T(8,128)(2,1)} %bitcast.21), channel_id=1, source_target_pairs={{0,1},{1,0},{2,3},{3,2},{4,5},{5,4},{6,7},{7,6},{8,9},{9,8},{10,11... | collective-permute-start | bytes 3538952 | tf_op jit(solution)/shard_map/ppermute | solution.py:675
  77.9 22.3 %collective-permute-start.3 = (bf16[20,3,14,384]{3,2,1,0:T(8,128)(2,1)}, bf16[20,3,14,384]{3,2,1,0:T(8,128)(2,1)S(1)}, u32[]{:S(2)}, u32[]{:S(2)}) collective-permute-start(bf16[20,3,14,384]{3,2,1,0:T(8,128)(2,1)} %get-tuple-element.140), channel_id=1, source_target_pairs={{0,16},{1,17},{2,18},{3,19},{4,20},{5,21},{6,22},{7,23},{8,24},{9,... | collective-permute-start | bytes 1935368 | tf_op jit(solution)/shard_map/ppermute | solution.py:675
  78.8 15.6 %copy-start.5 = (bf16[4,384,384]{2,1,0:T(8,128)(2,1)S(1)}, bf16[4,384,384]{2,1,0:T(8,128)(2,1)}, u32[]{:S(2)}) copy-start(bf16[4,384,384]{2,1,0:T(8,128)(2,1)} %get-tuple-element.152) | copy-start | bytes 3538948
  78.8 15.6 %copy-start.10 = (s32[4]{0:T(128)S(1)}, s32[4]{0:T(128)}, u32[]{:S(2)}) copy-start(s32[4]{0:T(128)} %pad_add_fusion.where.refs_0_) | copy-start | bytes 52
  96.7 16.9 %collective-permute-start.6 = (bf16[384,384]{1,0:T(8,128)(2,1)}, bf16[384,384]{1,0:T(8,128)(2,1)S(1)}, u32[]{:S(2)}, u32[]{:S(2)}) collective-permute-start(bf16[384,384]{1,0:T(8,128)(2,1)} %get-tuple-element.160), channel_id=1, source_target_pairs={{0,2},{1,3},{2,0},{3,1},{4,6},{5,7},{6,4},{7,5},{8,10},{9,11},{10,... | collective-permute-start | bytes 884744 | tf_op jit(solution)/shard_map/ppermute | solution.py:675
  98.2 15.4 %collective-permute-start.7 = (bf16[384,384]{1,0:T(8,128)(2,1)}, bf16[384,384]{1,0:T(8,128)(2,1)S(1)}, u32[]{:S(2)}, u32[]{:S(2)}) collective-permute-start(bf16[384,384]{1,0:T(8,128)(2,1)} %get-tuple-element.161), channel_id=1, source_target_pairs={{0,16},{1,17},{2,18},{3,19},{4,20},{5,21},{6,22},{7,23},{8,24},{9,... | collective-permute-start | bytes 884744 | tf_op jit(solution)/shard_map/ppermute | solution.py:675
  99.4 14.3 %collective-permute-start.8 = (bf16[384,384]{1,0:T(8,128)(2,1)S(1)}, bf16[384,384]{1,0:T(8,128)(2,1)S(1)}, u32[]{:S(2)}, u32[]{:S(2)}) collective-permute-start(bf16[384,384]{1,0:T(8,128)(2,1)S(1)} %get-tuple-element.162), channel_id=1, source_target_pairs={{0,18},{1,19},{2,16},{3,17},{4,22},{5,23},{6,20},{7,21},{8,26},{9,... | collective-permute-start | bytes 884744 | tf_op jit(solution)/shard_map/ppermute | solution.py:675
  113.5 6.2 %collective-permute-start.5 = (bf16[768,384]{1,0:T(8,128)(2,1)}, bf16[768,384]{1,0:T(8,128)(2,1)S(1)}, u32[]{:S(2)}, u32[]{:S(2)}) collective-permute-start(bf16[768,384]{1,0:T(8,128)(2,1)} %bitcast.22), channel_id=1, source_target_pairs={{0,1},{1,0},{2,3},{3,2},{4,5},{5,4},{6,7},{7,6},{8,9},{9,8},{10,11... | collective-permute-start | bytes 1769480 | tf_op jit(solution)/shard_map/ppermute | solution.py:675
  115.2 7.9 %collective-permute-start.10 = (bf16[96,384]{1,0:T(8,128)(2,1)S(1)}, bf16[96,384]{1,0:T(8,128)(2,1)S(1)}, u32[]{:S(2)}, u32[]{:S(2)}) collective-permute-start(bf16[96,384]{1,0:T(8,128)(2,1)S(1)} %get-tuple-element.170), channel_id=1, source_target_pairs={{0,4},{1,5},{2,6},{3,7},{4,0},{5,1},{6,2},{7,3},{8,12},{9,13},{10,... | collective-permute-start | bytes 221192 | tf_op jit(solution)/shard_map/ppermute | solution.py:675
  116.8 15.5 %collective-permute-start.11 = (bf16[96,384]{1,0:T(8,128)(2,1)S(1)}, bf16[96,384]{1,0:T(8,128)(2,1)S(1)}, u32[]{:S(2)}, u32[]{:S(2)}) collective-permute-start(bf16[96,384]{1,0:T(8,128)(2,1)S(1)} %get-tuple-element.171), channel_id=1, source_target_pairs={{0,8},{1,9},{2,10},{3,11},{4,12},{5,13},{6,14},{7,15},{8,0},{9,1},... | collective-permute-start | bytes 221192 | tf_op jit(solution)/shard_map/ppermute | solution.py:675
  119.5 12.9 %collective-permute-start.12 = (bf16[96,384]{1,0:T(8,128)(2,1)S(1)}, bf16[96,384]{1,0:T(8,128)(2,1)S(1)}, u32[]{:S(2)}, u32[]{:S(2)}) collective-permute-start(bf16[96,384]{1,0:T(8,128)(2,1)S(1)} %get-tuple-element.172), channel_id=1, source_target_pairs={{0,12},{1,13},{2,14},{3,15},{4,8},{5,9},{6,10},{7,11},{8,4},{9,5},... | collective-permute-start | bytes 221192 | tf_op jit(solution)/shard_map/ppermute | solution.py:675
  120.4 12.0 %collective-permute-start.13 = (bf16[192,384]{1,0:T(8,128)(2,1)S(1)}, bf16[192,384]{1,0:T(8,128)(2,1)S(1)}, u32[]{:S(2)}, u32[]{:S(2)}) collective-permute-start(bf16[192,384]{1,0:T(8,128)(2,1)S(1)} %get-tuple-element.174), channel_id=1, source_target_pairs={{0,2},{1,3},{2,0},{3,1},{4,6},{5,7},{6,4},{7,5},{8,10},{9,11},{10,... | collective-permute-start | bytes 442376 | tf_op jit(solution)/shard_map/ppermute | solution.py:675
  122.0 10.4 %collective-permute-start.14 = (bf16[192,384]{1,0:T(8,128)(2,1)S(1)}, bf16[192,384]{1,0:T(8,128)(2,1)S(1)}, u32[]{:S(2)}, u32[]{:S(2)}) collective-permute-start(bf16[192,384]{1,0:T(8,128)(2,1)S(1)} %get-tuple-element.175), channel_id=1, source_target_pairs={{0,16},{1,17},{2,18},{3,19},{4,20},{5,21},{6,22},{7,23},{8,24},{9,... | collective-permute-start | bytes 442376 | tf_op jit(solution)/shard_map/ppermute | solution.py:675
  123.1 9.3 %collective-permute-start.15 = (bf16[192,384]{1,0:T(8,128)(2,1)S(1)}, bf16[192,384]{1,0:T(8,128)(2,1)S(1)}, u32[]{:S(2)}, u32[]{:S(2)}) collective-permute-start(bf16[192,384]{1,0:T(8,128)(2,1)S(1)} %get-tuple-element.176), channel_id=1, source_target_pairs={{0,18},{1,19},{2,16},{3,17},{4,22},{5,23},{6,20},{7,21},{8,26},{9,... | collective-permute-start | bytes 442376 | tf_op jit(solution)/shard_map/ppermute | solution.py:675
  131.0 17.4 %copy-start.4 = (bf16[20,3,14,384]{3,2,1,0:T(8,128)(2,1)S(1)}, bf16[20,3,14,384]{3,2,1,0:T(8,128)(2,1)}, u32[]{:S(2)}) copy-start(bf16[20,3,14,384]{3,2,1,0:T(8,128)(2,1)} %copy-done.3) | copy-start | bytes 1935364
  133.5 5.5 %collective-permute-start.16 = (bf16[96,384]{1,0:T(8,128)(2,1)S(1)}, bf16[96,384]{1,0:T(8,128)(2,1)S(1)}, u32[]{:S(2)}, u32[]{:S(2)}) collective-permute-start(bf16[96,384]{1,0:T(8,128)(2,1)S(1)} %get-tuple-element.182), channel_id=1, source_target_pairs={{0,4},{1,5},{2,6},{3,7},{4,0},{5,1},{6,2},{7,3},{8,12},{9,13},{10,... | collective-permute-start | bytes 221192 | tf_op jit(solution)/shard_map/ppermute | solution.py:675
  134.2 7.6 %collective-permute-start.17 = (bf16[96,384]{1,0:T(8,128)(2,1)S(1)}, bf16[96,384]{1,0:T(8,128)(2,1)S(1)}, u32[]{:S(2)}, u32[]{:S(2)}) collective-permute-start(bf16[96,384]{1,0:T(8,128)(2,1)S(1)} %get-tuple-element.183), channel_id=1, source_target_pairs={{0,8},{1,9},{2,10},{3,11},{4,12},{5,13},{6,14},{7,15},{8,0},{9,1},... | collective-permute-start | bytes 221192 | tf_op jit(solution)/shard_map/ppermute | solution.py:675
  137.7 6.2 %collective-permute-start.18 = (bf16[96,384]{1,0:T(8,128)(2,1)S(1)}, bf16[96,384]{1,0:T(8,128)(2,1)S(1)}, u32[]{:S(2)}, u32[]{:S(2)}) collective-permute-start(bf16[96,384]{1,0:T(8,128)(2,1)S(1)} %get-tuple-element.184), channel_id=1, source_target_pairs={{0,12},{1,13},{2,14},{3,15},{4,8},{5,9},{6,10},{7,11},{8,4},{9,5},... | collective-permute-start | bytes 221192 | tf_op jit(solution)/shard_map/ppermute | solution.py:675
  137.9 18.6 %collective-permute-start.9 = (bf16[20,3,14,384]{3,2,1,0:T(8,128)(2,1)S(1)}, bf16[20,3,14,384]{3,2,1,0:T(8,128)(2,1)S(1)}, u32[]{:S(2)}, u32[]{:S(2)}) collective-permute-start(bf16[20,3,14,384]{3,2,1,0:T(8,128)(2,1)S(1)} %get-tuple-element.166), channel_id=1, source_target_pairs={{0,16},{1,17},{2,18},{3,19},{4,20},{5,21},{6,22},{7,23},{8,24},{9,... | collective-permute-start | bytes 1935368 | tf_op jit(solution)/shard_map/ppermute | solution.py:675
  144.0 6.4 %collective-permute-start.19 = (bf16[144,384]{1,0:T(8,128)(2,1)S(1)}, bf16[144,384]{1,0:T(8,128)(2,1)S(1)}, u32[]{:S(2)}, u32[]{:S(2)}) collective-permute-start(bf16[144,384]{1,0:T(8,128)(2,1)S(1)} %get-tuple-element.186.refs_1_), channel_id=1, source_target_pairs={{0,4},{1,5},{2,6},{3,7},{4,0},{5,1},{6,2},{7,3},{8,12},{9,13},{10,... | collective-permute-start | bytes 331784 | tf_op jit(solution)/shard_map/ppermute | solution.py:675
  144.0 9.2 %collective-permute-start.20 = (bf16[144,384]{1,0:T(8,128)(2,1)S(1)}, bf16[144,384]{1,0:T(8,128)(2,1)S(1)}, u32[]{:S(2)}, u32[]{:S(2)}) collective-permute-start(bf16[144,384]{1,0:T(8,128)(2,1)S(1)} %get-tuple-element.186.refs_1_), channel_id=1, source_target_pairs={{0,8},{1,9},{2,10},{3,11},{4,12},{5,13},{6,14},{7,15},{8,0},{9,1},... | collective-permute-start | bytes 331784 | tf_op jit(solution)/shard_map/ppermute | solution.py:675
  145.7 7.5 %collective-permute-start.21 = (bf16[144,384]{1,0:T(8,128)(2,1)S(1)}, bf16[144,384]{1,0:T(8,128)(2,1)S(1)}, u32[]{:S(2)}, u32[]{:S(2)}) collective-permute-start(bf16[144,384]{1,0:T(8,128)(2,1)S(1)} %get-tuple-element.186.refs_1_), channel_id=1, source_target_pairs={{0,12},{1,13},{2,14},{3,15},{4,8},{5,9},{6,10},{7,11},{8,4},{9,5},... | collective-permute-start | bytes 331784 | tf_op jit(solution)/shard_map/ppermute | solution.py:675
  148.4 1.5 collective-permute-start.22
  153.8 11.1 %collective-permute-start.23 = (bf16[624,384]{1,0:T(8,128)(2,1)S(1)}, bf16[624,384]{1,0:T(8,128)(2,1)S(1)}, u32[]{:S(2)}, u32[]{:S(2)}) collective-permute-start(bf16[624,384]{1,0:T(8,128)(2,1)S(1)} %lay.1.own.first), channel_id=1, source_target_pairs={{0,16},{1,17},{2,18},{3,19},{4,20},{5,21},{6,22},{7,23},{8,24},{9,... | collective-permute-start | bytes 1437704 | tf_op jit(solution)/shard_map/ppermute | solution.py:675
  155.0 9.9 %collective-permute-start.24 = (bf16[624,384]{1,0:T(8,128)(2,1)S(1)}, bf16[624,384]{1,0:T(8,128)(2,1)S(1)}, u32[]{:S(2)}, u32[]{:S(2)}) collective-permute-start(bf16[624,384]{1,0:T(8,128)(2,1)S(1)} %lay.1.own.first), channel_id=1, source_target_pairs={{0,2},{1,3},{2,0},{3,1},{4,6},{5,7},{6,4},{7,5},{8,10},{9,11},{10,... | collective-permute-start | bytes 1437704 | tf_op jit(solution)/shard_map/ppermute | solution.py:675
  164.9 7.4 %collective-permute-start.26 = (bf16[320,384]{1,0:T(8,128)(2,1)S(1)}, bf16[320,384]{1,0:T(8,128)(2,1)S(1)}, u32[]{:S(2)}, u32[]{:S(2)}) collective-permute-start(bf16[320,384]{1,0:T(8,128)(2,1)S(1)} %get-tuple-element.191), channel_id=1, source_target_pairs={{0,16},{1,17},{2,18},{3,19},{4,20},{5,21},{6,22},{7,23},{8,24},{9,... | collective-permute-start | bytes 737288 | tf_op jit(solution)/shard_map/ppermute | solution.py:675
  166.2 6.1 %collective-permute-start.25 = (bf16[304,384]{1,0:T(8,128)(2,1)S(1)}, bf16[304,384]{1,0:T(8,128)(2,1)S(1)}, u32[]{:S(2)}, u32[]{:S(2)}) collective-permute-start(bf16[304,384]{1,0:T(8,128)(2,1)S(1)} %get-tuple-element.190), channel_id=1, source_target_pairs={{0,2},{1,3},{2,0},{3,1},{4,6},{5,7},{6,4},{7,5},{8,10},{9,11},{10,... | collective-permute-start | bytes 700424 | tf_op jit(solution)/shard_map/ppermute | solution.py:675
  172.5 5.9 %collective-permute-start.28 = (bf16[3,576,384]{2,1,0:T(8,128)(2,1)S(1)}, bf16[3,576,384]{2,1,0:T(8,128)(2,1)S(1)}, u32[]{:S(2)}, u32[]{:S(2)}) collective-permute-start(bf16[3,576,384]{2,1,0:T(8,128)(2,1)S(1)} %get-tuple-element.195.rest), channel_id=1, source_target_pairs={{0,1},{1,0},{2,3},{3,2},{4,5},{5,4},{6,7},{7,6},{8,9},{9,8},{10,11... | collective-permute-start | bytes 3981320 | tf_op jit(solution)/shard_map/ppermute | solution.py:675
  172.6 5.8 %collective-permute-start.27 = (bf16[624,384]{1,0:T(8,128)(2,1)S(1)}, bf16[624,384]{1,0:T(8,128)(2,1)S(1)}, u32[]{:S(2)}, u32[]{:S(2)}) collective-permute-start(bf16[624,384]{1,0:T(8,128)(2,1)S(1)} %lay.1.own.first), channel_id=1, source_target_pairs={{0,1},{1,0},{2,3},{3,2},{4,5},{5,4},{6,7},{7,6},{8,9},{9,8},{10,11... | collective-permute-start | bytes 1437704 | tf_op jit(solution)/shard_map/ppermute | solution.py:675
  (32 other events, 235.2 us)

commit v2 on v1

--- a/solution.py
+++ b/solution.py
@@ -208,9 +208,10 @@
         spread = dot(table, pick_offsets(place), HIGH)
         strip[:, 2 * place, 0:WIDE] = jnp.where(even, spread, MASKED)
         strip[:, 2 * place + 1, 0:WIDE] = jnp.where(even, MASKED, spread)
+    out[...] = jnp.zeros_like(out)
     for row in range(GROUP):
         start = (GROUP - 1 - row) * PAD_COLS
-        out[:, row * PAD_COLS : (row + 1) * PAD_COLS, :] = strip[:, :, start : start + TOKENS]
+        out[:, row * PAD_COLS : (row + 1) * PAD_COLS, 0:TOKENS] = strip[:, :, start : start + TOKENS]
 
 
 def pair_bias(pos, through):
@@ -218,7 +219,7 @@
         bias_kernel,
         "pair_bias",
         pos,
-        [shaped((HEADS, TOKENS, TOKENS), F32)],
+        [shaped((HEADS, TOKENS, LANES), F32)],
         [pltpu.VMEM((HEADS, PAD_COLS, 2 * LANES), F32)],
         through=through,
         vmem=60,
@@ -240,7 +241,7 @@
     strip = jnp.zeros((HEADS, PAD_COLS, WIDE), F32)
     for row in range(GROUP):
         start = (GROUP - 1 - row) * PAD_COLS
-        piece = grad_pair[:, row * PAD_COLS : (row + 1) * PAD_COLS, :]
+        piece = grad_pair[:, row * PAD_COLS : (row + 1) * PAD_COLS, 0:TOKENS]
         strip = strip + jnp.pad(piece, ((0, 0), (0, 0), (start, WIDE - start - TOKENS)))
     table = jnp.zeros((HEADS, OFFSETS), F32)
     for place in range(GROUP):
@@ -261,7 +262,7 @@
     return small_launch(
         gather_small_kernel,
         "gather_small",
-        (feed_small, feed_b1, att_small, norm_small, grad_pair.reshape(HEADS, TOKENS, TOKENS)),
+        (feed_small, feed_b1, att_small, norm_small, grad_pair.reshape(HEADS, TOKENS, LANES)),
         [shaped((2 * SMALL, width), BF16)],
         [pltpu.VMEM((SMALL, width), F32)],
     )[0]
@@ -321,6 +322,23 @@
     return jnp.concatenate([block] * PER_BLOCK, axis=0) * mask
 
 
+def two_images(two):
+    return [slice(image * TOKENS, (image + 1) * TOKENS) for image in (2 * two, 2 * two + 1)]
+
+
+def on_diagonal(blocks):
+    rest = jnp.zeros((LANES - TOKENS, LANES), BF16)
+    zero = jnp.zeros((LANES, LANES), BF16)
+    first, second = [jnp.concatenate([block, rest], axis=0) for block in blocks]
+    return jnp.concatenate(
+        [jnp.concatenate([first, zero], axis=1), jnp.concatenate([zero, second], axis=1)], axis=0
+    )
+
+
+def side_by_side(blocks, mask):
+    return jnp.concatenate([stack_heads(block, mask) for block in blocks], axis=1)
+
+
 def place_rows(band, kept_ref, received_ref, padded):
     upper = band * SENT
     lower = (1 - band) * KEPT
@@ -358,21 +376,23 @@
     qkv_out[:, width : 2 * width] = piece[:, width : 2 * width].astype(BF16)
     qkv_out[:, 2 * width :] = (piece[:, 2 * width :] + bias[1:2, :]).astype(BF16)
     masks = mask[...]
-    for image in range(count):
-        rows = slice(image * TOKENS, (image + 1) * TOKENS)
+    for two in range(count // 2):
+        both = two_images(two)
         for block in range(HEADS // PER_BLOCK):
             at = block * LANES
-            query = qkv_out[rows, at : at + LANES]
-            keys = stack_heads(qkv_out[rows, width + at : width + at + LANES], masks)
-            vals = stack_heads(qkv_out[rows, 2 * width + at : 2 * width + at + LANES], masks)
             here = slice(block * STACK, (block + 1) * STACK)
-            scores = dot_nt(keys, query) * SCALE + pair[here, :]
-            scores = scores.reshape(PER_BLOCK, TOKENS, TOKENS)
+            query = on_diagonal([qkv_out[rows, at : at + LANES] for rows in both])
+            keys = side_by_side([qkv_out[rows, width + at : width + at + LANES] for rows in both], masks)
+            scores = dot_nt(keys, query) * SCALE + jnp.concatenate([pair[here, :]] * 2, axis=1)
+            scores = scores.reshape(PER_BLOCK, TOKENS, 2 * LANES)
             probs = jnp.exp(scores - jnp.max(scores, axis=1, keepdims=True))
             probs = probs * (1.0 / jnp.sum(probs, axis=1, keepdims=True))
-            probs = probs.astype(BF16).reshape(STACK, TOKENS)
-            probs_out[image, here, :] = probs
-            att_out[rows, at : at + LANES] = dot_tn(probs, vals).astype(BF16)
+            probs = probs.astype(BF16).reshape(STACK, 2 * LANES)
+            probs_out[two, here, :] = probs
+            for half, rows in enumerate(both):
+                vals = stack_heads(qkv_out[rows, 2 * width + at : 2 * width + at + LANES], masks)
+                attended = dot_tn(probs[:, half * LANES : (half + 1) * LANES], vals)
+                att_out[rows, at : at + LANES] = attended[0:TOKENS, :].astype(BF16)
 
 
 def attend(where, images, received, first, per_step, gain, shift, weight, bias, pair, mask, so_far, through):
@@ -381,7 +401,7 @@
     begin = first // per_step
     rows = per_step * TOKENS
     row_spec = lambda w: pl.BlockSpec((rows, w), lambda i: (i + begin, 0))
-    fixed = (gain, shift, weight, bias, pair.reshape(HEADS * TOKENS, TOKENS), mask)
+    fixed = (gain, shift, weight, bias, pair.reshape(HEADS * TOKENS, LANES), mask)
     return launch(
         partial(attend_kernel, per_step),
         "attend",
@@ -397,14 +417,14 @@
             shaped((total * TOKENS, width), BF16),
             shaped((total * TOKENS, width), BF16),
             shaped((total * TOKENS, 3 * width), BF16),
-            shaped((total, HEADS * TOKENS, TOKENS), BF16),
+            shaped((total // 2, HEADS * TOKENS, 2 * LANES), BF16),
             shaped((total * TOKENS, width), BF16),
         ],
         [
             row_spec(width),
             row_spec(width),
             row_spec(3 * width),
-            pl.BlockSpec((per_step, HEADS * TOKENS, TOKENS), lambda i: (i + begin, 0, 0)),
+            pl.BlockSpec((per_step // 2, HEADS * TOKENS, 2 * LANES), lambda i: (i + begin, 0, 0)),
             row_spec(width),
         ],
         so_far=so_far,
@@ -438,16 +458,27 @@
     normed_turned = normed.T
     result = middle + b2[...][None, :]
     grad_normed = jnp.zeros((count * TOKENS, width), F32)
-    for start in range(0, hidden, FEED_PART):
+    starts = range(0, hidden, FEED_PART)
+
+    def ahead(start):
         cols = slice(start, start + FEED_PART)
-        active, slope = gelu_both(dot(normed, w1[:, cols]) + b1[cols][None, :])
+        return dot(normed, w1[:, cols]), dot_nt(up, w2[cols, :])
+
+    coming = ahead(0)
+    for start in starts:
+        cols = slice(start, start + FEED_PART)
+        pre_act, grad_act = coming
+        if start + FEED_PART < hidden:
+            coming = ahead(start + FEED_PART)
+        active, slope = gelu_both(pre_act + b1[cols][None, :])
         active = active.astype(BF16)
+        grad_pre = grad_act * slope
+        o_b1[:, cols] += column_sum(grad_pre)
+        grad_pre = grad_pre.astype(BF16)
         result = result + dot(active, w2[cols, :])
-        grad_pre = (dot_nt(up, w2[cols, :]) * slope).astype(BF16)
         grad_normed = grad_normed + dot_nt(grad_pre, w1[:, cols])
         pair[0, :, cols] += dot(normed_turned, grad_pre)
         pair[1, :, cols] += dot(up_turned, active)
-        o_b1[:, cols] += column_sum(grad_pre.astype(F32))
     placed[...] = result.astype(BF16).reshape(placed.shape)
     return_rows(where[0], placed, out_kept, out_send)
     grad_normed = grad_normed.astype(BF16).astype(F32)
@@ -530,28 +561,32 @@
             ref[...] = jnp.zeros_like(ref) if first_call else carried[index][...]
 
     masks = mask[...]
-    for image in range(count):
-        rows = slice(image * TOKENS, (image + 1) * TOKENS)
+    for two in range(count // 2):
+        both = two_images(two)
         for block in range(HEADS // PER_BLOCK):
             at = block * LANES
             here = slice(block * STACK, (block + 1) * STACK)
-            query = qkv[rows, at : at + LANES]
-            keys = stack_heads(qkv[rows, width + at : width + at + LANES], masks)
-            vals = stack_heads(qkv[rows, 2 * width + at : 2 * width + at + LANES], masks)
-            grad = grad_att[rows, at : at + LANES]
-            probs = probs_ref[image, here, :]
-            exact = probs.astype(F32).reshape(PER_BLOCK, TOKENS, TOKENS)
-            grad_probs = dot_nt(vals, grad).reshape(PER_BLOCK, TOKENS, TOKENS)
+            query = on_diagonal([qkv[rows, at : at + LANES] for rows in both])
+            grad = on_diagonal([grad_att[rows, at : at + LANES] for rows in both])
+            vals = side_by_side([qkv[rows, 2 * width + at : 2 * width + at + LANES] for rows in both], masks)
+            probs = probs_ref[two, here, :]
+            exact = probs.astype(F32).reshape(PER_BLOCK, TOKENS, 2 * LANES)
+            grad_probs = dot_nt(vals, grad).reshape(PER_BLOCK, TOKENS, 2 * LANES)
             inner = jnp.sum(grad_probs * exact, axis=1, keepdims=True)
-            grad_scores = (exact * (grad_probs - inner)).reshape(STACK, TOKENS).astype(BF16)
-            o_pair[here, :] += grad_scores.astype(F32)
-            grads[rows, at : at + LANES] = (dot_tn(grad_scores, keys) * SCALE).astype(BF16)
-            grads[rows, width + at : width + at + LANES] = (
-                pick_heads(dot(grad_scores, query)) * SCALE
-            ).astype(BF16)
-            grads[rows, 2 * width + at : 2 * width + at + LANES] = pick_heads(
-                dot(probs, grad)
-            ).astype(BF16)
+            exact_scores = (exact * (grad_probs - inner)).reshape(STACK, 2 * LANES)
+            o_pair[here, :] += exact_scores[:, :LANES] + exact_scores[:, LANES:]
+            grad_scores = exact_scores.astype(BF16)
+            grad_keys = dot(grad_scores, query)
+            grad_vals = dot(probs, grad)
+            for half, rows in enumerate(both):
+                lanes = slice(half * LANES, (half + 1) * LANES)
+                keys = stack_heads(qkv[rows, width + at : width + at + LANES], masks)
+                grad_query = dot_tn(grad_scores[:, lanes], keys)[0:TOKENS, :]
+                grads[rows, at : at + LANES] = (grad_query * SCALE).astype(BF16)
+                grads[rows, width + at : width + at + LANES] = (
+                    pick_heads(grad_keys[:, lanes]) * SCALE
+                ).astype(BF16)
+                grads[rows, 2 * width + at : 2 * width + at + LANES] = pick_heads(grad_vals[:, lanes]).astype(BF16)
     all_grads = grads[...]
     a_w[...] += dot(normed[...].T, all_grads)
     o_small[0:1, :] += column_sum(all_grads[:, :width].astype(F32))
@@ -587,7 +622,7 @@
         second_shape = shaped((8, LANES), F32)
     accumulated = [
         shaped((8, width), F32),
-        shaped((HEADS * TOKENS, TOKENS), F32),
+        shaped((HEADS * TOKENS, LANES), F32),
         first_shape,
         second_shape,
     ]
@@ -600,7 +635,7 @@
             pl.BlockSpec(memory_space=pltpu.SMEM),
             row_spec(width),
             row_spec(3 * width),
-            pl.BlockSpec((per_step, HEADS * TOKENS, TOKENS), lambda i: (i + begin, 0, 0)),
+            pl.BlockSpec((per_step // 2, HEADS * TOKENS, 2 * LANES), lambda i: (i + begin, 0, 0)),
             row_spec(width),
         ]
         + [whole(a.shape) for a in (*fixed, *extra)],
@@ -819,40 +854,43 @@
     width = o_proj.shape[0]
     late = width // 2 // ALONG
     low, high = slice(0, width // 2), slice(width // 2, width)
-    for d in range(PLANE):
-        quarter = first if d == 0 else rest.at[d - 1]
-        for share in range(ALONG):
-            start = share * (early + late)
-            feed_buf[d, share * early : (share + 1) * early, :] = quarter[start : start + early, :].astype(F32)
-            att_buf[me ^ d, share * late : (share + 1) * late, :] = quarter[
-                start + early : start + early + late, :
-            ].astype(F32)
-
-    def send(copies):
-        for index, (source, target) in enumerate(copies):
-            pltpu.make_async_copy(source, target, sems.at[index]).start()
-        for index, (source, target) in enumerate(copies):
-            pltpu.make_async_copy(source, target, sems.at[index]).wait()
+    def quarter_of(d):
+        return first if d == 0 else rest.at[d - 1]
 
     def place(d):
         return pl.ds(pl.multiple_of((me ^ d) * width, width), width)
 
-    def halves(target, cols, at):
-        return [(att_buf.at[at], target.at[low, cols]), (att_buf.at[at + 1], target.at[high, cols])]
+    for d in range(PLANE):
+        for share in range(ALONG):
+            start = share * (early + late) + early
+            att_buf[me ^ d, share * late : (share + 1) * late, :] = quarter_of(d)[start : start + late, :].astype(F32)
+
+    def run(att_targets, feed_target, turned):
+        copies = []
+        for index, (target, rows, cols) in enumerate(att_targets):
+            copies.append(pltpu.make_async_copy(att_buf.at[index], target.at[rows, cols], sems.at[len(copies)]))
+            copies[-1].start()
+        for d in range(PLANE):
+            shares = [quarter_of(d)[i * (early + late) : i * (early + late) + early, :] for i in range(ALONG)]
+            block = jnp.concatenate(shares, axis=0).astype(F32)
+            feed_buf[d] = block.T if turned else block
+            copies.append(pltpu.make_async_copy(feed_buf.at[d], feed_target(d), sems.at[len(copies)]))
+            copies[-1].start()
+        for copy in copies:
+            copy.wait()
+
+    def halves(target, cols):
+        return [(target, low, cols), (target, high, cols)]
 
     @pl.when(side == 0)
     def _():
-        copies = [(feed_buf.at[d], o_w1.at[:, place(d)]) for d in range(PLANE)]
-        copies += halves(o_qkv, slice(0, width), 0) + halves(o_qkv, slice(width, 2 * width), 2)
-        send(copies)
+        targets = halves(o_qkv, slice(0, width)) + halves(o_qkv, slice(width, 2 * width))
+        run(targets, lambda d: o_w1.at[:, place(d)], False)
 
     @pl.when(side == 1)
     def _():
-        for d in range(PLANE):
-            feed_buf[d] = feed_buf[d].T
-        copies = [(feed_buf.at[d], o_w2.at[place(d), :]) for d in range(PLANE)]
-        copies += halves(o_qkv, slice(2 * width, 3 * width), 0) + halves(o_proj, slice(0, width), 2)
-        send(copies)
+        targets = halves(o_qkv, slice(2 * width, 3 * width)) + halves(o_proj, slice(0, width))
+        run(targets, lambda d: o_w2.at[place(d), :], True)
 
 
 def unpack(flip, early, where, half, shapes, so_far):

time: 182 us -> 180 us (0.989)
  Pallas kernels: 117 us -> 114 us
    pallas_call x24, Pallas kernels: 117 us -> 114 us  [launch(): pl.pallas_call(kernel, grid=grid, in_specs=list(in_specs) + [pl.BlockSpec...]
  transfers between devices with their start and end apart: 29 -> 29, of which waited for: 8 -> 9; matrix products, arithmetic and copies ran while one was open for 0% -> 0% of each run, Pallas kernels for 41% -> 42%
where the time goes in v2:
time: 180 us; the launch traced here: 179 us
  Pallas kernels  114 us (63%)
  starting transfers between devices  31.9 us (18%)
  waiting for transfers between devices  26.8 us (15%)
  local copies, waits for them, and re-layouts  4.91 us (3%)
    pallas_call x24, Pallas kernels, launch(): pl.pallas_call(kernel, grid=grid, in_specs=list(in_specs) + [pl.BlockSpec...  114 us
    ppermute x29, starting transfers between devices, swap(): return lax.ppermute(value, ('band', 'batch'), pairs)  31.9 us
    ppermute x29, waiting for transfers between devices, swap(): return lax.ppermute(value, ('band', 'batch'), pairs)  26.8 us
    unnamed x70, local copies, waits for them, and re-layouts  4.91 us
  transfers between devices with their start and end apart: 29, of which 9 were waited for; matrix products, arithmetic and copies ran while one was open for 0% of the time, Pallas kernels for 42%

profile of v2, /device:TPU:0, one launch (start us, length us, event | category | flops | bytes accessed | tf_op | source)
XLA Modules:
  0.0 179.2 jit_solution(14607969025811217306)
XLA Ops:
  0.7 1.7 pack_rows.2
  2.4 3.0 %collective-permute-start = (bf16[8,3,14,384]{3,2,1,0:T(8,128)(2,1)}, bf16[8,3,14,384]{3,2,1,0:T(8,128)(2,1)S(1)}, u32[]{:S(2)}, u32[]{:S(2)}) collective-permute-start(bf16[8,3,14,384]{3,2,1,0:T(8,128)(2,1)} %get-tuple-element.125), channel_id=1, source_target_pairs={{0,16},{1,17},{2,18},{3,19},{4,20},{5,21},{6,22},{7,23},{8,24},{9,... | collective-permute-start | bytes 774152 | tf_op jit(solution)/shard_map/ppermute | solution.py:710
  5.4 2.4 %pack_rows.3 = (bf16[12,3,14,384]{3,2,1,0:T(8,128)(2,1)}, bf16[20,3,14,384]{3,2,1,0:T(8,128)(2,1)}, f32[8,128]{1,0:T(8,128)}) custom-call(bf16[20,7,14,384]{3,2,1,0:T(8,128)(2,1)} %refs_1_.6, bf16[20,7,14,384]{3,2,1,0:T(8,128)(2,1)} %cot.1, f32[8,128]{1,0:T(8,128)} %get-tuple-element.126.refs_2_), custom_call_target="tpu_custom_call" | custom-call | bytes 4046848 | tf_op jit(solution)/shard_map/pack_rows/pallas_call | solution.py:87
  7.8 4.3 %pair_bias.1 = (f32[12,112,128]{2,1,0:T(8,128)}, bf16[12,3,14,384]{3,2,1,0:T(8,128)(2,1)}, bf16[20,3,14,384]{3,2,1,0:T(8,128)(2,1)}) custom-call(f32[2,96]{1,0:T(2,128)} %refs_0_.7, f32[96]{0:T(128)} %refs_1_.7, f32[96]{0:T(128)} %refs_2_.3, f32[96]{0:T(128)} %refs_3_.5, f32[96,96]{1,0:T(8,128)} %refs_4_.7, ...), custom_call_target="tpu_custom_call", output_to_operand_aliasing={{1}: (13, {}), {2}: (14, {})} | custom-call | bytes 770688 | tf_op jit(solution)/shard_map/pair_bias/pallas_call | solution.py:87
  13.5 9.0 %attend.2 = (bf16[2240,384]{1,0:T(8,128)(2,1)}, bf16[2240,384]{1,0:T(8,128)(2,1)}, bf16[2240,1152]{1,0:T(8,128)(2,1)}, bf16[10,1344,256]{2,1,0:T(8,128)(2,1)}, bf16[2240,384]{1,0:T(8,128)(2,1)}) custom-call(s32[4]{0:T(128)} %pad_add_fusion.where.refs_0_, bf16[20,7,14,384]{3,2,1,0:T(8,128)(2,1)} %refs_1_.6, bf16[8,3,14,384]{3,2,1,0:T(8,128)(2,1)} %copy-done.32, ...), custom_call_target="tpu_custom_call" | custom-call | flops 1585446912 | bytes 20660240 | tf_op jit(solution)/shard_map/attend/pallas_call | solution.py:87
  22.4 1.5 collective-permute-done.1.refs_1_.refs_2_
  25.8 11.8 %attend.3 = (bf16[2240,384]{1,0:T(8,128)(2,1)}, bf16[2240,384]{1,0:T(8,128)(2,1)}, bf16[2240,1152]{1,0:T(8,128)(2,1)}, bf16[10,1344,256]{2,1,0:T(8,128)(2,1)}, bf16[2240,384]{1,0:T(8,128)(2,1)}) custom-call(s32[4]{0:T(128)} %pad_add_fusion.where.refs_0_, ...), custom_call_target="tpu_custom_call", output_to_operand_aliasing={{0}: (9, {}), {1}: (10, {}), {2}: (11, {}), {3}: (12, {}), ... | custom-call | flops 2378170368 | bytes 20789264 | tf_op jit(solution)/shard_map/attend/pallas_call | solution.py:87
  37.6 5.0 %collective-permute-done.2.received = bf16[20,3,14,384]{3,2,1,0:T(8,128)(2,1)S(1)} collective-permute-done((bf16[20,3,14,384]{3,2,1,0:T(8,128)(2,1)}, bf16[20,3,14,384]{3,2,1,0:T(8,128)(2,1)S(1)}, u32[]{:S(2)}, u32[]{:S(2)}) %collective-permute-start.2) | collective-permute-done | bytes 645152 | tf_op jit(solution)/shard_map/ppermute | solution.py:710
  43.4 33.0 %feed.1 = (bf16[20,7,14,384]{3,2,1,0:T(8,128)(2,1)}, f32[2240,384]{1,0:T(8,128)}, bf16[2240,384]{1,0:T(8,128)(2,1)}, bf16[20,3,14,384]{3,2,1,0:T(8,128)(2,1)}, f...) custom-call(s32[4]{0:T(128)} %pad_add_fusion.where.refs_0_, ...), custom_call_target="tpu_custom_call" | custom-call | flops 17836277760 | bytes 18536464 | tf_op jit(solution)/shard_map/feed/pallas_call | solution.py:87
  77.8 15.0 %attend_back.2 = (bf16[2240,1152]{1,0:T(8,128)(2,1)}, f32[8,384]{1,0:T(8,128)}, f32[1344,128]{1,0:T(8,128)}, f32[384,1152]{1,0:T(8,128)}, f32[8,128]{1,0:T(8,128)}) custom-call(s32[4]{0:T(128)} %pad_add_fusion.where.refs_0_, bf16[2240,384]{1,0:T(8,128)(2,1)} %get-tuple-element.143.normed.refs_1_, bf16[2240,1152]{1,0:T(8,128)(2,1)} %get-tuple-element.144.qkv.refs_2_, ...), custom_call_target="tpu_custom_call" | custom-call | flops 3567255552 | bytes 23822352 | tf_op jit(solution)/shard_map/attend_back/pallas_call | solution.py:87
  93.5 1.5 split_share.3
  95.0 1.5 collective-permute-start.6
  99.3 12.0 %attend_back.3 = (bf16[2240,1152]{1,0:T(8,128)(2,1)}, f32[8,384]{1,0:T(8,128)}, f32[1344,128]{1,0:T(8,128)}, bf16[2,384,384]{2,1,0:T(8,128)(2,1)}, bf16[2,384,384]{2,1,0:T(8,128)(2,1)}) custom-call(s32[4]{0:T(128)} %pad_add_fusion.where.refs_0_, bf16[2240,384]{1,0:T(8,128)(2,1)} %get-tuple-element.143.normed.refs_1_, ...), custom_call_target="tpu_custom_call", output_to_operand_aliasing={{0}: (10, {})} | custom-call | flops 2378170368 | bytes 25698320 | tf_op jit(solution)/shard_map/attend_back/pallas_call | solution.py:87
  113.3 1.7 collective-permute-start.10
  115.0 2.6 %collective-permute-start.11 = (bf16[96,384]{1,0:T(8,128)(2,1)S(1)}, bf16[96,384]{1,0:T(8,128)(2,1)S(1)}, u32[]{:S(2)}, u32[]{:S(2)}) collective-permute-start(bf16[96,384]{1,0:T(8,128)(2,1)S(1)} %get-tuple-element.171), channel_id=1, source_target_pairs={{0,8},{1,9},{2,10},{3,11},{4,12},{5,13},{6,14},{7,15},{8,0},{9,1},... | collective-permute-start | bytes 221192 | tf_op jit(solution)/shard_map/ppermute | solution.py:710
  118.5 1.6 collective-permute-start.13
  122.1 7.0 %image_grads.1 = (f32[20,7,14,384]{3,2,1,0:T(8,128)}, bf16[20,3,14,384]{3,2,1,0:T(8,128)(2,1)S(1)}, f32[8,384]{1,0:T(8,128)S(1)}) custom-call(s32[4]{0:T(128)S(1)} %copy-done.11, bf16[2240,1152]{1,0:T(8,128)(2,1)S(1)} %bitcast.13, bf16[2240,384]{1,0:T(8,128)(2,1)S(1)} %copy-done, f32[2240,384]{1,0:T(8,128)S(1)} %copy-done.2, f32[384]{0:T(512)S(1)} %copy-done.17, ...), custom_call_target="tpu_custom_call" | custom-call | flops 1981808640 | bytes 14876176 | tf_op jit(solution)/shard_map/image_grads/pallas_call | solution.py:87
  129.2 1.2 gather_small.1.refs_5_
  132.3 3.5 %collective-permute-start.17 = (bf16[96,384]{1,0:T(8,128)(2,1)S(1)}, bf16[96,384]{1,0:T(8,128)(2,1)S(1)}, u32[]{:S(2)}, u32[]{:S(2)}) collective-permute-start(bf16[96,384]{1,0:T(8,128)(2,1)S(1)} %get-tuple-element.183), channel_id=1, source_target_pairs={{0,8},{1,9},{2,10},{3,11},{4,12},{5,13},{6,14},{7,15},{8,0},{9,1},... | collective-permute-start | bytes 221192 | tf_op jit(solution)/shard_map/ppermute | solution.py:710
  136.9 2.8 %collective-permute-done.17.refs_6_ = bf16[96,384]{1,0:T(8,128)(2,1)S(1)} collective-permute-done((bf16[96,384]{1,0:T(8,128)(2,1)S(1)}, bf16[96,384]{1,0:T(8,128)(2,1)S(1)}, u32[]{:S(2)}, u32[]{:S(2)}) %collective-permute-start.17) | collective-permute-done | bytes 73760 | tf_op jit(solution)/shard_map/ppermute | solution.py:710
  139.7 2.6 %collective-permute-done.18.refs_7_ = bf16[96,384]{1,0:T(8,128)(2,1)S(1)} collective-permute-done((bf16[96,384]{1,0:T(8,128)(2,1)S(1)}, bf16[96,384]{1,0:T(8,128)(2,1)S(1)}, u32[]{:S(2)}, u32[]{:S(2)}) %collective-permute-start.18) | collective-permute-done | bytes 73760 | tf_op jit(solution)/shard_map/ppermute | solution.py:710
  143.6 3.3 %collective-permute-start.21 = (bf16[144,384]{1,0:T(8,128)(2,1)S(1)}, bf16[144,384]{1,0:T(8,128)(2,1)S(1)}, u32[]{:S(2)}, u32[]{:S(2)}) collective-permute-start(bf16[144,384]{1,0:T(8,128)(2,1)S(1)} %get-tuple-element.186.refs_1_), channel_id=1, source_target_pairs={{0,12},{1,13},{2,14},{3,15},{4,8},{5,9},{6,10},{7,11},{8,4},{9,5},... | collective-permute-start | bytes 331784 | tf_op jit(solution)/shard_map/ppermute | solution.py:710
  146.9 1.5 merge_rows.2
  148.4 2.7 %collective-permute-done.20.refs_3_ = bf16[144,384]{1,0:T(8,128)(2,1)S(1)} collective-permute-done((bf16[144,384]{1,0:T(8,128)(2,1)S(1)}, bf16[144,384]{1,0:T(8,128)(2,1)S(1)}, u32[]{:S(2)}, u32[]{:S(2)}) %collective-permute-start.20) | collective-permute-done | bytes 110624 | tf_op jit(solution)/shard_map/ppermute | solution.py:710
  152.7 1.5 collective-permute-start.24
  154.2 1.7 merge_rows.3
  155.9 6.6 %collective-permute-done.23.refs_0_.across = bf16[624,384]{1,0:T(8,128)(2,1)S(1)} collective-permute-done((bf16[624,384]{1,0:T(8,128)(2,1)S(1)}, bf16[624,384]{1,0:T(8,128)(2,1)S(1)}, u32[]{:S(2)}, u32[]{:S(2)}) %collective-permute-start.23) | collective-permute-done | bytes 479264 | tf_op jit(solution)/shard_map/ppermute | solution.py:710
  164.4 1.6 collective-permute-start.25
  166.0 4.6 %collective-permute-done.25.low = bf16[304,384]{1,0:T(8,128)(2,1)S(1)} collective-permute-done((bf16[304,384]{1,0:T(8,128)(2,1)S(1)}, bf16[304,384]{1,0:T(8,128)(2,1)S(1)}, u32[]{:S(2)}, u32[]{:S(2)}) %collective-permute-start.25) | collective-permute-done | bytes 233504 | tf_op jit(solution)/shard_map/ppermute | solution.py:710
  171.3 2.5 %unpack.2 = (f32[384,1536]{1,0:T(8,128)}, f32[1536,384]{1,0:T(8,128)}, f32[384,1152]{1,0:T(8,128)}, f32[384,384]{1,0:T(8,128)}) custom-call(s32[4]{0:T(128)S(1)} %copy-done.11, bf16[624,384]{1,0:T(8,128)(2,1)S(1)} %lay.1.own.first, bf16[3,576,384]{2,1,0:T(8,128)(2,1)S(1)} %get-tuple-element.195.rest), custom_call_target="tpu_custom_call" | custom-call | bytes 8884240 | tf_op jit(solution)/shard_map/unpack/pallas_call | solution.py:87
  173.9 2.6 %finish_small.1 = (f32[384]{0:T(512)}, f32[384]{0:T(512)}, f32[2,384]{1,0:T(2,128)}, f32[384]{0:T(512)}, f32[384]{0:T(512)}, /*index=5*/f32[384]{0:T(512)}, f32[...) custom-call(f32[2,96]{1,0:T(2,128)S(1)} %copy-done.20, ...), custom_call_target="tpu_custom_call" | custom-call | bytes 220416 | tf_op jit(solution)/shard_map/finish_small/pallas_call | solution.py:87
  176.5 2.5 %unpack.3 = (f32[384,1536]{1,0:T(8,128)}, f32[1536,384]{1,0:T(8,128)}, f32[384,1152]{1,0:T(8,128)}, f32[384,384]{1,0:T(8,128)}) custom-call(s32[4]{0:T(128)S(1)} %copy-done.11, bf16[624,384]{1,0:T(8,128)(2,1)S(1)} %collective-permute-done.27.refs_1_, ...), custom_call_target="tpu_custom_call", output_to_operand_aliasing={{0}: (3, {}), {1}: (4, {}), {2}: (5, {}), {3}: (6, {})} | custom-call | bytes 8884240 | tf_op jit(solution)/shard_map/unpack/pallas_call | solution.py:87
  (122 shorter events, 22.0 us)
Async XLA Ops:
  2.4 10.3 %collective-permute-start = (bf16[8,3,14,384]{3,2,1,0:T(8,128)(2,1)}, bf16[8,3,14,384]{3,2,1,0:T(8,128)(2,1)S(1)}, u32[]{:S(2)}, u32[]{:S(2)}) collective-permute-start(bf16[8,3,14,384]{3,2,1,0:T(8,128)(2,1)} %get-tuple-element.125), channel_id=1, source_target_pairs={{0,16},{1,17},{2,18},{3,19},{4,20},{5,21},{6,22},{7,23},{8,24},{9,... | collective-permute-start | bytes 774152 | tf_op jit(solution)/shard_map/ppermute | solution.py:710
  12.1 11.8 %collective-permute-start.1 = (bf16[12,3,14,384]{3,2,1,0:T(8,128)(2,1)}, bf16[12,3,14,384]{3,2,1,0:T(8,128)(2,1)S(1)}, u32[]{:S(2)}, u32[]{:S(2)}) collective-permute-start(bf16[12,3,14,384]{3,2,1,0:T(8,128)(2,1)} %get-tuple-element.131), channel_id=1, source_target_pairs={{0,16},{1,17},{2,18},{3,19},{4,20},{5,21},{6,22},{7,23},{8,24},{9,... | collective-permute-start | bytes 1161224 | tf_op jit(solution)/shard_map/ppermute | solution.py:710
  25.3 17.2 %collective-permute-start.2 = (bf16[20,3,14,384]{3,2,1,0:T(8,128)(2,1)}, bf16[20,3,14,384]{3,2,1,0:T(8,128)(2,1)S(1)}, u32[]{:S(2)}, u32[]{:S(2)}) collective-permute-start(bf16[20,3,14,384]{3,2,1,0:T(8,128)(2,1)} %get-tuple-element.133), channel_id=1, source_target_pairs={{0,16},{1,17},{2,18},{3,19},{4,20},{5,21},{6,22},{7,23},{8,24},{9,... | collective-permute-start | bytes 1935368 | tf_op jit(solution)/shard_map/ppermute | solution.py:710
  76.5 16.2 %collective-permute-start.4 = (bf16[1536,384]{1,0:T(8,128)(2,1)}, bf16[1536,384]{1,0:T(8,128)(2,1)S(1)}, u32[]{:S(2)}, u32[]{:S(2)}) collective-permute-start(bf16[1536,384]{1,0:T(8,128)(2,1)} %bitcast.21), channel_id=1, source_target_pairs={{0,1},{1,0},{2,3},{3,2},{4,5},{5,4},{6,7},{7,6},{8,9},{9,8},{10,11... | collective-permute-start | bytes 3538952 | tf_op jit(solution)/shard_map/ppermute | solution.py:710
  76.5 21.9 %collective-permute-start.3 = (bf16[20,3,14,384]{3,2,1,0:T(8,128)(2,1)}, bf16[20,3,14,384]{3,2,1,0:T(8,128)(2,1)S(1)}, u32[]{:S(2)}, u32[]{:S(2)}) collective-permute-start(bf16[20,3,14,384]{3,2,1,0:T(8,128)(2,1)} %get-tuple-element.140), channel_id=1, source_target_pairs={{0,16},{1,17},{2,18},{3,19},{4,20},{5,21},{6,22},{7,23},{8,24},{9,... | collective-permute-start | bytes 1935368 | tf_op jit(solution)/shard_map/ppermute | solution.py:710
  77.7 15.0 %copy-start.5 = (bf16[4,384,384]{2,1,0:T(8,128)(2,1)S(1)}, bf16[4,384,384]{2,1,0:T(8,128)(2,1)}, u32[]{:S(2)}) copy-start(bf16[4,384,384]{2,1,0:T(8,128)(2,1)} %get-tuple-element.152) | copy-start | bytes 3538948
  77.8 15.0 %copy-start.10 = (s32[4]{0:T(128)S(1)}, s32[4]{0:T(128)}, u32[]{:S(2)}) copy-start(s32[4]{0:T(128)} %pad_add_fusion.where.refs_0_) | copy-start | bytes 52
  95.0 16.4 %collective-permute-start.6 = (bf16[384,384]{1,0:T(8,128)(2,1)}, bf16[384,384]{1,0:T(8,128)(2,1)S(1)}, u32[]{:S(2)}, u32[]{:S(2)}) collective-permute-start(bf16[384,384]{1,0:T(8,128)(2,1)} %get-tuple-element.160), channel_id=1, source_target_pairs={{0,2},{1,3},{2,0},{3,1},{4,6},{5,7},{6,4},{7,5},{8,10},{9,11},{10,... | collective-permute-start | bytes 884744 | tf_op jit(solution)/shard_map/ppermute | solution.py:710
  96.5 14.9 %collective-permute-start.7 = (bf16[384,384]{1,0:T(8,128)(2,1)}, bf16[384,384]{1,0:T(8,128)(2,1)S(1)}, u32[]{:S(2)}, u32[]{:S(2)}) collective-permute-start(bf16[384,384]{1,0:T(8,128)(2,1)} %get-tuple-element.161), channel_id=1, source_target_pairs={{0,16},{1,17},{2,18},{3,19},{4,20},{5,21},{6,22},{7,23},{8,24},{9,... | collective-permute-start | bytes 884744 | tf_op jit(solution)/shard_map/ppermute | solution.py:710
  97.4 14.4 %collective-permute-start.8 = (bf16[384,384]{1,0:T(8,128)(2,1)S(1)}, bf16[384,384]{1,0:T(8,128)(2,1)S(1)}, u32[]{:S(2)}, u32[]{:S(2)}) collective-permute-start(bf16[384,384]{1,0:T(8,128)(2,1)S(1)} %get-tuple-element.162), channel_id=1, source_target_pairs={{0,18},{1,19},{2,16},{3,17},{4,22},{5,23},{6,20},{7,21},{8,26},{9,... | collective-permute-start | bytes 884744 | tf_op jit(solution)/shard_map/ppermute | solution.py:710
  111.3 6.5 %collective-permute-start.5 = (bf16[768,384]{1,0:T(8,128)(2,1)}, bf16[768,384]{1,0:T(8,128)(2,1)S(1)}, u32[]{:S(2)}, u32[]{:S(2)}) collective-permute-start(bf16[768,384]{1,0:T(8,128)(2,1)} %bitcast.22), channel_id=1, source_target_pairs={{0,1},{1,0},{2,3},{3,2},{4,5},{5,4},{6,7},{7,6},{8,9},{9,8},{10,11... | collective-permute-start | bytes 1769480 | tf_op jit(solution)/shard_map/ppermute | solution.py:710
  113.3 7.6 %collective-permute-start.10 = (bf16[96,384]{1,0:T(8,128)(2,1)S(1)}, bf16[96,384]{1,0:T(8,128)(2,1)S(1)}, u32[]{:S(2)}, u32[]{:S(2)}) collective-permute-start(bf16[96,384]{1,0:T(8,128)(2,1)S(1)} %get-tuple-element.170), channel_id=1, source_target_pairs={{0,4},{1,5},{2,6},{3,7},{4,0},{5,1},{6,2},{7,3},{8,12},{9,13},{10,... | collective-permute-start | bytes 221192 | tf_op jit(solution)/shard_map/ppermute | solution.py:710
  115.0 15.5 %collective-permute-start.11 = (bf16[96,384]{1,0:T(8,128)(2,1)S(1)}, bf16[96,384]{1,0:T(8,128)(2,1)S(1)}, u32[]{:S(2)}, u32[]{:S(2)}) collective-permute-start(bf16[96,384]{1,0:T(8,128)(2,1)S(1)} %get-tuple-element.171), channel_id=1, source_target_pairs={{0,8},{1,9},{2,10},{3,11},{4,12},{5,13},{6,14},{7,15},{8,0},{9,1},... | collective-permute-start | bytes 221192 | tf_op jit(solution)/shard_map/ppermute | solution.py:710
  117.6 12.9 %collective-permute-start.12 = (bf16[96,384]{1,0:T(8,128)(2,1)S(1)}, bf16[96,384]{1,0:T(8,128)(2,1)S(1)}, u32[]{:S(2)}, u32[]{:S(2)}) collective-permute-start(bf16[96,384]{1,0:T(8,128)(2,1)S(1)} %get-tuple-element.172), channel_id=1, source_target_pairs={{0,12},{1,13},{2,14},{3,15},{4,8},{5,9},{6,10},{7,11},{8,4},{9,5},... | collective-permute-start | bytes 221192 | tf_op jit(solution)/shard_map/ppermute | solution.py:710
  118.5 12.0 %collective-permute-start.13 = (bf16[192,384]{1,0:T(8,128)(2,1)S(1)}, bf16[192,384]{1,0:T(8,128)(2,1)S(1)}, u32[]{:S(2)}, u32[]{:S(2)}) collective-permute-start(bf16[192,384]{1,0:T(8,128)(2,1)S(1)} %get-tuple-element.174), channel_id=1, source_target_pairs={{0,2},{1,3},{2,0},{3,1},{4,6},{5,7},{6,4},{7,5},{8,10},{9,11},{10,... | collective-permute-start | bytes 442376 | tf_op jit(solution)/shard_map/ppermute | solution.py:710
  120.1 10.4 %collective-permute-start.14 = (bf16[192,384]{1,0:T(8,128)(2,1)S(1)}, bf16[192,384]{1,0:T(8,128)(2,1)S(1)}, u32[]{:S(2)}, u32[]{:S(2)}) collective-permute-start(bf16[192,384]{1,0:T(8,128)(2,1)S(1)} %get-tuple-element.175), channel_id=1, source_target_pairs={{0,16},{1,17},{2,18},{3,19},{4,20},{5,21},{6,22},{7,23},{8,24},{9,... | collective-permute-start | bytes 442376 | tf_op jit(solution)/shard_map/ppermute | solution.py:710
  121.0 9.5 %collective-permute-start.15 = (bf16[192,384]{1,0:T(8,128)(2,1)S(1)}, bf16[192,384]{1,0:T(8,128)(2,1)S(1)}, u32[]{:S(2)}, u32[]{:S(2)}) collective-permute-start(bf16[192,384]{1,0:T(8,128)(2,1)S(1)} %get-tuple-element.176), channel_id=1, source_target_pairs={{0,18},{1,19},{2,16},{3,17},{4,22},{5,23},{6,20},{7,21},{8,26},{9,... | collective-permute-start | bytes 442376 | tf_op jit(solution)/shard_map/ppermute | solution.py:710
  129.2 17.7 %copy-start.4 = (bf16[20,3,14,384]{3,2,1,0:T(8,128)(2,1)S(1)}, bf16[20,3,14,384]{3,2,1,0:T(8,128)(2,1)}, u32[]{:S(2)}) copy-start(bf16[20,3,14,384]{3,2,1,0:T(8,128)(2,1)} %copy-done.3) | copy-start | bytes 1935364
  131.6 5.3 %collective-permute-start.16 = (bf16[96,384]{1,0:T(8,128)(2,1)S(1)}, bf16[96,384]{1,0:T(8,128)(2,1)S(1)}, u32[]{:S(2)}, u32[]{:S(2)}) collective-permute-start(bf16[96,384]{1,0:T(8,128)(2,1)S(1)} %get-tuple-element.182), channel_id=1, source_target_pairs={{0,4},{1,5},{2,6},{3,7},{4,0},{5,1},{6,2},{7,3},{8,12},{9,13},{10,... | collective-permute-start | bytes 221192 | tf_op jit(solution)/shard_map/ppermute | solution.py:710
  132.3 7.4 %collective-permute-start.17 = (bf16[96,384]{1,0:T(8,128)(2,1)S(1)}, bf16[96,384]{1,0:T(8,128)(2,1)S(1)}, u32[]{:S(2)}, u32[]{:S(2)}) collective-permute-start(bf16[96,384]{1,0:T(8,128)(2,1)S(1)} %get-tuple-element.183), channel_id=1, source_target_pairs={{0,8},{1,9},{2,10},{3,11},{4,12},{5,13},{6,14},{7,15},{8,0},{9,1},... | collective-permute-start | bytes 221192 | tf_op jit(solution)/shard_map/ppermute | solution.py:710
  135.8 6.5 %collective-permute-start.18 = (bf16[96,384]{1,0:T(8,128)(2,1)S(1)}, bf16[96,384]{1,0:T(8,128)(2,1)S(1)}, u32[]{:S(2)}, u32[]{:S(2)}) collective-permute-start(bf16[96,384]{1,0:T(8,128)(2,1)S(1)} %get-tuple-element.184), channel_id=1, source_target_pairs={{0,12},{1,13},{2,14},{3,15},{4,8},{5,9},{6,10},{7,11},{8,4},{9,5},... | collective-permute-start | bytes 221192 | tf_op jit(solution)/shard_map/ppermute | solution.py:710
  136.0 18.2 %collective-permute-start.9 = (bf16[20,3,14,384]{3,2,1,0:T(8,128)(2,1)S(1)}, bf16[20,3,14,384]{3,2,1,0:T(8,128)(2,1)S(1)}, u32[]{:S(2)}, u32[]{:S(2)}) collective-permute-start(bf16[20,3,14,384]{3,2,1,0:T(8,128)(2,1)S(1)} %get-tuple-element.166), channel_id=1, source_target_pairs={{0,16},{1,17},{2,18},{3,19},{4,20},{5,21},{6,22},{7,23},{8,24},{9,... | collective-permute-start | bytes 1935368 | tf_op jit(solution)/shard_map/ppermute | solution.py:710
  142.4 6.0 %collective-permute-start.19 = (bf16[144,384]{1,0:T(8,128)(2,1)S(1)}, bf16[144,384]{1,0:T(8,128)(2,1)S(1)}, u32[]{:S(2)}, u32[]{:S(2)}) collective-permute-start(bf16[144,384]{1,0:T(8,128)(2,1)S(1)} %get-tuple-element.186.refs_1_), channel_id=1, source_target_pairs={{0,4},{1,5},{2,6},{3,7},{4,0},{5,1},{6,2},{7,3},{8,12},{9,13},{10,... | collective-permute-start | bytes 331784 | tf_op jit(solution)/shard_map/ppermute | solution.py:710
  142.5 8.6 %collective-permute-start.20 = (bf16[144,384]{1,0:T(8,128)(2,1)S(1)}, bf16[144,384]{1,0:T(8,128)(2,1)S(1)}, u32[]{:S(2)}, u32[]{:S(2)}) collective-permute-start(bf16[144,384]{1,0:T(8,128)(2,1)S(1)} %get-tuple-element.186.refs_1_), channel_id=1, source_target_pairs={{0,8},{1,9},{2,10},{3,11},{4,12},{5,13},{6,14},{7,15},{8,0},{9,1},... | collective-permute-start | bytes 331784 | tf_op jit(solution)/shard_map/ppermute | solution.py:710
  143.6 7.6 %collective-permute-start.21 = (bf16[144,384]{1,0:T(8,128)(2,1)S(1)}, bf16[144,384]{1,0:T(8,128)(2,1)S(1)}, u32[]{:S(2)}, u32[]{:S(2)}) collective-permute-start(bf16[144,384]{1,0:T(8,128)(2,1)S(1)} %get-tuple-element.186.refs_1_), channel_id=1, source_target_pairs={{0,12},{1,13},{2,14},{3,15},{4,8},{5,9},{6,10},{7,11},{8,4},{9,5},... | collective-permute-start | bytes 331784 | tf_op jit(solution)/shard_map/ppermute | solution.py:710
  146.9 1.5 collective-permute-start.22
  151.7 10.8 %collective-permute-start.23 = (bf16[624,384]{1,0:T(8,128)(2,1)S(1)}, bf16[624,384]{1,0:T(8,128)(2,1)S(1)}, u32[]{:S(2)}, u32[]{:S(2)}) collective-permute-start(bf16[624,384]{1,0:T(8,128)(2,1)S(1)} %lay.1.own.first), channel_id=1, source_target_pairs={{0,16},{1,17},{2,18},{3,19},{4,20},{5,21},{6,22},{7,23},{8,24},{9,... | collective-permute-start | bytes 1437704 | tf_op jit(solution)/shard_map/ppermute | solution.py:710
  152.7 10.4 %collective-permute-start.24 = (bf16[624,384]{1,0:T(8,128)(2,1)S(1)}, bf16[624,384]{1,0:T(8,128)(2,1)S(1)}, u32[]{:S(2)}, u32[]{:S(2)}) collective-permute-start(bf16[624,384]{1,0:T(8,128)(2,1)S(1)} %lay.1.own.first), channel_id=1, source_target_pairs={{0,2},{1,3},{2,0},{3,1},{4,6},{5,7},{6,4},{7,5},{8,10},{9,11},{10,... | collective-permute-start | bytes 1437704 | tf_op jit(solution)/shard_map/ppermute | solution.py:710
  163.1 7.5 %collective-permute-start.26 = (bf16[320,384]{1,0:T(8,128)(2,1)S(1)}, bf16[320,384]{1,0:T(8,128)(2,1)S(1)}, u32[]{:S(2)}, u32[]{:S(2)}) collective-permute-start(bf16[320,384]{1,0:T(8,128)(2,1)S(1)} %get-tuple-element.191), channel_id=1, source_target_pairs={{0,16},{1,17},{2,18},{3,19},{4,20},{5,21},{6,22},{7,23},{8,24},{9,... | collective-permute-start | bytes 737288 | tf_op jit(solution)/shard_map/ppermute | solution.py:710
  164.4 6.1 %collective-permute-start.25 = (bf16[304,384]{1,0:T(8,128)(2,1)S(1)}, bf16[304,384]{1,0:T(8,128)(2,1)S(1)}, u32[]{:S(2)}, u32[]{:S(2)}) collective-permute-start(bf16[304,384]{1,0:T(8,128)(2,1)S(1)} %get-tuple-element.190), channel_id=1, source_target_pairs={{0,2},{1,3},{2,0},{3,1},{4,6},{5,7},{6,4},{7,5},{8,10},{9,11},{10,... | collective-permute-start | bytes 700424 | tf_op jit(solution)/shard_map/ppermute | solution.py:710
  170.7 5.8 %collective-permute-start.28 = (bf16[3,576,384]{2,1,0:T(8,128)(2,1)S(1)}, bf16[3,576,384]{2,1,0:T(8,128)(2,1)S(1)}, u32[]{:S(2)}, u32[]{:S(2)}) collective-permute-start(bf16[3,576,384]{2,1,0:T(8,128)(2,1)S(1)} %get-tuple-element.195.rest), channel_id=1, source_target_pairs={{0,1},{1,0},{2,3},{3,2},{4,5},{5,4},{6,7},{7,6},{8,9},{9,8},{10,11... | collective-permute-start | bytes 3981320 | tf_op jit(solution)/shard_map/ppermute | solution.py:710
  170.8 5.7 %collective-permute-start.27 = (bf16[624,384]{1,0:T(8,128)(2,1)S(1)}, bf16[624,384]{1,0:T(8,128)(2,1)S(1)}, u32[]{:S(2)}, u32[]{:S(2)}) collective-permute-start(bf16[624,384]{1,0:T(8,128)(2,1)S(1)} %lay.1.own.first), channel_id=1, source_target_pairs={{0,1},{1,0},{2,3},{3,2},{4,5},{5,4},{6,7},{7,6},{8,9},{9,8},{10,11... | collective-permute-start | bytes 1437704 | tf_op jit(solution)/shard_map/ppermute | solution.py:710
  (32 other events, 234.1 us)

commit v3 on v2

--- a/solution.py
+++ b/solution.py
@@ -71,6 +71,21 @@
 
 
 SMALL = 24
+
+
+ROWS = 32
+
+
+def by_rows(function, *arrays):
+    parts = [
+        function(*(array[start : start + ROWS, :] for array in arrays))
+        for start in range(0, arrays[0].shape[0], ROWS)
+    ]
+    return tuple(jnp.concatenate(part, axis=0) for part in zip(*parts))
+
+
+def by_eights(values):
+    return jnp.sum(values.reshape(values.shape[0] // 8, 8, values.shape[1]), axis=0)
 
 
 def launch(kernel, name, grid, inputs, in_specs, out_shape, out_specs, so_far=(), scratch=(), flops=0,
@@ -269,7 +284,8 @@
 
 
 def finish_small_kernel(*refs):
-    ins, small, outs = refs[:13], refs[13], refs[14:]
+    ins, small, outs, token = refs[:13], refs[13], refs[14:-1], refs[-1]
+    token[...] = jnp.zeros_like(token)
     (in_w, in_b, g1, s1, w1, b1, g2, s2, w2, b2, g3, s3, w3) = ins
     (o_n1_gain, o_n1_shift, o_qv, o_proj_b, o_n2_gain, o_n2_shift, o_fc1_b, o_fc2_b) = outs[:8]
     (o_in_w, o_in_b, o_g1, o_s1, o_w1, o_b1, o_g2, o_s2, o_w2, o_b2, o_g3, o_s3, o_w3) = outs[8:]
@@ -314,12 +330,20 @@
         finish_small_kernel,
         "finish_small",
         (*pos, small),
-        [shaped(s, F32) for s in shapes] + [shaped(p.shape, F32) for p in pos],
+        [shaped(s, F32) for s in shapes] + [shaped(p.shape, F32) for p in pos] + [TOKEN],
     )
 
 
 def stack_heads(block, mask):
     return jnp.concatenate([block] * PER_BLOCK, axis=0) * mask
+
+
+def head_rows(head, start=0):
+    return slice(start + head * TOKENS, start + (head + 1) * TOKENS)
+
+
+def half_lanes(half):
+    return slice(half * LANES, (half + 1) * LANES)
 
 
 def two_images(two):
@@ -368,8 +392,8 @@
     place_rows(where[0], images, received, padded)
     x = padded[...].reshape(count * TOKENS, width)
     x_out[...] = x
-    hat, _ = normalise(x.astype(F32))
-    normed = (hat * gain[...][None, :] + shift[...][None, :]).astype(BF16)
+    gains, shifts = gain[...][None, :], shift[...][None, :]
+    (normed,) = by_rows(lambda v: ((normalise(v.astype(F32))[0] * gains + shifts).astype(BF16),), x)
     normed_out[...] = normed
     piece = dot(normed, weight[...])
     qkv_out[:, 0:width] = (piece[:, 0:width] + bias[0:1, :]).astype(BF16)
@@ -383,11 +407,18 @@
             here = slice(block * STACK, (block + 1) * STACK)
             query = on_diagonal([qkv_out[rows, at : at + LANES] for rows in both])
             keys = side_by_side([qkv_out[rows, width + at : width + at + LANES] for rows in both], masks)
-            scores = dot_nt(keys, query) * SCALE + jnp.concatenate([pair[here, :]] * 2, axis=1)
-            scores = scores.reshape(PER_BLOCK, TOKENS, 2 * LANES)
-            probs = jnp.exp(scores - jnp.max(scores, axis=1, keepdims=True))
-            probs = probs * (1.0 / jnp.sum(probs, axis=1, keepdims=True))
-            probs = probs.astype(BF16).reshape(STACK, 2 * LANES)
+            scores = dot_nt(keys, query)
+            probs = []
+            for head in range(PER_BLOCK):
+                bias_here = pair[head_rows(head, block * STACK), :]
+                halves = []
+                for half in range(2):
+                    values = scores[head_rows(head), half_lanes(half)] * SCALE + bias_here
+                    values = jnp.exp(values - jnp.max(values, axis=0, keepdims=True))
+                    values = values * (1.0 / jnp.sum(values, axis=0, keepdims=True))
+                    halves.append(values.astype(BF16))
+                probs.append(jnp.concatenate(halves, axis=1))
+            probs = jnp.concatenate(probs, axis=0)
             probs_out[two, here, :] = probs
             for half, rows in enumerate(both):
                 vals = stack_heads(qkv_out[rows, 2 * width + at : 2 * width + at + LANES], masks)
@@ -570,12 +601,20 @@
             grad = on_diagonal([grad_att[rows, at : at + LANES] for rows in both])
             vals = side_by_side([qkv[rows, 2 * width + at : 2 * width + at + LANES] for rows in both], masks)
             probs = probs_ref[two, here, :]
-            exact = probs.astype(F32).reshape(PER_BLOCK, TOKENS, 2 * LANES)
-            grad_probs = dot_nt(vals, grad).reshape(PER_BLOCK, TOKENS, 2 * LANES)
-            inner = jnp.sum(grad_probs * exact, axis=1, keepdims=True)
-            exact_scores = (exact * (grad_probs - inner)).reshape(STACK, 2 * LANES)
-            o_pair[here, :] += exact_scores[:, :LANES] + exact_scores[:, LANES:]
-            grad_scores = exact_scores.astype(BF16)
+            grad_probs = dot_nt(vals, grad)
+            grad_scores = []
+            for head in range(PER_BLOCK):
+                halves, total = [], None
+                for half in range(2):
+                    exact = probs[head_rows(head), half_lanes(half)].astype(F32)
+                    values = grad_probs[head_rows(head), half_lanes(half)]
+                    inner = jnp.sum(values * exact, axis=0, keepdims=True)
+                    values = exact * (values - inner)
+                    total = values if total is None else total + values
+                    halves.append(values.astype(BF16))
+                o_pair[head_rows(head, block * STACK), :] += total
+                grad_scores.append(jnp.concatenate(halves, axis=1))
+            grad_scores = jnp.concatenate(grad_scores, axis=0)
             grad_keys = dot(grad_scores, query)
             grad_vals = dot(probs, grad)
             for half, rows in enumerate(both):
@@ -589,8 +628,13 @@
                 grads[rows, 2 * width + at : 2 * width + at + LANES] = pick_heads(grad_vals[:, lanes]).astype(BF16)
     all_grads = grads[...]
     a_w[...] += dot(normed[...].T, all_grads)
-    o_small[0:1, :] += column_sum(all_grads[:, :width].astype(F32))
-    o_small[1:2, :] += column_sum(all_grads[:, 2 * width :].astype(F32))
+    sums = [jnp.zeros((8, width), F32)] * 2
+    for start in range(0, count * TOKENS, ROWS):
+        piece = grads[start : start + ROWS, :]
+        sums[0] = sums[0] + by_eights(piece[:, :width].astype(F32))
+        sums[1] = sums[1] + by_eights(piece[:, 2 * width :].astype(F32))
+    o_small[0:1, :] += column_sum(sums[0])
+    o_small[1:2, :] += column_sum(sums[1])
 
     @pl.when(step == pl.num_programs(0) - 1)
     def _():
@@ -607,7 +651,7 @@
             o_second[...] = jnp.zeros_like(o_second)
 
 
-def attend_back(where, first, count, per_step, saved, mask, grad_proj, carried, so_far, last_call, after):
+def attend_back(where, first, count, per_step, saved, mask, grad_proj, carried, so_far, last_call, after, through):
     normed, qkv, probs, grad_att = saved
     width = normed.shape[1]
     begin = first // per_step
@@ -648,6 +692,7 @@
         ],
         flops=count * TOKENS * width * width * 18,
         after=after,
+        through=through,
         vmem=60,
     )
 
@@ -660,11 +705,20 @@
     def _():
         o_small[...] = jnp.zeros_like(o_small) if first_call else carried[0][...]
 
-    grad_normed = dot_nt(grads[...], weight[...]).astype(BF16).astype(F32)
-    hat, inverse = normalise(x_ref[...].astype(F32))
-    o_small[0:1, :] += column_sum(grad_normed * hat)
-    o_small[1:2, :] += column_sum(grad_normed)
-    grad_image = grad_mid[...] + normalise_back(grad_normed * gain[...][None, :], hat, inverse)
+    product = dot_nt(grads[...], weight[...])
+    gains = gain[...][None, :]
+    sums = [jnp.zeros((8, product.shape[1]), F32)] * 2
+
+    def rows_of(values, x, grad_middle):
+        grad_normed = values.astype(BF16).astype(F32)
+        hat, inverse = normalise(x.astype(F32))
+        sums[0] = sums[0] + by_eights(grad_normed * hat)
+        sums[1] = sums[1] + by_eights(grad_normed)
+        return (grad_middle + normalise_back(grad_normed * gains, hat, inverse),)
+
+    (grad_image,) = by_rows(rows_of, product, x_ref, grad_mid)
+    o_small[0:1, :] += column_sum(sums[0])
+    o_small[1:2, :] += column_sum(sums[1])
     placed[...] = grad_image.reshape(placed.shape)
     return_rows(where[0], placed, gi_kept, gi_send)
 
@@ -789,11 +843,12 @@
 
 
 def lay_kernel(slot, where, *refs):
-    parts, (small, other, out) = refs[:-3], refs[-3:]
+    parts, (small, other, out, pair) = refs[:-4], refs[-4:]
     rows = parts[0].shape[0]
     for d, ref in enumerate(parts):
         out[pl.ds(pl.multiple_of((where[slot] ^ d) * rows, rows), rows), :] = ref[...]
-    put_pair(out, len(parts) * rows, small[...] + other[...])
+    put_pair(pair, 0, small[...] + other[...])
+    out[len(parts) * rows :, :] = pair[...]
 
 
 def along(value, d):
@@ -811,42 +866,47 @@
         partial(lay_kernel, 3),
         "lay",
         (where, *parts, small, swap(small, (0, 1))),
-        [shaped((ALONG * rows + 2 * SMALL, width), BF16)],
+        [shaped((ALONG * rows + 2 * SMALL, width), BF16), shaped((2 * SMALL, width), BF16)],
         after=after,
-    )[0]
-
-
-def halve_kernel(across, along_row, low, high):
-    low[...] = across[0 : low.shape[0], :]
-    high[...] = along_row[low.shape[0] :, :]
-
-
-def collect_kernel(own, across, along_row, low, high, out, small):
+    )
+
+
+def halve_kernel(own, across, along_row, far, low, high, small):
+    rows, cut = own.shape[0] - 2 * SMALL, low.shape[0]
+    low[...] = across[0:cut, :]
+    high[...] = along_row[cut:rows, :]
+    small[...] = (get_pair(own, rows) + get_pair(along_row, rows)) + (get_pair(across, rows) + get_pair(far, 0))
+
+
+def collect_kernel(across, along_row, low, high, out):
     rows, cut = out.shape[1], low.shape[0]
     out[0] = along_row[0:rows, :]
     out[1] = across[0:rows, :]
     out[2, 0:cut, :] = low[...]
-    out[2, cut:rows, :] = high[0 : rows - cut, :]
-    far = get_pair(high, rows - cut)
-    small[...] = (get_pair(own, rows) + get_pair(along_row, rows)) + (get_pair(across, rows) + far)
-
-
-def gather_plane(quarter, after):
+    out[2, cut:rows, :] = high[...]
+
+
+def gather_plane(quarter, pair, after, finish):
     theirs = swap(quarter, (0, 1))
-    rows, width = quarter.shape
+    rows, width = quarter.shape[0] - 2 * SMALL, quarter.shape[1]
     across, along_row = in_plane(quarter, 2), in_plane(quarter, 1)
     cut = rows // 32 * 16
-    low, high = small_launch(
-        halve_kernel, "halve", (across, along_row), [shaped((cut, width), BF16), shaped((rows - cut, width), BF16)],
+    low, high, small = small_launch(
+        halve_kernel,
+        "halve",
+        (quarter, across, along_row, in_plane(pair, 3)),
+        [shaped((cut, width), BF16), shaped((rows - cut, width), BF16), shaped((SMALL, width), F32)],
         after=after,
     )
-    mine, small = small_launch(
+    *smalls, token = finish(small)
+    mine = small_launch(
         collect_kernel,
         "collect",
-        (quarter, across, along_row, in_plane(low, 1), in_plane(high, 2)),
-        [shaped((PLANE - 1, rows - 2 * SMALL, width), BF16), shaped((SMALL, width), F32)],
-    )
-    return small, (quarter, mine), (theirs, swap(mine, (0, 1)))
+        (across, along_row, in_plane(low, 1), in_plane(high, 2)),
+        [shaped((PLANE - 1, rows, width), BF16)],
+        after=(token,),
+    )[0]
+    return smalls, (quarter, mine), (theirs, swap(mine, (0, 1)))
 
 
 def unpack_kernel(flip, early, where, first, rest, o_w1, o_w2, o_qkv, o_proj, feed_buf, att_buf, sems):
@@ -934,7 +994,7 @@
     later_packed, cot_packed, _ = pack_rows(
         (images, cotangent), [(0, *image_chunks[1]), (1, 0, total)], (token,)
     )
-    pair, later_packed, cot_packed = pair_bias(pos, (later_packed, cot_packed))
+    pair, cot_packed = pair_bias(pos, (cot_packed,))
     later_received = to_partner(later_packed)
     norm_one = (norm1_gain, norm1_shift, qkv_weight, qv_bias, pair, mask)
     so_far = attend(where, images, received, 0, per_step, *norm_one, (), ())
@@ -949,15 +1009,16 @@
     out_images, grad_mid, grad_att, out_sent, feed_small, feed_b1, mine, theirs, grad_proj = result
     out_rows = to_partner(out_sent)
     flat = lambda value: value.reshape(-1, width)
-    early = [flat(mine), swap(flat(theirs), (0, 1))]
 
     saved = (normed, qkv, probs, grad_att)
     chunks = [(0, total - later), (total - later, later)]
-    result = attend_back(where, *chunks[0], per_step, saved, mask, grad_proj, None, (), False, ())
-    *pieces, token = split_share(where, 2, PLANE, early, (result[1],))
+    theirs = swap(flat(theirs), (0, 1))
+    *result, mine = attend_back(where, *chunks[0], per_step, saved, mask, grad_proj, None, (), False, (), (flat(mine),))
+    early = [mine, theirs]
+    *pieces, token = split_share(where, 2, PLANE, early, (out_rows,))
     early = spread(pieces, in_plane)
     result = attend_back(where, *chunks[1], per_step, saved, mask, grad_proj, result[1:4], result[:1], True,
-                         (token, out_rows))
+                         (token,), ())
     grads, att_small, grad_pair = result[:3]
     mine, theirs = flat(result[3]), flat(result[4])
     *pieces, token = split_share(where, 3, ALONG, early, (att_small,), 5e9)
@@ -977,10 +1038,11 @@
         small = small + swap(small, (0, stride))
         stride *= 2
     out_images, token = merge_rows(out_rows, out_images, 0)
-    quarter = gather_along(where, share, small, (token,))
+    quarter, own_pair = gather_along(where, share, small, (token,))
     grad_images, token = merge_rows(grad_rows, grad_images, 0)
-    small, half, other_half = gather_plane(quarter, (token,))
-    smalls = finish_small(pos, small, hidden)
+    smalls, half, other_half = gather_plane(
+        quarter, own_pair, (token,), lambda small: finish_small(pos, small, hidden)
+    )
     shapes = [w.shape for w in (fc1_weight, fc2_weight, qkv_weight, proj_weight)]
     large = unpack(0, early[0].shape[0], where, half, shapes, ())
     grad_fc1, grad_fc2, grad_qkv, grad_proj = unpack(1, early[0].shape[0], where, other_half, shapes, large)

time: 180 us -> 181 us (level)
  starting transfers between devices: 31.9 us -> 36.3 us
    ppermute x29 -> x30, starting transfers between devices: 31.9 us -> 36.3 us  [swap(): return lax.ppermute(value, ('band', 'batch'), pairs)]
    ppermute x29 -> x30, waiting for transfers between devices: 26.8 us -> 25.2 us  [swap(): return lax.ppermute(value, ('band', 'batch'), pairs)]
    unnamed x70 -> x64, local copies, waits for them, and re-layouts: 4.91 us -> 4.71 us
  transfers between devices with their start and end apart: 29 -> 30, of which waited for: 9 -> 12; matrix products, arithmetic and copies ran while one was open for 0% -> 0% of each run, Pallas kernels for 42% -> 40%
where the time goes in v3:
time: 181 us
  Pallas kernels  113 us (62%)
  starting transfers between devices  36.3 us (20%)
  waiting for transfers between devices  25.2 us (14%)
  local copies, waits for them, and re-layouts  4.71 us (3%)
    pallas_call x24, Pallas kernels, launch(): pl.pallas_call(kernel, grid=grid, in_specs=list(in_specs) + [pl.BlockSpec...  113 us
    ppermute x30, starting transfers between devices, swap(): return lax.ppermute(value, ('band', 'batch'), pairs)  36.3 us
    ppermute x30, waiting for transfers between devices, swap(): return lax.ppermute(value, ('band', 'batch'), pairs)  25.2 us
    unnamed x64, local copies, waits for them, and re-layouts  4.71 us
  transfers between devices with their start and end apart: 30, of which 12 were waited for; matrix products, arithmetic and copies ran while one was open for 0% of the time, Pallas kernels for 40%

profile of v3, /device:TPU:0, one launch (start us, length us, event | category | flops | bytes accessed | tf_op | source)
XLA Modules:
  0.0 180.8 jit_solution(13617925978035867388)
XLA Ops:
  0.7 1.7 pack_rows.2
  2.4 3.0 %collective-permute-start = (bf16[8,3,14,384]{3,2,1,0:T(8,128)(2,1)}, bf16[8,3,14,384]{3,2,1,0:T(8,128)(2,1)S(1)}, u32[]{:S(2)}, u32[]{:S(2)}) collective-permute-start(bf16[8,3,14,384]{3,2,1,0:T(8,128)(2,1)} %get-tuple-element.127), channel_id=1, source_target_pairs={{0,16},{1,17},{2,18},{3,19},{4,20},{5,21},{6,22},{7,23},{8,24},{9,... | collective-permute-start | bytes 774152 | tf_op jit(solution)/shard_map/ppermute | solution.py:764
  5.4 2.4 %pack_rows.3 = (bf16[12,3,14,384]{3,2,1,0:T(8,128)(2,1)}, bf16[20,3,14,384]{3,2,1,0:T(8,128)(2,1)}, f32[8,128]{1,0:T(8,128)}) custom-call(bf16[20,7,14,384]{3,2,1,0:T(8,128)(2,1)} %refs_1_.6, bf16[20,7,14,384]{3,2,1,0:T(8,128)(2,1)} %cot.1, f32[8,128]{1,0:T(8,128)} %get-tuple-element.128.refs_2_), custom_call_target="tpu_custom_call" | custom-call | bytes 4046848 | tf_op jit(solution)/shard_map/pack_rows/pallas_call | solution.py:102
  8.0 4.3 %pair_bias.1 = (f32[12,112,128]{2,1,0:T(8,128)}, bf16[20,3,14,384]{3,2,1,0:T(8,128)(2,1)}) custom-call(f32[2,96]{1,0:T(2,128)} %refs_0_.7, f32[96]{0:T(128)} %refs_1_.7, f32[96]{0:T(128)} %refs_2_.3, f32[96]{0:T(128)} %refs_3_.5, f32[96,96]{1,0:T(8,128)} %refs_4_.7, f32[96]{0:T(128)} %refs_5_.9, f32[96]{0:T(128)} %refs_6_.5, ...), custom_call_target="tpu_custom_call", output_to_operand_aliasing={{1}: (13, {})} | custom-call | bytes 770688 | tf_op jit(solution)/shard_map/pair_bias/pallas_call | solution.py:102
  14.2 9.0 %attend.2 = (bf16[2240,384]{1,0:T(8,128)(2,1)}, bf16[2240,384]{1,0:T(8,128)(2,1)}, bf16[2240,1152]{1,0:T(8,128)(2,1)}, bf16[10,1344,256]{2,1,0:T(8,128)(2,1)}, bf16[2240,384]{1,0:T(8,128)(2,1)}) custom-call(s32[4]{0:T(128)} %pad_add_fusion.where.refs_0_, bf16[20,7,14,384]{3,2,1,0:T(8,128)(2,1)} %refs_1_.6, bf16[8,3,14,384]{3,2,1,0:T(8,128)(2,1)} %copy-done.29, ...), custom_call_target="tpu_custom_call" | custom-call | flops 1585446912 | bytes 20660240 | tf_op jit(solution)/shard_map/attend/pallas_call | solution.py:102
  24.5 2.1 %collective-permute-start.2 = (bf16[20,3,14,384]{3,2,1,0:T(8,128)(2,1)}, bf16[20,3,14,384]{3,2,1,0:T(8,128)(2,1)S(1)}, u32[]{:S(2)}, u32[]{:S(2)}) collective-permute-start(bf16[20,3,14,384]{3,2,1,0:T(8,128)(2,1)} %get-tuple-element.134), channel_id=1, source_target_pairs={{0,16},{1,17},{2,18},{3,19},{4,20},{5,21},{6,22},{7,23},{8,24},{9,... | collective-permute-start | bytes 1935368 | tf_op jit(solution)/shard_map/ppermute | solution.py:764
  26.6 11.8 %attend.3 = (bf16[2240,384]{1,0:T(8,128)(2,1)}, bf16[2240,384]{1,0:T(8,128)(2,1)}, bf16[2240,1152]{1,0:T(8,128)(2,1)}, bf16[10,1344,256]{2,1,0:T(8,128)(2,1)}, bf16[2240,384]{1,0:T(8,128)(2,1)}) custom-call(s32[4]{0:T(128)} %pad_add_fusion.where.refs_0_, ...), custom_call_target="tpu_custom_call", output_to_operand_aliasing={{0}: (9, {}), {1}: (10, {}), {2}: (11, {}), {3}: (12, {}), ... | custom-call | flops 2378170368 | bytes 20789264 | tf_op jit(solution)/shard_map/attend/pallas_call | solution.py:102
  38.4 3.8 %collective-permute-done.2.received = bf16[20,3,14,384]{3,2,1,0:T(8,128)(2,1)S(1)} collective-permute-done((bf16[20,3,14,384]{3,2,1,0:T(8,128)(2,1)}, bf16[20,3,14,384]{3,2,1,0:T(8,128)(2,1)S(1)}, u32[]{:S(2)}, u32[]{:S(2)}) %collective-permute-start.2) | collective-permute-done | bytes 645152 | tf_op jit(solution)/shard_map/ppermute | solution.py:764
  43.0 33.0 %feed.1 = (bf16[20,7,14,384]{3,2,1,0:T(8,128)(2,1)}, f32[2240,384]{1,0:T(8,128)}, bf16[2240,384]{1,0:T(8,128)(2,1)}, bf16[20,3,14,384]{3,2,1,0:T(8,128)(2,1)}, f...) custom-call(s32[4]{0:T(128)} %pad_add_fusion.where.refs_0_, ...), custom_call_target="tpu_custom_call" | custom-call | flops 17836277760 | bytes 18536464 | tf_op jit(solution)/shard_map/feed/pallas_call | solution.py:102
  76.2 1.8 collective-permute-start.3
  77.9 14.7 %attend_back.2 = (bf16[2240,1152]{1,0:T(8,128)(2,1)}, f32[8,384]{1,0:T(8,128)}, f32[1344,128]{1,0:T(8,128)}, f32[384,1152]{1,0:T(8,128)}, f32[8,128]{1,0:T(8,128)}, /*index=5*/bf16[1536,384]{1,0:T(8,128)(2,1)}) custom-call(s32[4]{0:T(128)} %pad_add_fusion.where.refs_0_, ...), custom_call_target="tpu_custom_call", output_to_operand_aliasing={{5}: (7, {})} | custom-call | flops 3567255552 | bytes 23822352 | tf_op jit(solution)/shard_map/attend_back/pallas_call | solution.py:102
  92.6 2.7 %collective-permute-done.3.refs_0_.refs_3_ = bf16[20,3,14,384]{3,2,1,0:T(8,128)(2,1)S(1)} collective-permute-done((bf16[20,3,14,384]{3,2,1,0:T(8,128)(2,1)}, bf16[20,3,14,384]{3,2,1,0:T(8,128)(2,1)S(1)}, u32[]{:S(2)}, u32[]{:S(2)}) %collective-permute-start.3) | collective-permute-done | bytes 645152 | tf_op jit(solution)/shard_map/ppermute | solution.py:764
  97.4 1.7 collective-permute-start.6
  101.0 11.8 %attend_back.3 = (bf16[2240,1152]{1,0:T(8,128)(2,1)}, f32[8,384]{1,0:T(8,128)}, f32[1344,128]{1,0:T(8,128)}, bf16[2,384,384]{2,1,0:T(8,128)(2,1)}, bf16[2,384,384]{2,1,0:T(8,128)(2,1)}) custom-call(s32[4]{0:T(128)} %pad_add_fusion.where.refs_0_, bf16[2240,384]{1,0:T(8,128)(2,1)} %get-tuple-element.144.refs_1_, ...), custom_call_target="tpu_custom_call", output_to_operand_aliasing={{0}: (10, {})} | custom-call | flops 2378170368 | bytes 25698320 | tf_op jit(solution)/shard_map/attend_back/pallas_call | solution.py:102
  115.2 1.8 collective-permute-start.10
  116.9 2.6 %collective-permute-start.11 = (bf16[96,384]{1,0:T(8,128)(2,1)S(1)}, bf16[96,384]{1,0:T(8,128)(2,1)S(1)}, u32[]{:S(2)}, u32[]{:S(2)}) collective-permute-start(bf16[96,384]{1,0:T(8,128)(2,1)S(1)} %get-tuple-element.173), channel_id=1, source_target_pairs={{0,8},{1,9},{2,10},{3,11},{4,12},{5,13},{6,14},{7,15},{8,0},{9,1},... | collective-permute-start | bytes 221192 | tf_op jit(solution)/shard_map/ppermute | solution.py:764
  120.3 1.7 collective-permute-start.13
  122.0 1.5 collective-permute-start.14
  123.9 6.9 %image_grads.1 = (f32[20,7,14,384]{3,2,1,0:T(8,128)}, bf16[20,3,14,384]{3,2,1,0:T(8,128)(2,1)S(1)}, f32[8,384]{1,0:T(8,128)S(1)}) custom-call(s32[4]{0:T(128)S(1)} %copy-done.9, bf16[2240,1152]{1,0:T(8,128)(2,1)S(1)} %bitcast.13, bf16[2240,384]{1,0:T(8,128)(2,1)S(1)} %copy-done, f32[2240,384]{1,0:T(8,128)S(1)} %copy-done.3, f32[384]{0:T(512)S(1)} %copy-done.14, ...), custom_call_target="tpu_custom_call" | custom-call | flops 1981808640 | bytes 14876176 | tf_op jit(solution)/shard_map/image_grads/pallas_call | solution.py:102
  134.2 3.5 %collective-permute-start.17 = (bf16[96,384]{1,0:T(8,128)(2,1)S(1)}, bf16[96,384]{1,0:T(8,128)(2,1)S(1)}, u32[]{:S(2)}, u32[]{:S(2)}) collective-permute-start(bf16[96,384]{1,0:T(8,128)(2,1)S(1)} %get-tuple-element.185), channel_id=1, source_target_pairs={{0,8},{1,9},{2,10},{3,11},{4,12},{5,13},{6,14},{7,15},{8,0},{9,1},... | collective-permute-start | bytes 221192 | tf_op jit(solution)/shard_map/ppermute | solution.py:764
  137.8 1.7 collective-permute-start.9
  139.4 2.3 %collective-permute-done.17.refs_6_ = bf16[96,384]{1,0:T(8,128)(2,1)S(1)} collective-permute-done((bf16[96,384]{1,0:T(8,128)(2,1)S(1)}, bf16[96,384]{1,0:T(8,128)(2,1)S(1)}, u32[]{:S(2)}, u32[]{:S(2)}) %collective-permute-start.17) | collective-permute-done | bytes 73760 | tf_op jit(solution)/shard_map/ppermute | solution.py:764
  141.8 2.2 %collective-permute-done.18.refs_7_ = bf16[96,384]{1,0:T(8,128)(2,1)S(1)} collective-permute-done((bf16[96,384]{1,0:T(8,128)(2,1)S(1)}, bf16[96,384]{1,0:T(8,128)(2,1)S(1)}, u32[]{:S(2)}, u32[]{:S(2)}) %collective-permute-start.18) | collective-permute-done | bytes 73760 | tf_op jit(solution)/shard_map/ppermute | solution.py:764
  146.3 2.2 %collective-permute-start.19 = (bf16[144,384]{1,0:T(8,128)(2,1)S(1)}, bf16[144,384]{1,0:T(8,128)(2,1)S(1)}, u32[]{:S(2)}, u32[]{:S(2)}) collective-permute-start(bf16[144,384]{1,0:T(8,128)(2,1)S(1)} %get-tuple-element.188.refs_1_), channel_id=1, source_target_pairs={{0,4},{1,5},{2,6},{3,7},{4,0},{5,1},{6,2},{7,3},{8,12},{9,13},{10,... | collective-permute-start | bytes 331784 | tf_op jit(solution)/shard_map/ppermute | solution.py:764
  150.8 2.7 %collective-permute-done.20.refs_3_ = bf16[144,384]{1,0:T(8,128)(2,1)S(1)} collective-permute-done((bf16[144,384]{1,0:T(8,128)(2,1)S(1)}, bf16[144,384]{1,0:T(8,128)(2,1)S(1)}, u32[]{:S(2)}, u32[]{:S(2)}) %collective-permute-start.20) | collective-permute-done | bytes 110624 | tf_op jit(solution)/shard_map/ppermute | solution.py:764
  154.1 1.6 collective-permute-start.24
  157.8 1.7 merge_rows.3
  159.6 7.0 %collective-permute-done.25.refs_3_ = bf16[48,384]{1,0:T(8,128)(2,1)S(1)} collective-permute-done((bf16[48,384]{1,0:T(8,128)(2,1)S(1)}, bf16[48,384]{1,0:T(8,128)(2,1)S(1)}, u32[]{:S(2)}, u32[]{:S(2)}) %collective-permute-start.25) | collective-permute-done | bytes 36896 | tf_op jit(solution)/shard_map/ppermute | solution.py:764
  166.6 1.6 collective-permute-start.27
  169.8 2.6 %finish_small.1 = (f32[384]{0:T(512)}, f32[384]{0:T(512)}, f32[2,384]{1,0:T(2,128)}, f32[384]{0:T(512)}, f32[384]{0:T(512)}, /*index=5*/f32[384]{0:T(512)}, f32[...) custom-call(f32[2,96]{1,0:T(2,128)S(1)} %copy-done.17, ...), custom_call_target="tpu_custom_call" | custom-call | bytes 224512 | tf_op jit(solution)/shard_map/finish_small/pallas_call | solution.py:102
  174.8 2.5 %unpack.2 = (f32[384,1536]{1,0:T(8,128)}, f32[1536,384]{1,0:T(8,128)}, f32[384,1152]{1,0:T(8,128)}, f32[384,384]{1,0:T(8,128)}) custom-call(s32[4]{0:T(128)S(1)} %copy-done.9, bf16[624,384]{1,0:T(8,128)(2,1)S(1)} %get-tuple-element.191.refs_0_.first, bf16[3,576,384]{2,1,0:T(8,128)(2,1)S(1)} %collect.1.rest), custom_call_target="tpu_custom_call" | custom-call | bytes 8884240 | tf_op jit(solution)/shard_map/unpack/pallas_call | solution.py:102
  178.1 2.5 %unpack.3 = (f32[384,1536]{1,0:T(8,128)}, f32[1536,384]{1,0:T(8,128)}, f32[384,1152]{1,0:T(8,128)}, f32[384,384]{1,0:T(8,128)}) custom-call(s32[4]{0:T(128)S(1)} %copy-done.9, bf16[624,384]{1,0:T(8,128)(2,1)S(1)} %collective-permute-done.26.refs_1_, ...), custom_call_target="tpu_custom_call", output_to_operand_aliasing={{0}: (3, {}), {1}: (4, {}), {2}: (5, {}), {3}: (6, {})} | custom-call | bytes 8884240 | tf_op jit(solution)/shard_map/unpack/pallas_call | solution.py:102
  (118 shorter events, 27.0 us)
Async XLA Ops:
  2.4 11.1 %collective-permute-start = (bf16[8,3,14,384]{3,2,1,0:T(8,128)(2,1)}, bf16[8,3,14,384]{3,2,1,0:T(8,128)(2,1)S(1)}, u32[]{:S(2)}, u32[]{:S(2)}) collective-permute-start(bf16[8,3,14,384]{3,2,1,0:T(8,128)(2,1)} %get-tuple-element.127), channel_id=1, source_target_pairs={{0,16},{1,17},{2,18},{3,19},{4,20},{5,21},{6,22},{7,23},{8,24},{9,... | collective-permute-start | bytes 774152 | tf_op jit(solution)/shard_map/ppermute | solution.py:764
  7.8 15.3 %collective-permute-start.1 = (bf16[12,3,14,384]{3,2,1,0:T(8,128)(2,1)}, bf16[12,3,14,384]{3,2,1,0:T(8,128)(2,1)S(1)}, u32[]{:S(2)}, u32[]{:S(2)}) collective-permute-start(bf16[12,3,14,384]{3,2,1,0:T(8,128)(2,1)} %get-tuple-element.132), channel_id=1, source_target_pairs={{0,16},{1,17},{2,18},{3,19},{4,20},{5,21},{6,22},{7,23},{8,24},{9,... | collective-permute-start | bytes 1161224 | tf_op jit(solution)/shard_map/ppermute | solution.py:764
  24.5 17.6 %collective-permute-start.2 = (bf16[20,3,14,384]{3,2,1,0:T(8,128)(2,1)}, bf16[20,3,14,384]{3,2,1,0:T(8,128)(2,1)S(1)}, u32[]{:S(2)}, u32[]{:S(2)}) collective-permute-start(bf16[20,3,14,384]{3,2,1,0:T(8,128)(2,1)} %get-tuple-element.134), channel_id=1, source_target_pairs={{0,16},{1,17},{2,18},{3,19},{4,20},{5,21},{6,22},{7,23},{8,24},{9,... | collective-permute-start | bytes 1935368 | tf_op jit(solution)/shard_map/ppermute | solution.py:764
  76.1 19.2 %collective-permute-start.4 = (bf16[1536,384]{1,0:T(8,128)(2,1)}, bf16[1536,384]{1,0:T(8,128)(2,1)S(1)}, u32[]{:S(2)}, u32[]{:S(2)}) collective-permute-start(bf16[1536,384]{1,0:T(8,128)(2,1)} %bitcast.21), channel_id=1, source_target_pairs={{0,1},{1,0},{2,3},{3,2},{4,5},{5,4},{6,7},{7,6},{8,9},{9,8},{10,11... | collective-permute-start | bytes 3538952 | tf_op jit(solution)/shard_map/ppermute | solution.py:764
  76.2 19.1 %collective-permute-start.3 = (bf16[20,3,14,384]{3,2,1,0:T(8,128)(2,1)}, bf16[20,3,14,384]{3,2,1,0:T(8,128)(2,1)S(1)}, u32[]{:S(2)}, u32[]{:S(2)}) collective-permute-start(bf16[20,3,14,384]{3,2,1,0:T(8,128)(2,1)} %get-tuple-element.141), channel_id=1, source_target_pairs={{0,16},{1,17},{2,18},{3,19},{4,20},{5,21},{6,22},{7,23},{8,24},{9,... | collective-permute-start | bytes 1935368 | tf_op jit(solution)/shard_map/ppermute | solution.py:764
  77.9 17.4 %copy-start.8 = (s32[4]{0:T(128)S(1)}, s32[4]{0:T(128)}, u32[]{:S(2)}) copy-start(s32[4]{0:T(128)} %pad_add_fusion.where.refs_0_) | copy-start | bytes 52
  97.4 15.5 %collective-permute-start.6 = (bf16[384,384]{1,0:T(8,128)(2,1)S(1)}, bf16[384,384]{1,0:T(8,128)(2,1)S(1)}, u32[]{:S(2)}, u32[]{:S(2)}) collective-permute-start(bf16[384,384]{1,0:T(8,128)(2,1)S(1)} %get-tuple-element.162), channel_id=1, source_target_pairs={{0,2},{1,3},{2,0},{3,1},{4,6},{5,7},{6,4},{7,5},{8,10},{9,11},{10,... | collective-permute-start | bytes 884744 | tf_op jit(solution)/shard_map/ppermute | solution.py:764
  99.2 13.7 %collective-permute-start.7 = (bf16[384,384]{1,0:T(8,128)(2,1)S(1)}, bf16[384,384]{1,0:T(8,128)(2,1)S(1)}, u32[]{:S(2)}, u32[]{:S(2)}) collective-permute-start(bf16[384,384]{1,0:T(8,128)(2,1)S(1)} %get-tuple-element.163), channel_id=1, source_target_pairs={{0,16},{1,17},{2,18},{3,19},{4,20},{5,21},{6,22},{7,23},{8,24},{9,... | collective-permute-start | bytes 884744 | tf_op jit(solution)/shard_map/ppermute | solution.py:764
  100.7 12.9 %collective-permute-start.8 = (bf16[384,384]{1,0:T(8,128)(2,1)S(1)}, bf16[384,384]{1,0:T(8,128)(2,1)S(1)}, u32[]{:S(2)}, u32[]{:S(2)}) collective-permute-start(bf16[384,384]{1,0:T(8,128)(2,1)S(1)} %get-tuple-element.164), channel_id=1, source_target_pairs={{0,18},{1,19},{2,16},{3,17},{4,22},{5,23},{6,20},{7,21},{8,26},{9,... | collective-permute-start | bytes 884744 | tf_op jit(solution)/shard_map/ppermute | solution.py:764
  101.0 12.6 %copy-start.9 = (s32[4]{0:T(128)S(1)}, s32[4]{0:T(128)}, u32[]{:S(2)}) copy-start(s32[4]{0:T(128)} %pad_add_fusion.where.refs_0_) | copy-start | bytes 52
  112.8 6.8 %collective-permute-start.5 = (bf16[768,384]{1,0:T(8,128)(2,1)}, bf16[768,384]{1,0:T(8,128)(2,1)S(1)}, u32[]{:S(2)}, u32[]{:S(2)}) collective-permute-start(bf16[768,384]{1,0:T(8,128)(2,1)} %bitcast.22), channel_id=1, source_target_pairs={{0,1},{1,0},{2,3},{3,2},{4,5},{5,4},{6,7},{7,6},{8,9},{9,8},{10,11... | collective-permute-start | bytes 1769480 | tf_op jit(solution)/shard_map/ppermute | solution.py:764
  115.2 8.4 %collective-permute-start.10 = (bf16[96,384]{1,0:T(8,128)(2,1)S(1)}, bf16[96,384]{1,0:T(8,128)(2,1)S(1)}, u32[]{:S(2)}, u32[]{:S(2)}) collective-permute-start(bf16[96,384]{1,0:T(8,128)(2,1)S(1)} %get-tuple-element.172), channel_id=1, source_target_pairs={{0,4},{1,5},{2,6},{3,7},{4,0},{5,1},{6,2},{7,3},{8,12},{9,13},{10,... | collective-permute-start | bytes 221192 | tf_op jit(solution)/shard_map/ppermute | solution.py:764
  116.9 15.2 %collective-permute-start.11 = (bf16[96,384]{1,0:T(8,128)(2,1)S(1)}, bf16[96,384]{1,0:T(8,128)(2,1)S(1)}, u32[]{:S(2)}, u32[]{:S(2)}) collective-permute-start(bf16[96,384]{1,0:T(8,128)(2,1)S(1)} %get-tuple-element.173), channel_id=1, source_target_pairs={{0,8},{1,9},{2,10},{3,11},{4,12},{5,13},{6,14},{7,15},{8,0},{9,1},... | collective-permute-start | bytes 221192 | tf_op jit(solution)/shard_map/ppermute | solution.py:764
  119.5 12.6 %collective-permute-start.12 = (bf16[96,384]{1,0:T(8,128)(2,1)S(1)}, bf16[96,384]{1,0:T(8,128)(2,1)S(1)}, u32[]{:S(2)}, u32[]{:S(2)}) collective-permute-start(bf16[96,384]{1,0:T(8,128)(2,1)S(1)} %get-tuple-element.174), channel_id=1, source_target_pairs={{0,12},{1,13},{2,14},{3,15},{4,8},{5,9},{6,10},{7,11},{8,4},{9,5},... | collective-permute-start | bytes 221192 | tf_op jit(solution)/shard_map/ppermute | solution.py:764
  120.3 11.9 %collective-permute-start.13 = (bf16[192,384]{1,0:T(8,128)(2,1)S(1)}, bf16[192,384]{1,0:T(8,128)(2,1)S(1)}, u32[]{:S(2)}, u32[]{:S(2)}) collective-permute-start(bf16[192,384]{1,0:T(8,128)(2,1)S(1)} %get-tuple-element.176), channel_id=1, source_target_pairs={{0,2},{1,3},{2,0},{3,1},{4,6},{5,7},{6,4},{7,5},{8,10},{9,11},{10,... | collective-permute-start | bytes 442376 | tf_op jit(solution)/shard_map/ppermute | solution.py:764
  122.0 10.2 %collective-permute-start.14 = (bf16[192,384]{1,0:T(8,128)(2,1)S(1)}, bf16[192,384]{1,0:T(8,128)(2,1)S(1)}, u32[]{:S(2)}, u32[]{:S(2)}) collective-permute-start(bf16[192,384]{1,0:T(8,128)(2,1)S(1)} %get-tuple-element.177), channel_id=1, source_target_pairs={{0,16},{1,17},{2,18},{3,19},{4,20},{5,21},{6,22},{7,23},{8,24},{9,... | collective-permute-start | bytes 442376 | tf_op jit(solution)/shard_map/ppermute | solution.py:764
  123.6 8.6 %collective-permute-start.15 = (bf16[192,384]{1,0:T(8,128)(2,1)S(1)}, bf16[192,384]{1,0:T(8,128)(2,1)S(1)}, u32[]{:S(2)}, u32[]{:S(2)}) collective-permute-start(bf16[192,384]{1,0:T(8,128)(2,1)S(1)} %get-tuple-element.178), channel_id=1, source_target_pairs={{0,18},{1,19},{2,16},{3,17},{4,22},{5,23},{6,20},{7,21},{8,26},{9,... | collective-permute-start | bytes 442376 | tf_op jit(solution)/shard_map/ppermute | solution.py:764
  133.4 6.1 %collective-permute-start.16 = (bf16[96,384]{1,0:T(8,128)(2,1)S(1)}, bf16[96,384]{1,0:T(8,128)(2,1)S(1)}, u32[]{:S(2)}, u32[]{:S(2)}) collective-permute-start(bf16[96,384]{1,0:T(8,128)(2,1)S(1)} %get-tuple-element.184), channel_id=1, source_target_pairs={{0,4},{1,5},{2,6},{3,7},{4,0},{5,1},{6,2},{7,3},{8,12},{9,13},{10,... | collective-permute-start | bytes 221192 | tf_op jit(solution)/shard_map/ppermute | solution.py:764
  134.2 7.6 %collective-permute-start.17 = (bf16[96,384]{1,0:T(8,128)(2,1)S(1)}, bf16[96,384]{1,0:T(8,128)(2,1)S(1)}, u32[]{:S(2)}, u32[]{:S(2)}) collective-permute-start(bf16[96,384]{1,0:T(8,128)(2,1)S(1)} %get-tuple-element.185), channel_id=1, source_target_pairs={{0,8},{1,9},{2,10},{3,11},{4,12},{5,13},{6,14},{7,15},{8,0},{9,1},... | collective-permute-start | bytes 221192 | tf_op jit(solution)/shard_map/ppermute | solution.py:764
  137.7 6.3 %collective-permute-start.18 = (bf16[96,384]{1,0:T(8,128)(2,1)S(1)}, bf16[96,384]{1,0:T(8,128)(2,1)S(1)}, u32[]{:S(2)}, u32[]{:S(2)}) collective-permute-start(bf16[96,384]{1,0:T(8,128)(2,1)S(1)} %get-tuple-element.186), channel_id=1, source_target_pairs={{0,12},{1,13},{2,14},{3,15},{4,8},{5,9},{6,10},{7,11},{8,4},{9,5},... | collective-permute-start | bytes 221192 | tf_op jit(solution)/shard_map/ppermute | solution.py:764
  137.8 19.9 %collective-permute-start.9 = (bf16[20,3,14,384]{3,2,1,0:T(8,128)(2,1)S(1)}, bf16[20,3,14,384]{3,2,1,0:T(8,128)(2,1)S(1)}, u32[]{:S(2)}, u32[]{:S(2)}) collective-permute-start(bf16[20,3,14,384]{3,2,1,0:T(8,128)(2,1)S(1)} %get-tuple-element.168), channel_id=1, source_target_pairs={{0,16},{1,17},{2,18},{3,19},{4,20},{5,21},{6,22},{7,23},{8,24},{9,... | collective-permute-start | bytes 1935368 | tf_op jit(solution)/shard_map/ppermute | solution.py:764
  144.0 6.8 %collective-permute-start.21 = (bf16[144,384]{1,0:T(8,128)(2,1)S(1)}, bf16[144,384]{1,0:T(8,128)(2,1)S(1)}, u32[]{:S(2)}, u32[]{:S(2)}) collective-permute-start(bf16[144,384]{1,0:T(8,128)(2,1)S(1)} %get-tuple-element.188.refs_1_), channel_id=1, source_target_pairs={{0,12},{1,13},{2,14},{3,15},{4,8},{5,9},{6,10},{7,11},{8,4},{9,5},... | collective-permute-start | bytes 331784 | tf_op jit(solution)/shard_map/ppermute | solution.py:764
  144.9 8.7 %collective-permute-start.20 = (bf16[144,384]{1,0:T(8,128)(2,1)S(1)}, bf16[144,384]{1,0:T(8,128)(2,1)S(1)}, u32[]{:S(2)}, u32[]{:S(2)}) collective-permute-start(bf16[144,384]{1,0:T(8,128)(2,1)S(1)} %get-tuple-element.188.refs_1_), channel_id=1, source_target_pairs={{0,8},{1,9},{2,10},{3,11},{4,12},{5,13},{6,14},{7,15},{8,0},{9,1},... | collective-permute-start | bytes 331784 | tf_op jit(solution)/shard_map/ppermute | solution.py:764
  146.3 7.2 %collective-permute-start.19 = (bf16[144,384]{1,0:T(8,128)(2,1)S(1)}, bf16[144,384]{1,0:T(8,128)(2,1)S(1)}, u32[]{:S(2)}, u32[]{:S(2)}) collective-permute-start(bf16[144,384]{1,0:T(8,128)(2,1)S(1)} %get-tuple-element.188.refs_1_), channel_id=1, source_target_pairs={{0,4},{1,5},{2,6},{3,7},{4,0},{5,1},{6,2},{7,3},{8,12},{9,13},{10,... | collective-permute-start | bytes 331784 | tf_op jit(solution)/shard_map/ppermute | solution.py:764
  148.5 1.5 collective-permute-start.22
  154.1 12.4 %collective-permute-start.24 = (bf16[624,384]{1,0:T(8,128)(2,1)S(1)}, bf16[624,384]{1,0:T(8,128)(2,1)S(1)}, u32[]{:S(2)}, u32[]{:S(2)}) collective-permute-start(bf16[624,384]{1,0:T(8,128)(2,1)S(1)} %get-tuple-element.191.refs_0_.first), channel_id=1, source_target_pairs={{0,2},{1,3},{2,0},{3,1},{4,6},{5,7},{6,4},{7,5},{8,10},{9,11},{10,... | collective-permute-start | bytes 1437704 | tf_op jit(solution)/shard_map/ppermute | solution.py:764
  155.7 10.8 %collective-permute-start.23 = (bf16[624,384]{1,0:T(8,128)(2,1)S(1)}, bf16[624,384]{1,0:T(8,128)(2,1)S(1)}, u32[]{:S(2)}, u32[]{:S(2)}) collective-permute-start(bf16[624,384]{1,0:T(8,128)(2,1)S(1)} %get-tuple-element.191.refs_0_.first), channel_id=1, source_target_pairs={{0,16},{1,17},{2,18},{3,19},{4,20},{5,21},{6,22},{7,23},{8,24},{9,... | collective-permute-start | bytes 1437704 | tf_op jit(solution)/shard_map/ppermute | solution.py:764
  157.2 9.3 %collective-permute-start.25 = (bf16[48,384]{1,0:T(8,128)(2,1)S(1)}, bf16[48,384]{1,0:T(8,128)(2,1)S(1)}, u32[]{:S(2)}, u32[]{:S(2)}) collective-permute-start(bf16[48,384]{1,0:T(8,128)(2,1)S(1)} %get-tuple-element.192), channel_id=1, source_target_pairs={{0,18},{1,19},{2,16},{3,17},{4,22},{5,23},{6,20},{7,21},{8,26},{9,... | collective-permute-start | bytes 110600 | tf_op jit(solution)/shard_map/ppermute | solution.py:764
  166.6 6.0 %collective-permute-start.27 = (bf16[288,384]{1,0:T(8,128)(2,1)S(1)}, bf16[288,384]{1,0:T(8,128)(2,1)S(1)}, u32[]{:S(2)}, u32[]{:S(2)}) collective-permute-start(bf16[288,384]{1,0:T(8,128)(2,1)S(1)} %get-tuple-element.197), channel_id=1, source_target_pairs={{0,2},{1,3},{2,0},{3,1},{4,6},{5,7},{6,4},{7,5},{8,10},{9,11},{10,... | collective-permute-start | bytes 663560 | tf_op jit(solution)/shard_map/ppermute | solution.py:764
  168.2 5.9 %collective-permute-start.28 = (bf16[288,384]{1,0:T(8,128)(2,1)S(1)}, bf16[288,384]{1,0:T(8,128)(2,1)S(1)}, u32[]{:S(2)}, u32[]{:S(2)}) collective-permute-start(bf16[288,384]{1,0:T(8,128)(2,1)S(1)} %get-tuple-element.198), channel_id=1, source_target_pairs={{0,16},{1,17},{2,18},{3,19},{4,20},{5,21},{6,22},{7,23},{8,24},{9,... | collective-permute-start | bytes 663560 | tf_op jit(solution)/shard_map/ppermute | solution.py:764
  174.3 3.8 %collective-permute-start.29 = (bf16[3,576,384]{2,1,0:T(8,128)(2,1)S(1)}, bf16[3,576,384]{2,1,0:T(8,128)(2,1)S(1)}, u32[]{:S(2)}, u32[]{:S(2)}) collective-permute-start(bf16[3,576,384]{2,1,0:T(8,128)(2,1)S(1)} %collect.1.rest), channel_id=1, source_target_pairs={{0,1},{1,0},{2,3},{3,2},{4,5},{5,4},{6,7},{7,6},{8,9},{9,8},{10,11... | collective-permute-start | bytes 3981320 | tf_op jit(solution)/shard_map/ppermute | solution.py:764
  174.3 3.7 %collective-permute-start.26 = (bf16[624,384]{1,0:T(8,128)(2,1)S(1)}, bf16[624,384]{1,0:T(8,128)(2,1)S(1)}, u32[]{:S(2)}, u32[]{:S(2)}) collective-permute-start(bf16[624,384]{1,0:T(8,128)(2,1)S(1)} %get-tuple-element.191.refs_0_.first), channel_id=1, source_target_pairs={{0,1},{1,0},{2,3},{3,2},{4,5},{5,4},{6,7},{7,6},{8,9},{9,8},{10,11... | collective-permute-start | bytes 1437704 | tf_op jit(solution)/shard_map/ppermute | solution.py:764
  (30 other events, 254.4 us)

commit v4 on v2

--- a/solution.py
+++ b/solution.py
@@ -952,23 +952,20 @@
     early = [flat(mine), swap(flat(theirs), (0, 1))]
 
     saved = (normed, qkv, probs, grad_att)
-    chunks = [(0, total - later), (total - later, later)]
-    result = attend_back(where, *chunks[0], per_step, saved, mask, grad_proj, None, (), False, ())
-    *pieces, token = split_share(where, 2, PLANE, early, (result[1],))
+    grads, att_small, grad_pair, mine, theirs = attend_back(
+        where, 0, total, per_step, saved, mask, grad_proj, None, (), True, ()
+    )
+    *pieces, token = split_share(where, 2, PLANE, early, (out_rows, att_small), 5e9)
     early = spread(pieces, in_plane)
-    result = attend_back(where, *chunks[1], per_step, saved, mask, grad_proj, result[1:4], result[:1], True,
-                         (token, out_rows))
-    grads, att_small, grad_pair = result[:3]
-    mine, theirs = flat(result[3]), flat(result[4])
-    *pieces, token = split_share(where, 3, ALONG, early, (att_small,), 5e9)
-    early = spread(pieces, along)
-    *pieces, token = split_share(where, 2, PLANE, [mine, swap(theirs, (0, 1))], (token,))
+    *pieces, token = split_share(where, 2, PLANE, [flat(mine), swap(flat(theirs), (0, 1))], (token,))
     late = spread(pieces, in_plane)
     grad_images, sent, norm_small = image_grads(where, 0, total, per_step, grads, x, grad_mid, norm1_gain,
                                                 qkv_weight, images.shape, (), (), (token,))
     grad_rows = to_partner(sent)
     small = gather_small(feed_small, feed_b1, att_small, norm_small, grad_pair)
-    *pieces, small, _ = split_with_small(where, 3, ALONG, late, [small], early[1:])
+    *pieces, token = split_share(where, 3, ALONG, early, (small,))
+    early = spread(pieces, along)
+    *pieces, small, _ = split_with_small(where, 3, ALONG, late, [small], (token,))
     late = spread(pieces, along)
     share, small = join_shares(early, late, small, ())
     stride = PLANE * ALONG

time: 180 us -> 179 us (level)
  waiting for transfers between devices: 26.8 us -> 33.3 us
  Pallas kernels: 114 us -> 108 us
    ppermute x29, waiting for transfers between devices: 26.8 us -> 33.3 us  [swap(): return lax.ppermute(value, ('band', 'batch'), pairs)]
    pallas_call x24 -> x23, Pallas kernels: 114 us -> 108 us  [launch(): pl.pallas_call(kernel, grid=grid, in_specs=list(in_specs) + [pl.BlockSpec...]
    unnamed x70 -> x60, local copies, waits for them, and re-layouts: 4.91 us -> 3.44 us
  transfers between devices with their start and end apart: 29 -> 29, of which waited for: 9 -> 9; matrix products, arithmetic and copies ran while one was open for 0% -> 0% of each run, Pallas kernels for 42% -> 39%
where the time goes in v4:
time: 179 us; the launch traced here: 178 us
  Pallas kernels  108 us (60%)
  waiting for transfers between devices  33.3 us (19%)
  starting transfers between devices  31.5 us (18%)
  local copies, waits for them, and re-layouts  3.44 us (2%)
    pallas_call x23, Pallas kernels, launch(): pl.pallas_call(kernel, grid=grid, in_specs=list(in_specs) + [pl.BlockSpec...  108 us
    ppermute x29, waiting for transfers between devices, swap(): return lax.ppermute(value, ('band', 'batch'), pairs)  33.3 us
    ppermute x29, starting transfers between devices, swap(): return lax.ppermute(value, ('band', 'batch'), pairs)  31.5 us
  transfers between devices with their start and end apart: 29, of which 9 were waited for; matrix products, arithmetic and copies ran while one was open for 0% of the time, Pallas kernels for 39%

profile of v4, /device:TPU:0, one launch (start us, length us, event | category | flops | bytes accessed | tf_op | source)
XLA Modules:
  0.0 177.9 jit_solution(9684726719494582851)
XLA Ops:
  0.7 1.7 pack_rows.2
  2.4 3.0 %collective-permute-start = (bf16[8,3,14,384]{3,2,1,0:T(8,128)(2,1)}, bf16[8,3,14,384]{3,2,1,0:T(8,128)(2,1)S(1)}, u32[]{:S(2)}, u32[]{:S(2)}) collective-permute-start(bf16[8,3,14,384]{3,2,1,0:T(8,128)(2,1)} %get-tuple-element.121), channel_id=1, source_target_pairs={{0,16},{1,17},{2,18},{3,19},{4,20},{5,21},{6,22},{7,23},{8,24},{9,... | collective-permute-start | bytes 774152 | tf_op jit(solution)/shard_map/ppermute | solution.py:710
  5.4 2.4 %pack_rows.3 = (bf16[12,3,14,384]{3,2,1,0:T(8,128)(2,1)}, bf16[20,3,14,384]{3,2,1,0:T(8,128)(2,1)}, f32[8,128]{1,0:T(8,128)}) custom-call(bf16[20,7,14,384]{3,2,1,0:T(8,128)(2,1)} %refs_1_.6, bf16[20,7,14,384]{3,2,1,0:T(8,128)(2,1)} %cot.1, f32[8,128]{1,0:T(8,128)} %get-tuple-element.122.refs_2_), custom_call_target="tpu_custom_call" | custom-call | bytes 4046848 | tf_op jit(solution)/shard_map/pack_rows/pallas_call | solution.py:87
  7.8 4.3 %pair_bias.1 = (f32[12,112,128]{2,1,0:T(8,128)}, bf16[12,3,14,384]{3,2,1,0:T(8,128)(2,1)}, bf16[20,3,14,384]{3,2,1,0:T(8,128)(2,1)}) custom-call(f32[2,96]{1,0:T(2,128)} %refs_0_.7, f32[96]{0:T(128)} %refs_1_.7, f32[96]{0:T(128)} %refs_2_.3, f32[96]{0:T(128)} %refs_3_.5, f32[96,96]{1,0:T(8,128)} %refs_4_.7, ...), custom_call_target="tpu_custom_call", output_to_operand_aliasing={{1}: (13, {}), {2}: (14, {})} | custom-call | bytes 770688 | tf_op jit(solution)/shard_map/pair_bias/pallas_call | solution.py:87
  13.5 9.0 %attend.2 = (bf16[2240,384]{1,0:T(8,128)(2,1)}, bf16[2240,384]{1,0:T(8,128)(2,1)}, bf16[2240,1152]{1,0:T(8,128)(2,1)}, bf16[10,1344,256]{2,1,0:T(8,128)(2,1)}, bf16[2240,384]{1,0:T(8,128)(2,1)}) custom-call(s32[4]{0:T(128)} %pad_add_fusion.where.refs_0_, bf16[20,7,14,384]{3,2,1,0:T(8,128)(2,1)} %refs_1_.6, bf16[8,3,14,384]{3,2,1,0:T(8,128)(2,1)} %copy-done.27, ...), custom_call_target="tpu_custom_call" | custom-call | flops 1585446912 | bytes 20660240 | tf_op jit(solution)/shard_map/attend/pallas_call | solution.py:87
  22.5 1.5 collective-permute-done.1.refs_1_.refs_2_
  25.8 11.8 %attend.3 = (bf16[2240,384]{1,0:T(8,128)(2,1)}, bf16[2240,384]{1,0:T(8,128)(2,1)}, bf16[2240,1152]{1,0:T(8,128)(2,1)}, bf16[10,1344,256]{2,1,0:T(8,128)(2,1)}, bf16[2240,384]{1,0:T(8,128)(2,1)}) custom-call(s32[4]{0:T(128)} %pad_add_fusion.where.refs_0_, ...), custom_call_target="tpu_custom_call", output_to_operand_aliasing={{0}: (9, {}), {1}: (10, {}), {2}: (11, {}), {3}: (12, {}), ... | custom-call | flops 2378170368 | bytes 20789264 | tf_op jit(solution)/shard_map/attend/pallas_call | solution.py:87
  37.6 5.0 %collective-permute-done.2.received = bf16[20,3,14,384]{3,2,1,0:T(8,128)(2,1)S(1)} collective-permute-done((bf16[20,3,14,384]{3,2,1,0:T(8,128)(2,1)}, bf16[20,3,14,384]{3,2,1,0:T(8,128)(2,1)S(1)}, u32[]{:S(2)}, u32[]{:S(2)}) %collective-permute-start.2) | collective-permute-done | bytes 645152 | tf_op jit(solution)/shard_map/ppermute | solution.py:710
  43.5 33.0 %feed.1 = (bf16[20,7,14,384]{3,2,1,0:T(8,128)(2,1)}, f32[2240,384]{1,0:T(8,128)}, bf16[2240,384]{1,0:T(8,128)(2,1)}, bf16[20,3,14,384]{3,2,1,0:T(8,128)(2,1)}, f...) custom-call(s32[4]{0:T(128)} %pad_add_fusion.where.refs_0_, ...), custom_call_target="tpu_custom_call" | custom-call | flops 17836277760 | bytes 18536464 | tf_op jit(solution)/shard_map/feed/pallas_call | solution.py:87
  77.9 21.7 %attend_back.1 = (bf16[2240,1152]{1,0:T(8,128)(2,1)}, f32[8,384]{1,0:T(8,128)}, f32[1344,128]{1,0:T(8,128)}, bf16[2,384,384]{2,1,0:T(8,128)(2,1)}, bf16[2,384,384]{2,1,0:T(8,128)(2,1)}) custom-call(s32[4]{0:T(128)} %pad_add_fusion.where.refs_0_, bf16[2240,384]{1,0:T(8,128)(2,1)} %get-tuple-element.139.normed, bf16[2240,1152]{1,0:T(8,128)(2,1)} %get-tuple-element.140.qkv, ...), custom_call_target="tpu_custom_call" | custom-call | flops 5945425920 | bytes 23228432 | tf_op jit(solution)/shard_map/attend_back/pallas_call | solution.py:87
  101.6 1.6 collective-permute-start.7
  105.8 1.6 collective-permute-start.13
  108.3 3.5 %collective-permute-done.7.refs_2_ = bf16[384,384]{1,0:T(8,128)(2,1)S(1)} collective-permute-done((bf16[384,384]{1,0:T(8,128)(2,1)S(1)}, bf16[384,384]{1,0:T(8,128)(2,1)S(1)}, u32[]{:S(2)}, u32[]{:S(2)}) %collective-permute-start.7) | collective-permute-done | bytes 294944 | tf_op jit(solution)/shard_map/ppermute | solution.py:710
  111.7 1.8 %collective-permute-start.15 = (bf16[192,384]{1,0:T(8,128)(2,1)S(1)}, bf16[192,384]{1,0:T(8,128)(2,1)S(1)}, u32[]{:S(2)}, u32[]{:S(2)}) collective-permute-start(bf16[192,384]{1,0:T(8,128)(2,1)S(1)} %get-tuple-element.171), channel_id=1, source_target_pairs={{0,18},{1,19},{2,16},{3,17},{4,22},{5,23},{6,20},{7,21},{8,26},{9,... | collective-permute-start | bytes 442376 | tf_op jit(solution)/shard_map/ppermute | solution.py:710
  113.6 7.0 %image_grads.1 = (f32[20,7,14,384]{3,2,1,0:T(8,128)}, bf16[20,3,14,384]{3,2,1,0:T(8,128)(2,1)S(1)}, f32[8,384]{1,0:T(8,128)S(1)}) custom-call(s32[4]{0:T(128)S(1)} %copy-done.7, bf16[2240,1152]{1,0:T(8,128)(2,1)S(1)} %bitcast.13, bf16[2240,384]{1,0:T(8,128)(2,1)S(1)} %copy-done, f32[2240,384]{1,0:T(8,128)S(1)} %copy-done.2, f32[384]{0:T(512)S(1)} %copy-done.12, ...), custom_call_target="tpu_custom_call" | custom-call | flops 1981808640 | bytes 14876176 | tf_op jit(solution)/shard_map/image_grads/pallas_call | solution.py:87
  120.7 1.2 gather_small.1.refs_5_
  122.7 1.6 collective-permute-start.10
  124.3 2.6 %collective-permute-start.11 = (bf16[96,384]{1,0:T(8,128)(2,1)S(1)}, bf16[96,384]{1,0:T(8,128)(2,1)S(1)}, u32[]{:S(2)}, u32[]{:S(2)}) collective-permute-start(bf16[96,384]{1,0:T(8,128)(2,1)S(1)} %get-tuple-element.166), channel_id=1, source_target_pairs={{0,8},{1,9},{2,10},{3,11},{4,12},{5,13},{6,14},{7,15},{8,0},{9,1},... | collective-permute-start | bytes 221192 | tf_op jit(solution)/shard_map/ppermute | solution.py:710
  128.9 3.5 %collective-permute-start.17 = (bf16[96,384]{1,0:T(8,128)(2,1)S(1)}, bf16[96,384]{1,0:T(8,128)(2,1)S(1)}, u32[]{:S(2)}, u32[]{:S(2)}) collective-permute-start(bf16[96,384]{1,0:T(8,128)(2,1)S(1)} %get-tuple-element.175), channel_id=1, source_target_pairs={{0,8},{1,9},{2,10},{3,11},{4,12},{5,13},{6,14},{7,15},{8,0},{9,1},... | collective-permute-start | bytes 221192 | tf_op jit(solution)/shard_map/ppermute | solution.py:710
  133.8 3.6 %collective-permute-done.17.refs_6_ = bf16[96,384]{1,0:T(8,128)(2,1)S(1)} collective-permute-done((bf16[96,384]{1,0:T(8,128)(2,1)S(1)}, bf16[96,384]{1,0:T(8,128)(2,1)S(1)}, u32[]{:S(2)}, u32[]{:S(2)}) %collective-permute-start.17) | collective-permute-done | bytes 73760 | tf_op jit(solution)/shard_map/ppermute | solution.py:710
  137.5 1.2 collective-permute-done.18.refs_7_
  139.7 1.3 collective-permute-start.20
  141.1 2.2 %collective-permute-start.21 = (bf16[144,384]{1,0:T(8,128)(2,1)S(1)}, bf16[144,384]{1,0:T(8,128)(2,1)S(1)}, u32[]{:S(2)}, u32[]{:S(2)}) collective-permute-start(bf16[144,384]{1,0:T(8,128)(2,1)S(1)} %get-tuple-element.178.refs_1_), channel_id=1, source_target_pairs={{0,12},{1,13},{2,14},{3,15},{4,8},{5,9},{6,10},{7,11},{8,4},{9,5},... | collective-permute-start | bytes 331784 | tf_op jit(solution)/shard_map/ppermute | solution.py:710
  143.2 1.5 merge_rows.2
  144.8 5.6 %collective-permute-done.20.refs_3_ = bf16[144,384]{1,0:T(8,128)(2,1)S(1)} collective-permute-done((bf16[144,384]{1,0:T(8,128)(2,1)S(1)}, bf16[144,384]{1,0:T(8,128)(2,1)S(1)}, u32[]{:S(2)}, u32[]{:S(2)}) %collective-permute-start.20) | collective-permute-done | bytes 110624 | tf_op jit(solution)/shard_map/ppermute | solution.py:710
  152.6 1.7 merge_rows.3
  154.3 7.1 %collective-permute-done.23.refs_0_.across = bf16[624,384]{1,0:T(8,128)(2,1)S(1)} collective-permute-done((bf16[624,384]{1,0:T(8,128)(2,1)S(1)}, bf16[624,384]{1,0:T(8,128)(2,1)S(1)}, u32[]{:S(2)}, u32[]{:S(2)}) %collective-permute-start.23) | collective-permute-done | bytes 479264 | tf_op jit(solution)/shard_map/ppermute | solution.py:710
  163.2 1.4 collective-permute-start.25
  164.6 4.7 %collective-permute-done.25.low = bf16[304,384]{1,0:T(8,128)(2,1)S(1)} collective-permute-done((bf16[304,384]{1,0:T(8,128)(2,1)S(1)}, bf16[304,384]{1,0:T(8,128)(2,1)S(1)}, u32[]{:S(2)}, u32[]{:S(2)}) %collective-permute-start.25) | collective-permute-done | bytes 233504 | tf_op jit(solution)/shard_map/ppermute | solution.py:710
  170.0 2.5 %unpack.2 = (f32[384,1536]{1,0:T(8,128)}, f32[1536,384]{1,0:T(8,128)}, f32[384,1152]{1,0:T(8,128)}, f32[384,384]{1,0:T(8,128)}) custom-call(s32[4]{0:T(128)S(1)} %copy-done.7, bf16[624,384]{1,0:T(8,128)(2,1)S(1)} %lay.1.own.first, bf16[3,576,384]{2,1,0:T(8,128)(2,1)S(1)} %get-tuple-element.187.rest), custom_call_target="tpu_custom_call" | custom-call | bytes 8884240 | tf_op jit(solution)/shard_map/unpack/pallas_call | solution.py:87
  172.6 2.6 %finish_small.1 = (f32[384]{0:T(512)}, f32[384]{0:T(512)}, f32[2,384]{1,0:T(2,128)}, f32[384]{0:T(512)}, f32[384]{0:T(512)}, /*index=5*/f32[384]{0:T(512)}, f32[...) custom-call(f32[2,96]{1,0:T(2,128)S(1)} %copy-done.14, ...), custom_call_target="tpu_custom_call" | custom-call | bytes 220416 | tf_op jit(solution)/shard_map/finish_small/pallas_call | solution.py:87
  175.2 2.5 %unpack.3 = (f32[384,1536]{1,0:T(8,128)}, f32[1536,384]{1,0:T(8,128)}, f32[384,1152]{1,0:T(8,128)}, f32[384,384]{1,0:T(8,128)}) custom-call(s32[4]{0:T(128)S(1)} %copy-done.7, bf16[624,384]{1,0:T(8,128)(2,1)S(1)} %collective-permute-done.27.refs_1_, ...), custom_call_target="tpu_custom_call", output_to_operand_aliasing={{0}: (3, {}), {1}: (4, {}), {2}: (5, {}), {3}: (6, {})} | custom-call | bytes 8884240 | tf_op jit(solution)/shard_map/unpack/pallas_call | solution.py:87
  (111 shorter events, 20.8 us)
Async XLA Ops:
  2.4 10.3 %collective-permute-start = (bf16[8,3,14,384]{3,2,1,0:T(8,128)(2,1)}, bf16[8,3,14,384]{3,2,1,0:T(8,128)(2,1)S(1)}, u32[]{:S(2)}, u32[]{:S(2)}) collective-permute-start(bf16[8,3,14,384]{3,2,1,0:T(8,128)(2,1)} %get-tuple-element.121), channel_id=1, source_target_pairs={{0,16},{1,17},{2,18},{3,19},{4,20},{5,21},{6,22},{7,23},{8,24},{9,... | collective-permute-start | bytes 774152 | tf_op jit(solution)/shard_map/ppermute | solution.py:710
  12.1 11.8 %collective-permute-start.1 = (bf16[12,3,14,384]{3,2,1,0:T(8,128)(2,1)}, bf16[12,3,14,384]{3,2,1,0:T(8,128)(2,1)S(1)}, u32[]{:S(2)}, u32[]{:S(2)}) collective-permute-start(bf16[12,3,14,384]{3,2,1,0:T(8,128)(2,1)} %get-tuple-element.127), channel_id=1, source_target_pairs={{0,16},{1,17},{2,18},{3,19},{4,20},{5,21},{6,22},{7,23},{8,24},{9,... | collective-permute-start | bytes 1161224 | tf_op jit(solution)/shard_map/ppermute | solution.py:710
  25.3 17.2 %collective-permute-start.2 = (bf16[20,3,14,384]{3,2,1,0:T(8,128)(2,1)}, bf16[20,3,14,384]{3,2,1,0:T(8,128)(2,1)S(1)}, u32[]{:S(2)}, u32[]{:S(2)}) collective-permute-start(bf16[20,3,14,384]{3,2,1,0:T(8,128)(2,1)} %get-tuple-element.129), channel_id=1, source_target_pairs={{0,16},{1,17},{2,18},{3,19},{4,20},{5,21},{6,22},{7,23},{8,24},{9,... | collective-permute-start | bytes 1935368 | tf_op jit(solution)/shard_map/ppermute | solution.py:710
  76.5 23.3 %collective-permute-start.5 = (bf16[1536,384]{1,0:T(8,128)(2,1)}, bf16[1536,384]{1,0:T(8,128)(2,1)S(1)}, u32[]{:S(2)}, u32[]{:S(2)}) collective-permute-start(bf16[1536,384]{1,0:T(8,128)(2,1)} %bitcast.21), channel_id=1, source_target_pairs={{0,1},{1,0},{2,3},{3,2},{4,5},{5,4},{6,7},{7,6},{8,9},{9,8},{10,11... | collective-permute-start | bytes 3538952 | tf_op jit(solution)/shard_map/ppermute | solution.py:710
  76.6 23.2 %collective-permute-start.3 = (bf16[20,3,14,384]{3,2,1,0:T(8,128)(2,1)}, bf16[20,3,14,384]{3,2,1,0:T(8,128)(2,1)S(1)}, u32[]{:S(2)}, u32[]{:S(2)}) collective-permute-start(bf16[20,3,14,384]{3,2,1,0:T(8,128)(2,1)} %get-tuple-element.136), channel_id=1, source_target_pairs={{0,16},{1,17},{2,18},{3,19},{4,20},{5,21},{6,22},{7,23},{8,24},{9,... | collective-permute-start | bytes 1935368 | tf_op jit(solution)/shard_map/ppermute | solution.py:710
  77.9 22.0 %copy-start.7 = (s32[4]{0:T(128)S(1)}, s32[4]{0:T(128)}, u32[]{:S(2)}) copy-start(s32[4]{0:T(128)} %pad_add_fusion.where.refs_0_) | copy-start | bytes 52
  77.9 22.0 %copy-start.24 = (bf16[4,384,384]{2,1,0:T(8,128)(2,1)S(1)}, bf16[4,384,384]{2,1,0:T(8,128)(2,1)}, u32[]{:S(2)}) copy-start(bf16[4,384,384]{2,1,0:T(8,128)(2,1)} %get-tuple-element.148) | copy-start | bytes 3538948
  99.6 5.5 %collective-permute-start.4 = (bf16[768,384]{1,0:T(8,128)(2,1)}, bf16[768,384]{1,0:T(8,128)(2,1)S(1)}, u32[]{:S(2)}, u32[]{:S(2)}) collective-permute-start(bf16[768,384]{1,0:T(8,128)(2,1)} %bitcast.22), channel_id=1, source_target_pairs={{0,1},{1,0},{2,3},{3,2},{4,5},{5,4},{6,7},{7,6},{8,9},{9,8},{10,11... | collective-permute-start | bytes 1769480 | tf_op jit(solution)/shard_map/ppermute | solution.py:710
  99.8 13.7 %slice-start = ((s8[5160960]{0:T(1024)(128)(4,1)}), s8[4194304]{0:T(1024)(128)(4,1)S(1)}, s32[]{:S(2)}) async-start(s8[5160960]{0:T(1024)(128)(4,1)} %bitcast.12), calls=%async_computation | async-start | bytes 8388608
  101.6 10.2 %collective-permute-start.7 = (bf16[384,384]{1,0:T(8,128)(2,1)S(1)}, bf16[384,384]{1,0:T(8,128)(2,1)S(1)}, u32[]{:S(2)}, u32[]{:S(2)}) collective-permute-start(bf16[384,384]{1,0:T(8,128)(2,1)S(1)} %get-tuple-element.157), channel_id=1, source_target_pairs={{0,2},{1,3},{2,0},{3,1},{4,6},{5,7},{6,4},{7,5},{8,10},{9,11},{10,... | collective-permute-start | bytes 884744 | tf_op jit(solution)/shard_map/ppermute | solution.py:710
  103.2 18.8 %collective-permute-start.8 = (bf16[384,384]{1,0:T(8,128)(2,1)S(1)}, bf16[384,384]{1,0:T(8,128)(2,1)S(1)}, u32[]{:S(2)}, u32[]{:S(2)}) collective-permute-start(bf16[384,384]{1,0:T(8,128)(2,1)S(1)} %get-tuple-element.158), channel_id=1, source_target_pairs={{0,16},{1,17},{2,18},{3,19},{4,20},{5,21},{6,22},{7,23},{8,24},{9,... | collective-permute-start | bytes 884744 | tf_op jit(solution)/shard_map/ppermute | solution.py:710
  104.0 17.9 %collective-permute-start.9 = (bf16[384,384]{1,0:T(8,128)(2,1)S(1)}, bf16[384,384]{1,0:T(8,128)(2,1)S(1)}, u32[]{:S(2)}, u32[]{:S(2)}) collective-permute-start(bf16[384,384]{1,0:T(8,128)(2,1)S(1)} %get-tuple-element.159), channel_id=1, source_target_pairs={{0,18},{1,19},{2,16},{3,17},{4,22},{5,23},{6,20},{7,21},{8,26},{9,... | collective-permute-start | bytes 884744 | tf_op jit(solution)/shard_map/ppermute | solution.py:710
  105.8 21.1 %collective-permute-start.13 = (bf16[192,384]{1,0:T(8,128)(2,1)S(1)}, bf16[192,384]{1,0:T(8,128)(2,1)S(1)}, u32[]{:S(2)}, u32[]{:S(2)}) collective-permute-start(bf16[192,384]{1,0:T(8,128)(2,1)S(1)} %get-tuple-element.169), channel_id=1, source_target_pairs={{0,2},{1,3},{2,0},{3,1},{4,6},{5,7},{6,4},{7,5},{8,10},{9,11},{10,... | collective-permute-start | bytes 442376 | tf_op jit(solution)/shard_map/ppermute | solution.py:710
  107.4 19.7 %collective-permute-start.14 = (bf16[192,384]{1,0:T(8,128)(2,1)S(1)}, bf16[192,384]{1,0:T(8,128)(2,1)S(1)}, u32[]{:S(2)}, u32[]{:S(2)}) collective-permute-start(bf16[192,384]{1,0:T(8,128)(2,1)S(1)} %get-tuple-element.170), channel_id=1, source_target_pairs={{0,16},{1,17},{2,18},{3,19},{4,20},{5,21},{6,22},{7,23},{8,24},{9,... | collective-permute-start | bytes 442376 | tf_op jit(solution)/shard_map/ppermute | solution.py:710
  111.7 15.4 %collective-permute-start.15 = (bf16[192,384]{1,0:T(8,128)(2,1)S(1)}, bf16[192,384]{1,0:T(8,128)(2,1)S(1)}, u32[]{:S(2)}, u32[]{:S(2)}) collective-permute-start(bf16[192,384]{1,0:T(8,128)(2,1)S(1)} %get-tuple-element.171), channel_id=1, source_target_pairs={{0,18},{1,19},{2,16},{3,17},{4,22},{5,23},{6,20},{7,21},{8,26},{9,... | collective-permute-start | bytes 442376 | tf_op jit(solution)/shard_map/ppermute | solution.py:710
  122.7 9.8 %collective-permute-start.10 = (bf16[96,384]{1,0:T(8,128)(2,1)S(1)}, bf16[96,384]{1,0:T(8,128)(2,1)S(1)}, u32[]{:S(2)}, u32[]{:S(2)}) collective-permute-start(bf16[96,384]{1,0:T(8,128)(2,1)S(1)} %get-tuple-element.165), channel_id=1, source_target_pairs={{0,4},{1,5},{2,6},{3,7},{4,0},{5,1},{6,2},{7,3},{8,12},{9,13},{10,... | collective-permute-start | bytes 221192 | tf_op jit(solution)/shard_map/ppermute | solution.py:710
  124.3 8.4 %collective-permute-start.11 = (bf16[96,384]{1,0:T(8,128)(2,1)S(1)}, bf16[96,384]{1,0:T(8,128)(2,1)S(1)}, u32[]{:S(2)}, u32[]{:S(2)}) collective-permute-start(bf16[96,384]{1,0:T(8,128)(2,1)S(1)} %get-tuple-element.166), channel_id=1, source_target_pairs={{0,8},{1,9},{2,10},{3,11},{4,12},{5,13},{6,14},{7,15},{8,0},{9,1},... | collective-permute-start | bytes 221192 | tf_op jit(solution)/shard_map/ppermute | solution.py:710
  126.9 6.9 %collective-permute-start.12 = (bf16[96,384]{1,0:T(8,128)(2,1)S(1)}, bf16[96,384]{1,0:T(8,128)(2,1)S(1)}, u32[]{:S(2)}, u32[]{:S(2)}) collective-permute-start(bf16[96,384]{1,0:T(8,128)(2,1)S(1)} %get-tuple-element.167), channel_id=1, source_target_pairs={{0,12},{1,13},{2,14},{3,15},{4,8},{5,9},{6,10},{7,11},{8,4},{9,5},... | collective-permute-start | bytes 221192 | tf_op jit(solution)/shard_map/ppermute | solution.py:710
  128.3 5.6 %collective-permute-start.16 = (bf16[96,384]{1,0:T(8,128)(2,1)S(1)}, bf16[96,384]{1,0:T(8,128)(2,1)S(1)}, u32[]{:S(2)}, u32[]{:S(2)}) collective-permute-start(bf16[96,384]{1,0:T(8,128)(2,1)S(1)} %get-tuple-element.174), channel_id=1, source_target_pairs={{0,4},{1,5},{2,6},{3,7},{4,0},{5,1},{6,2},{7,3},{8,12},{9,13},{10,... | collective-permute-start | bytes 221192 | tf_op jit(solution)/shard_map/ppermute | solution.py:710
  128.9 8.5 %collective-permute-start.17 = (bf16[96,384]{1,0:T(8,128)(2,1)S(1)}, bf16[96,384]{1,0:T(8,128)(2,1)S(1)}, u32[]{:S(2)}, u32[]{:S(2)}) collective-permute-start(bf16[96,384]{1,0:T(8,128)(2,1)S(1)} %get-tuple-element.175), channel_id=1, source_target_pairs={{0,8},{1,9},{2,10},{3,11},{4,12},{5,13},{6,14},{7,15},{8,0},{9,1},... | collective-permute-start | bytes 221192 | tf_op jit(solution)/shard_map/ppermute | solution.py:710
  132.4 6.3 %collective-permute-start.18 = (bf16[96,384]{1,0:T(8,128)(2,1)S(1)}, bf16[96,384]{1,0:T(8,128)(2,1)S(1)}, u32[]{:S(2)}, u32[]{:S(2)}) collective-permute-start(bf16[96,384]{1,0:T(8,128)(2,1)S(1)} %get-tuple-element.176), channel_id=1, source_target_pairs={{0,12},{1,13},{2,14},{3,15},{4,8},{5,9},{6,10},{7,11},{8,4},{9,5},... | collective-permute-start | bytes 221192 | tf_op jit(solution)/shard_map/ppermute | solution.py:710
  132.7 19.9 %collective-permute-start.6 = (bf16[20,3,14,384]{3,2,1,0:T(8,128)(2,1)S(1)}, bf16[20,3,14,384]{3,2,1,0:T(8,128)(2,1)S(1)}, u32[]{:S(2)}, u32[]{:S(2)}) collective-permute-start(bf16[20,3,14,384]{3,2,1,0:T(8,128)(2,1)S(1)} %get-tuple-element.153), channel_id=1, source_target_pairs={{0,16},{1,17},{2,18},{3,19},{4,20},{5,21},{6,22},{7,23},{8,24},{9,... | collective-permute-start | bytes 1935368 | tf_op jit(solution)/shard_map/ppermute | solution.py:710
  138.8 6.0 %collective-permute-start.19 = (bf16[144,384]{1,0:T(8,128)(2,1)S(1)}, bf16[144,384]{1,0:T(8,128)(2,1)S(1)}, u32[]{:S(2)}, u32[]{:S(2)}) collective-permute-start(bf16[144,384]{1,0:T(8,128)(2,1)S(1)} %get-tuple-element.178.refs_1_), channel_id=1, source_target_pairs={{0,4},{1,5},{2,6},{3,7},{4,0},{5,1},{6,2},{7,3},{8,12},{9,13},{10,... | collective-permute-start | bytes 331784 | tf_op jit(solution)/shard_map/ppermute | solution.py:710
  139.7 10.6 %collective-permute-start.20 = (bf16[144,384]{1,0:T(8,128)(2,1)S(1)}, bf16[144,384]{1,0:T(8,128)(2,1)S(1)}, u32[]{:S(2)}, u32[]{:S(2)}) collective-permute-start(bf16[144,384]{1,0:T(8,128)(2,1)S(1)} %get-tuple-element.178.refs_1_), channel_id=1, source_target_pairs={{0,8},{1,9},{2,10},{3,11},{4,12},{5,13},{6,14},{7,15},{8,0},{9,1},... | collective-permute-start | bytes 331784 | tf_op jit(solution)/shard_map/ppermute | solution.py:710
  141.1 9.3 %collective-permute-start.21 = (bf16[144,384]{1,0:T(8,128)(2,1)S(1)}, bf16[144,384]{1,0:T(8,128)(2,1)S(1)}, u32[]{:S(2)}, u32[]{:S(2)}) collective-permute-start(bf16[144,384]{1,0:T(8,128)(2,1)S(1)} %get-tuple-element.178.refs_1_), channel_id=1, source_target_pairs={{0,12},{1,13},{2,14},{3,15},{4,8},{5,9},{6,10},{7,11},{8,4},{9,5},... | collective-permute-start | bytes 331784 | tf_op jit(solution)/shard_map/ppermute | solution.py:710
  143.2 1.5 collective-permute-start.22
  150.9 10.4 %collective-permute-start.23 = (bf16[624,384]{1,0:T(8,128)(2,1)S(1)}, bf16[624,384]{1,0:T(8,128)(2,1)S(1)}, u32[]{:S(2)}, u32[]{:S(2)}) collective-permute-start(bf16[624,384]{1,0:T(8,128)(2,1)S(1)} %lay.1.own.first), channel_id=1, source_target_pairs={{0,16},{1,17},{2,18},{3,19},{4,20},{5,21},{6,22},{7,23},{8,24},{9,... | collective-permute-start | bytes 1437704 | tf_op jit(solution)/shard_map/ppermute | solution.py:710
  152.2 10.3 %collective-permute-start.24 = (bf16[624,384]{1,0:T(8,128)(2,1)S(1)}, bf16[624,384]{1,0:T(8,128)(2,1)S(1)}, u32[]{:S(2)}, u32[]{:S(2)}) collective-permute-start(bf16[624,384]{1,0:T(8,128)(2,1)S(1)} %lay.1.own.first), channel_id=1, source_target_pairs={{0,2},{1,3},{2,0},{3,1},{4,6},{5,7},{6,4},{7,5},{8,10},{9,11},{10,... | collective-permute-start | bytes 1437704 | tf_op jit(solution)/shard_map/ppermute | solution.py:710
  162.5 6.8 %collective-permute-start.26 = (bf16[320,384]{1,0:T(8,128)(2,1)S(1)}, bf16[320,384]{1,0:T(8,128)(2,1)S(1)}, u32[]{:S(2)}, u32[]{:S(2)}) collective-permute-start(bf16[320,384]{1,0:T(8,128)(2,1)S(1)} %get-tuple-element.183), channel_id=1, source_target_pairs={{0,16},{1,17},{2,18},{3,19},{4,20},{5,21},{6,22},{7,23},{8,24},{9,... | collective-permute-start | bytes 737288 | tf_op jit(solution)/shard_map/ppermute | solution.py:710
  163.2 6.1 %collective-permute-start.25 = (bf16[304,384]{1,0:T(8,128)(2,1)S(1)}, bf16[304,384]{1,0:T(8,128)(2,1)S(1)}, u32[]{:S(2)}, u32[]{:S(2)}) collective-permute-start(bf16[304,384]{1,0:T(8,128)(2,1)S(1)} %get-tuple-element.182), channel_id=1, source_target_pairs={{0,2},{1,3},{2,0},{3,1},{4,6},{5,7},{6,4},{7,5},{8,10},{9,11},{10,... | collective-permute-start | bytes 700424 | tf_op jit(solution)/shard_map/ppermute | solution.py:710
  169.4 5.8 %collective-permute-start.28 = (bf16[3,576,384]{2,1,0:T(8,128)(2,1)S(1)}, bf16[3,576,384]{2,1,0:T(8,128)(2,1)S(1)}, u32[]{:S(2)}, u32[]{:S(2)}) collective-permute-start(bf16[3,576,384]{2,1,0:T(8,128)(2,1)S(1)} %get-tuple-element.187.rest), channel_id=1, source_target_pairs={{0,1},{1,0},{2,3},{3,2},{4,5},{5,4},{6,7},{7,6},{8,9},{9,8},{10,11... | collective-permute-start | bytes 3981320 | tf_op jit(solution)/shard_map/ppermute | solution.py:710
  169.5 5.7 %collective-permute-start.27 = (bf16[624,384]{1,0:T(8,128)(2,1)S(1)}, bf16[624,384]{1,0:T(8,128)(2,1)S(1)}, u32[]{:S(2)}, u32[]{:S(2)}) collective-permute-start(bf16[624,384]{1,0:T(8,128)(2,1)S(1)} %lay.1.own.first), channel_id=1, source_target_pairs={{0,1},{1,0},{2,3},{3,2},{4,5},{5,4},{6,7},{7,6},{8,9},{9,8},{10,11... | collective-permute-start | bytes 1437704 | tf_op jit(solution)/shard_map/ppermute | solution.py:710
  (27 other events, 222.5 us)
